TPU v7x, 32 devices: a whole 2x2x4 slice. The times are simulated.
32 devices in a mesh: groups: 2 (over x), space: 16 (over z, y, core).
Axes of the slice: x: 2, y: 2, z: 4, core: 2. Of those that a mesh axis runs over, the one named last changes fastest.
Arguments:
- eigvecs: bfloat16 [2, 384, 3, 12288], P(None, None, None, ('groups', 'space')), parts along dimension 3, may hold values from -1.5 to 1.5
- momenta: int32 [4, 3], replicated, may hold values from -2 to 2
- peram: bfloat16 [32, 2, 384, 384], P(('groups', 'space')), parts along dimension 0, may hold values from -0.21875 to 0.21875
- graph: int32 [3072, 8], P(('groups', 'space')), parts along dimension 0, may hold values from 0 to 15, all different within a row; in each aligned block of 96 rows (0 to 95, 96 to 191, ...) at most 96 rows name the same one
Outputs:
- contracted: bfloat16 [3072, 8, 768], P(('groups', 'space')), parts along dimension 0
There are 2 independent parts, one for each index of `groups`. A program takes and returns all parts, laid end to end along the dimension named above; an argument that names none is the same for every part. Nothing has to cross between parts.
Inputs may be any that keep to these rules, and one draw needn't show every extreme that they name: `graph`: each row names 8 different owners; among the rows of one device no owner is named more than 96 times, a bound that some block reaches.
All inputs are finite; a program needn't handle non-finite values.
Results may differ from a plain program's by a relative error of at most 0.0064.
Values may be sent and summed in bfloat16 or wider, within the bound.
No kernel may reach another device: no remote copies, remote signals or barrier semaphores. Data moves between devices by JAX's collectives and lax.ppermute only.
A program may use at most 64 MiB of HBM per device.

v0:
```python
import math

import jax
import jax.numpy as jnp
from jax import lax
from jax.sharding import PartitionSpec as P

EXTENT = 128


def partner(block, axis, bit):
    count = lax.axis_size(axis)
    route = []
    for low in range(count):
        high = low | 1 << bit
        if high != low and high < count:
            route += [(low, high), (high, low)]
    return lax.ppermute(block, axis, route)


def phase_tables(momenta, site_index, extent):
    coord_x = site_index % extent
    coord_y = site_index // extent % extent
    coord_z = site_index // (extent * extent)
    wave_number = (
        momenta[:, 0:1] * coord_x[None, :]
        + momenta[:, 1:2] * coord_y[None, :]
        + momenta[:, 2:3] * coord_z[None, :]
    )
    wave_number = jnp.mod(wave_number, extent)
    phase_angle = wave_number.astype(jnp.float32) * (2.0 * math.pi / extent)
    return (jnp.cos(phase_angle), jnp.sin(phase_angle))


def block_form(peram_pair):
    peram_re = peram_pair[0]
    peram_im = peram_pair[1]
    top_half = jnp.concatenate([peram_re, peram_im], axis=1)
    bottom_half = jnp.concatenate([-peram_im, peram_re], axis=1)
    return jnp.concatenate([top_half, bottom_half], axis=0)


def sink_product(arrived, block):
    return lax.dot_general(
        arrived, block, (((2,), (0,)), ((), ())), preferred_element_type=jnp.float32
    ).astype(jnp.bfloat16)


def adjoint_product(sinks, block):
    return lax.dot_general(
        sinks, block, (((2,), (1,)), ((), ())), preferred_element_type=jnp.float32
    ).astype(jnp.bfloat16)


def on_device(eigvecs, momenta, peram, graph):
    num_vec = eigvecs.shape[1]
    local_sites = eigvecs.shape[3]
    spaces = lax.axis_size("space")
    position = lax.axis_index("space")
    site_index = position * local_sites + jnp.arange(local_sites, dtype=jnp.int32)
    cosine, sine = phase_tables(momenta, site_index, EXTENT)
    total_rows = cosine.shape[0] * num_vec
    rows_here = total_rows // spaces
    right_side = jnp.concatenate(
        [
            jnp.concatenate([eigvecs[0], -eigvecs[1]], axis=1),
            jnp.concatenate([eigvecs[1], eigvecs[0]], axis=1),
        ],
        axis=0,
    ).reshape(2 * num_vec, 6 * local_sites)
    row_index = jnp.arange(rows_here * lax.axis_size("space"), dtype=jnp.int32)
    vector_index = row_index % num_vec
    momentum_index = row_index // num_vec
    vec_re = jnp.take(eigvecs[0], vector_index, axis=0).astype(jnp.float32)
    vec_im = jnp.take(eigvecs[1], vector_index, axis=0).astype(jnp.float32)
    cos_rows = jnp.take(cosine, momentum_index, axis=0)[:, None, :]
    sin_rows = jnp.take(sine, momentum_index, axis=0)[:, None, :]
    left_re = vec_re * cos_rows - vec_im * sin_rows
    left_im = -(vec_re * sin_rows + vec_im * cos_rows)
    left_cat = (
        jnp.concatenate([left_re, left_im], axis=1)
        .astype(jnp.bfloat16)
        .reshape(rows_here * lax.axis_size("space"), 6 * local_sites)
    )
    summed = lax.psum_scatter(
        lax.dot_general(
            left_cat, right_side, (((1,), (1,)), ((), ())), preferred_element_type=jnp.float32
        ),
        "space",
        scatter_dimension=0,
        tiled=True,
    )
    elemental = summed.astype(jnp.bfloat16)
    fanout = graph.shape[1]
    capacity = max(2, 2 * rows_here * fanout // spaces)
    flat_owner = graph.reshape(-1)
    entries = flat_owner.shape[0]
    onehot = (flat_owner[:, None] == jnp.arange(spaces, dtype=jnp.int32)[None, :]).astype(jnp.int32)
    earlier = jnp.cumsum(onehot, axis=0) - onehot
    slot = jnp.sum(earlier * onehot, axis=1)
    source_row = jnp.arange(entries, dtype=jnp.int32) // fanout
    payload = jnp.take(elemental, source_row, axis=0)
    outgoing = (
        jnp.zeros((spaces, capacity, 2 * num_vec), jnp.bfloat16).at[flat_owner, slot].set(payload)
    )
    own_block = block_form(peram[0])
    partner_block = partner(own_block, "space", 0)
    sinks = sink_product(
        lax.all_to_all(outgoing, "space", split_axis=0, concat_axis=0, tiled=True), own_block
    )
    finished = adjoint_product(sinks, partner_block)
    returned = lax.all_to_all(finished, "space", split_axis=0, concat_axis=0, tiled=True)
    collected = returned[flat_owner, slot]
    return collected.reshape(rows_here, fanout, 2 * num_vec)


def solution(mesh):
    placed = (
        P(None, None, None, ("groups", "space")),
        P(),
        P(("groups", "space"), None, None, None),
        P(("groups", "space"), None),
    )
    return jax.shard_map(
        on_device,
        mesh=mesh,
        in_specs=placed,
        out_specs=P(("groups", "space"), None, None),
        check_vma=False,
    )
```

profile of v0, /device:TPU:1, one launch (start us, length us, event | category | flops | bytes accessed | tf_op | source)
XLA Modules:
  0.0 390.8 jit_solution(3400149718919486665)
XLA Ops:
  6.5 0.0 reduce-scatter.2.cloned.1.call-start
  6.6 0.6 compare_and_fusion
  7.2 0.6 compare_and_fusion.1
  7.8 1.0 slice_reduce_fusion.3
  8.8 0.1 fusion.50
  9.0 4.8 %gather_fusion.3 = f32[1536,384]{1,0:T(8,128)} fusion(f32[4,384]{1,0:T(4,128)S(1)} %get-tuple-element.18, s32[2048]{0:T(1024)S(1)} %pad_clamp_fusion), kind=kCustom, calls=%fused_computation.1.clone | custom fusion | bytes 4724736 | tf_op jit(solution)/shard_map/jit(_take)/gather | solution.py:76
  13.7 0.0 copy-start
  13.7 4.8 %gather_fusion.5 = f32[1536,384]{1,0:T(8,128)} fusion(f32[4,384]{1,0:T(4,128)S(1)} %get-tuple-element.19, s32[2048]{0:T(1024)S(1)} %pad_clamp_fusion), kind=kCustom, calls=%fused_computation.3.clone | custom fusion | bytes 4724736 | tf_op jit(solution)/shard_map/jit(_take)/gather | solution.py:77
  18.5 0.0 copy-done
  18.5 0.2 fusion.54
  18.7 0.8 fusion.52
  19.5 1.5 copy_bitcast_fusion
  21.1 7.7 %gather_fusion.2 = bf16[1536,3,384]{2,1,0:T(4,128)(2,1)} fusion(bf16[384,3,384]{2,1,0:T(4,128)(2,1)S(1)} %get-tuple-element.25, s32[2048]{0:T(1024)S(1)} %pad_clamp_fusion.1), kind=kCustom, calls=%fused_computation.clone | custom fusion | bytes 7084032 | tf_op jit(solution)/shard_map/jit(_take)/gather | solution.py:74
  28.8 0.0 copy-start.4
  28.8 7.8 %gather_fusion.4 = bf16[1536,3,384]{2,1,0:T(4,128)(2,1)} fusion(bf16[384,3,384]{2,1,0:T(4,128)(2,1)S(1)} %get-tuple-element.24, s32[2048]{0:T(1024)S(1)} %pad_clamp_fusion.1), kind=kCustom, calls=%fused_computation.2.clone | custom fusion | bytes 7084032 | tf_op jit(solution)/shard_map/jit(_take)/gather | solution.py:75
  36.6 0.0 slice-start
  36.6 0.0 slice-start.2
  36.6 2.6 maximum_maximum_fusion
  39.2 0.0 copy-done.4
  39.2 0.0 slice-start.1
  39.2 0.0 slice-start.3
  39.2 0.0 copy-start.3
  39.2 2.9 broadcast_select_fusion.3
  42.1 0.0 slice-done
  42.1 0.0 slice-done.2
  42.1 0.0 slice-done.1
  42.1 0.0 slice-done.3
  42.1 0.0 copy-done.3
  42.2 12.0 %fusion.1 = (bf16[1536,3,384]{2,1,0:T(4,128)(2,1)S(1)}, bf16[1536,3,384]{2,1,0:T(4,128)(2,1)S(1)}) fusion(f32[1536,384]{1,0:T(8,128)S(1)} %get-tuple-element.21, f32[1536,384]{1,0:T(8,128)S(1)} %get-tuple-element.20, bf16[1536,3,384]{2,1,0:T(4,128)(2,1)S(1)} %bitcast.47, pred[1536]{0:T(1024)(128)(4,1)S(1)} %copy-done.3, bf16[1536,3,384]{2,1,0:T(4,128)(2,1)S(1)} %bitcast.49), kind=kLoop, calls=%fused_computation.12 | loop fusion | flops 23003136 | bytes 18875904 | tf_op jit(solution)/shard_map/convert
  54.1 5.0 %pad_maximum_fusion = bf16[1536,6,384]{2,1,0:T(8,128)(2,1)S(1)} fusion(bf16[1536,3,384]{2,1,0:T(4,128)(2,1)S(1)} %get-tuple-element.13, bf16[1536,3,384]{2,1,0:T(4,128)(2,1)S(1)} %get-tuple-element.12), kind=kLoop, calls=%fused_computation.16 | loop fusion | flops 14155776 | bytes 14155776 | tf_op jit(solution)/shard_map/concatenate | solution.py:81
  59.1 7.4 %fusion.7 = f32[1536,768]{1,0:T(8,128)} fusion(bf16[1536,6,384]{2,1,0:T(8,128)(2,1)S(1)} %pad_maximum_fusion, bf16[768,6,384]{2,1,0:T(8,128)(2,1)S(1)} %maximum_maximum_fusion), kind=kOutput, calls=%fused_computation.22 | convolution fusion | flops 5435817984 | bytes 15335424 | tf_op jit(solution)/shard_map/dot_general | solution.py:86
  66.5 0.0 copy-start.5
  66.5 0.0 reduce-scatter.2.cloned.1.call-update
  66.5 0.7 copy-done.5
  67.2 0.1 copy.5
  67.3 0.1 eq.36
  67.4 0.1 eq.32
  67.5 0.1 reshape.185
  67.6 1.7 reduce-window.6
  69.3 0.3 slice_reduce_fusion
  69.6 0.2 fusion.41
  69.8 0.1 fusion.25
  69.9 73.4 %reduce-scatter.2.cloned.1.call-done = f32[96,768]{1,0:T(8,128)} async-done(((f32[1536,768]{1,0:T(8,128)}), f32[96,768]{1,0:T(8,128)}) %reduce-scatter.2.cloned.1.call-update) | async-done | bytes 294928 | tf_op jit(solution)/shard_map/reduce_scatter | solution.py:85
  143.3 1.0 convert_element_type.31
  144.3 2.8 gather_fusion
  147.1 0.2 broadcast_select_fusion.4
  147.2 1.6 broadcast_in_dim.41
  148.9 101.6 %scatter_fusion = bf16[16,96,768]{2,1,0:T(8,128)(2,1)} fusion(bf16[16,96,768]{2,1,0:T(8,128)(2,1)} %broadcast_in_dim.41, s32[768]{0:T(1024)S(1)} %get-tuple-element.8, bf16[768,768]{1,0:T(8,128)(2,1)S(1)} %broadcast_select_fusion.4), kind=kCustom, calls=%fused_computation.6 | custom fusion | bytes 3545088 | tf_op jit(solution)/shard_map/scatter | solution.py:104
  250.5 0.0 copy-start.1
  250.5 5.6 %all-to-all-start = ((bf16[16,96,768]{2,1,0:T(8,128)(2,1)}), bf16[16,96,768]{2,1,0:T(8,128)(2,1)S(1)}, u32[]{:S(2)}, u32[]{:S(2)}) async-start(bf16[16,96,768]{2,1,0:T(8,128)(2,1)} %scatter_fusion), calls=%async_computation.1 | async-start | bytes 4718592 | tf_op jit(solution)/shard_map/all_to_all | solution.py:109
  256.1 0.0 copy-done.1
  256.1 0.1 slice_bitcast_fusion
  256.2 0.0 copy-start.2
  256.2 0.1 maximum_maximum_fusion.1
  256.3 0.2 collective-permute-start
  256.5 0.4 copy-done.2
  256.9 2.4 collective-permute-done
  259.4 42.8 %all-to-all-done = bf16[16,96,768]{2,1,0:T(8,128)(2,1)S(1)} async-done(((bf16[16,96,768]{2,1,0:T(8,128)(2,1)}), bf16[16,96,768]{2,1,0:T(8,128)(2,1)S(1)}, u32[]{:S(2)}, u32[]{:S(2)}) %all-to-all-start) | async-done | bytes 2359328 | tf_op jit(solution)/shard_map/all_to_all | solution.py:109
  302.1 6.9 %fusion.13 = bf16[16,96,768]{2,1,0:T(8,128)(2,1)} fusion(bf16[768,768]{1,0:T(8,128)(2,1)} %collective-permute-done, bf16[16,96,768]{2,1,0:T(8,128)(2,1)S(1)} %all-to-all-done, bf16[384,384]{1,0:T(8,128)(2,1)} %copy-done.2, bf16[384,384]{1,0:T(8,128)(2,1)S(1)} %fusion.51, bf16[384,384]{1,0:T(8,128)(2,1)S(1)} %get-tuple-element.16), kind=kOutput, calls=%fused_computation.26 | convolution fusion | flops 3630956544 | bytes 6782976 | tf_op jit(solution)/shard_map/dot_general | solution.py:50
  309.0 66.3 %all_to_all.10 = bf16[16,96,768]{2,1,0:T(8,128)(2,1)S(1)} all-to-all(bf16[16,96,768]{2,1,0:T(8,128)(2,1)} %fusion.13), channel_id=1, replica_groups=mesh['groups'=2,'space'=16] {'space'}, dimensions={0} | all-to-all | bytes 4718592 | tf_op jit(solution)/shard_map/all_to_all | solution.py:112
  375.3 8.7 %gather_fusion.1 = bf16[768,768]{1,0:T(8,128)(2,1)} fusion(bf16[16,96,768]{2,1,0:T(8,128)(2,1)S(1)} %all_to_all.10, s32[768]{0:T(1024)S(1)} %get-tuple-element.6), kind=kCustom, calls=%fused_computation.5 | custom fusion | bytes 2365440 | tf_op jit(solution)/shard_map/gather | solution.py:113
  (14 shorter events, 0.2 us)
Async XLA Ops:
  6.5 136.8 %reduce-scatter.2.cloned.1.call-start = ((), (), s32[]{:S(2)}) async-start(), calls=%async_computation.3 | async-start | bytes 5013504 | tf_op jit(solution)/shard_map/reduce_scatter | solution.py:85
  13.7 4.8 %copy-start = (bf16[2,384,3,384]{3,1,2,0:T(8,128)(2,1)S(1)}, bf16[2,384,3,384]{3,1,2,0:T(8,128)(2,1)}, u32[]{:S(2)}) copy-start(bf16[2,384,3,384]{3,1,2,0:T(8,128)(2,1)} %param.8) | copy-start | bytes 5308420
  28.8 10.4 %copy-start.4 = (pred[1536]{0:T(1024)(128)(4,1)S(1)}, pred[1536]{0:T(1024)(128)(4,1)}, u32[]{:S(2)}) copy-start(pred[1536]{0:T(1024)(128)(4,1)} %compare_and_fusion) | copy-start | bytes 4612
  36.6 5.6 %slice-start = ((s8[4718592]{0:T(1024)(128)(4,1)}), s8[4194304]{0:T(1024)(128)(4,1)S(1)}, s32[]{:S(2)}) async-start(s8[4718592]{0:T(1024)(128)(4,1)} %bitcast.46), calls=%async_computation.4 | async-start | bytes 8388608
  36.6 5.6 %slice-start.2 = ((s8[4718592]{0:T(1024)(128)(4,1)}), s8[4194304]{0:T(1024)(128)(4,1)S(1)}, s32[]{:S(2)}) async-start(s8[4718592]{0:T(1024)(128)(4,1)} %bitcast.48), calls=%async_computation.6 | async-start | bytes 8388608
  39.2 2.9 slice-start.1
  39.2 2.9 slice-start.3
  39.2 2.9 copy-start.3
  66.5 0.7 copy-start.5
  250.5 5.6 %copy-start.1 = (bf16[1,2,384,384]{3,2,1,0:T(8,128)(2,1)S(1)}, bf16[1,2,384,384]{3,2,1,0:T(8,128)(2,1)}, u32[]{:S(2)}) copy-start(bf16[1,2,384,384]{3,2,1,0:T(8,128)(2,1)} %param.10) | copy-start | bytes 1769476
  250.5 51.6 %all-to-all-start = ((bf16[16,96,768]{2,1,0:T(8,128)(2,1)}), bf16[16,96,768]{2,1,0:T(8,128)(2,1)S(1)}, u32[]{:S(2)}, u32[]{:S(2)}) async-start(bf16[16,96,768]{2,1,0:T(8,128)(2,1)} %scatter_fusion), calls=%async_computation.1 | async-start | bytes 4718592 | tf_op jit(solution)/shard_map/all_to_all | solution.py:109
  256.2 0.7 copy-start.2
  256.3 3.0 collective-permute-start
Sparse Core Ops, SparseCore 0:
  66.6 76.6 reduce-scatter.1
where the time goes:
time: 395 us; the launch traced here: 391 us
  local copies, waits for them, and re-layouts  144 us (36%)
  waiting for transfers between devices  119 us (30%)
  blocking collectives  66.3 us (17%)
  other arithmetic  28 us (7%)
  matrix products  14.3 us (4%)
  between operations  13.7 us (3%)
  starting transfers between devices  5.75 us (1%)
    scatter x1, local copies, waits for them, and re-layouts, on_device(): jnp.zeros((spaces, capacity, 2 * num_vec), jnp.bfloat16)  102 us
    reduce_scatter x1, waiting for transfers between devices, on_device(): lax.psum_scatter(lax.dot_general(left_cat, right_side, (((1,), (1,)), (()...  73.4 us
    all_to_all x1, blocking collectives, on_device(): lax.all_to_all(finished, 'space', split_axis=0, concat_axis=0, tiled=True)  66.3 us
    all_to_all x1, waiting for transfers between devices, on_device(): lax.all_to_all(outgoing, 'space', split_axis=0, concat_axis=0, tiled=True)  42.8 us
    another operation x3, other arithmetic  13.7 us
    gather x1, local copies, waits for them, and re-layouts, on_device(): collected = returned[flat_owner, slot]  8.68 us
  transfers between devices with their start and end apart: 3, of which 3 were waited for; matrix products, arithmetic and copies ran while one was open for 1% of the time, Pallas kernels for 0%

commit v1 on v0

--- a/solution.py
+++ b/solution.py
@@ -1,8 +1,11 @@
+import functools
 import math
 
 import jax
 import jax.numpy as jnp
 from jax import lax
+from jax.experimental import pallas as pl
+from jax.experimental.pallas import tpu as pltpu
 from jax.sharding import PartitionSpec as P
 
 EXTENT = 128
@@ -52,7 +55,7 @@
     ).astype(jnp.bfloat16)
 
 
-def on_device(eigvecs, momenta, peram, graph):
+def exchange_plan(eigvecs, momenta, peram, graph):
     num_vec = eigvecs.shape[1]
     local_sites = eigvecs.shape[3]
     spaces = lax.axis_size("space")
@@ -114,6 +117,265 @@
     return collected.reshape(rows_here, fanout, 2 * num_vec)
 
 
+CORES = 2
+PAIR = 2
+VMEM_LIMIT = 40 * 1024 * 1024
+
+
+def whole(space):
+    return pl.BlockSpec(memory_space=space)
+
+
+def nt_dot(left, right):
+    return lax.dot_general(
+        left, right, (((1,), (1,)), ((), ())), preferred_element_type=jnp.float32
+    )
+
+
+def nn_dot(left, right):
+    return lax.dot_general(
+        left, right, (((1,), (0,)), ((), ())), preferred_element_type=jnp.float32
+    )
+
+
+def product_kernel(core_ref, own_ref, other_ref, out_ref):
+    @pl.when(core_ref[0] == 0)
+    def _():
+        out_ref[...] = (
+            nt_dot(own_ref[0], other_ref[0]) + nt_dot(own_ref[1], other_ref[1])
+        ).astype(out_ref.dtype)
+
+    @pl.when(core_ref[0] != 0)
+    def _():
+        out_ref[...] = (
+            nt_dot(other_ref[1], own_ref[0]) - nt_dot(other_ref[0], own_ref[1])
+        ).astype(out_ref.dtype)
+
+
+def partial_kernel(rows, chain, keep, place_ref, mom_ref, v_ref, out_ref, left_ref, right_ref):
+    num_vec, sites = v_ref.shape[2], v_ref.shape[3]
+    colours = v_ref.shape[1]
+    zed, why, core = place_ref[0], place_ref[1], place_ref[2]
+    position = (zed * PAIR + why) * CORES + core
+    side = core if keep else 1 - core
+    for c in range(colours):
+        for part in range(2):
+            column = pl.ds((part * colours + c) * sites, sites)
+            right_ref[:num_vec, column] = v_ref[part, c]
+            if part == 1:
+                right_ref[num_vec:, column] = -v_ref[0, c]
+            else:
+                right_ref[num_vec:, column] = v_ref[1, c]
+    site = position * sites + lax.broadcasted_iota(jnp.int32, (1, sites), 1)
+    coord_x = site & (EXTENT - 1)
+    coord_y = lax.div(site, EXTENT) & (EXTENT - 1)
+    coord_z = lax.div(site, EXTENT * EXTENT)
+    for shift in range(chain):
+        for half in range(PAIR):
+            target_z = lax.rem(zed + shift, chain)
+            target_y = why if half else 1 - why
+            first = ((target_z * PAIR + target_y) * CORES + side) * rows
+            momentum = lax.div(first, num_vec)
+            start = pl.multiple_of(lax.rem(first, num_vec), rows)
+            wave = (
+                mom_ref[momentum, 0] * coord_x
+                + mom_ref[momentum, 1] * coord_y
+                + mom_ref[momentum, 2] * coord_z
+            ) & (EXTENT - 1)
+            angle = wave.astype(jnp.float32) * (2.0 * math.pi / EXTENT)
+            cosine, sine = jnp.cos(angle), jnp.sin(angle)
+            place = pl.ds((half * chain + shift) * rows, rows)
+            for c in range(colours):
+                vec_re = v_ref[0, c, pl.ds(start, rows), :].astype(jnp.float32)
+                vec_im = v_ref[1, c, pl.ds(start, rows), :].astype(jnp.float32)
+                left_ref[place, pl.ds(c * sites, sites)] = (
+                    vec_re * cosine - vec_im * sine
+                ).astype(jnp.bfloat16)
+                left_ref[place, pl.ds((colours + c) * sites, sites)] = (
+                    vec_re * sine + vec_im * cosine
+                ).astype(jnp.bfloat16)
+    out_ref[...] = nt_dot(left_ref[...], right_ref[...]).astype(out_ref.dtype)
+
+
+def partial_rows(rows, chain, keep, place, momenta, vectors):
+    _, colours, num_vec, sites = vectors.shape
+    depth = 2 * colours * sites
+    height = PAIR * chain * rows
+    dtype = jnp.float32 if keep else jnp.bfloat16
+    return pl.pallas_call(
+        functools.partial(partial_kernel, rows, chain, keep),
+        out_shape=jax.ShapeDtypeStruct((height, 2 * num_vec), dtype),
+        in_specs=[whole(pltpu.SMEM), whole(pltpu.SMEM), whole(pltpu.VMEM)],
+        out_specs=whole(pltpu.VMEM),
+        scratch_shapes=[
+            pltpu.VMEM((height, depth), jnp.bfloat16),
+            pltpu.VMEM((2 * num_vec, depth), jnp.bfloat16),
+        ],
+        compiler_params=pltpu.CompilerParams(vmem_limit_bytes=VMEM_LIMIT),
+        cost_estimate=pl.CostEstimate(
+            flops=2 * height * depth * 2 * num_vec,
+            bytes_accessed=vectors.size * 2 + height * 2 * num_vec * 4,
+            transcendentals=0,
+        ),
+    )(place, momenta, vectors)
+
+
+def owner_products(core, stacked, own, other, even_ref, odd_ref):
+    rows = even_ref.shape[0]
+    num_vec = own.shape[1]
+    for direct, ref in ((True, even_ref), (False, odd_ref)):
+        product = nn_dot if direct else nt_dot
+        by_own, by_other = product(stacked, own), product(stacked, other)
+        by_real = jnp.where(core == 0, by_own, by_other)
+        by_imag = jnp.where(core == 0, by_other, by_own)
+        if direct:
+            real = by_real[:rows] - by_imag[rows:]
+            imag = by_imag[:rows] + by_real[rows:]
+        else:
+            real = by_real[:rows] + by_imag[rows:]
+            imag = by_real[rows:] - by_imag[:rows]
+        ref[:, :num_vec] = real.astype(jnp.bfloat16)
+        ref[:, num_vec:] = imag.astype(jnp.bfloat16)
+
+
+def contract_kernel(slots, arrivals, group, core_ref, *refs):
+    terms, refs = refs[:arrivals], refs[arrivals:]
+    own, refs = refs[:slots], refs[slots:]
+    other, refs = refs[:slots], refs[slots:]
+    pick_ref, out_ref, full_ref = refs
+    rows, fanout, width = out_ref.shape
+    num_vec = width // 2
+    total = terms[0][...].astype(jnp.float32)
+    for term in terms[1:]:
+        total = total + term[...].astype(jnp.float32)
+    elemental = total.astype(jnp.bfloat16)
+    stacked = jnp.concatenate([elemental[:, :num_vec], elemental[:, num_vec:]], axis=0)
+    for slot in range(slots):
+        owner_products(
+            core_ref[0],
+            stacked,
+            own[slot][...],
+            other[slot][...],
+            full_ref.at[2 * slot],
+            full_ref.at[2 * slot + 1],
+        )
+    for block in range(rows // group):
+        table = full_ref[:, pl.ds(block * group, group), :].reshape(2 * slots * group, width)
+        picked = nn_dot(pick_ref[pl.ds(block * group * fanout, group * fanout), :], table)
+        out_ref[pl.ds(block * group, group)] = picked.astype(jnp.bfloat16).reshape(
+            group, fanout, width
+        )
+
+
+def gather_plan(eigvecs, momenta, peram, graph):
+    num_vec = eigvecs.shape[1]
+    spaces = lax.axis_size("space")
+    chain = spaces // (PAIR * CORES)
+    rows = momenta.shape[0] * num_vec // spaces
+    fanout = graph.shape[1]
+    here = lax.axis_index("space")
+    zed, why, core = here // (PAIR * CORES), here // CORES % PAIR, here % CORES
+    place = jnp.stack([zed, why, core]).astype(jnp.int32)
+    core_at = place[2:]
+
+    def index(z, y, c):
+        return (z * PAIR + y) * CORES + c
+
+    def send(block, moves):
+        route = [
+            (index(a, y, c), index(b, y, c))
+            for a, b in moves
+            for y in range(PAIR)
+            for c in range(CORES)
+        ]
+        return lax.ppermute(block, "space", route)
+
+    def across(block):
+        return lax.ppermute(block, "space", [(i, i ^ CORES) for i in range(spaces)])
+
+    def swap(block):
+        return lax.ppermute(block, "space", [(i, i ^ 1) for i in range(spaces)])
+
+    with jax.named_scope("matrices"):
+        mine = peram[0]
+        own = pl.pallas_call(
+            product_kernel,
+            out_shape=jax.ShapeDtypeStruct((num_vec, num_vec), jnp.bfloat16),
+            in_specs=[whole(pltpu.SMEM), whole(pltpu.VMEM), whole(pltpu.VMEM)],
+            out_specs=whole(pltpu.VMEM),
+            compiler_params=pltpu.CompilerParams(vmem_limit_bytes=VMEM_LIMIT),
+            cost_estimate=pl.CostEstimate(
+                flops=4 * num_vec**3, bytes_accessed=10 * num_vec**2, transcendentals=0
+            ),
+        )(core_at, mine, swap(mine))
+    inner = (zed > 0) & (zed < chain - 1)
+    with jax.named_scope("spread"):
+        near = send(own, [(0, 1), (1, 0), (2, 3), (3, 2)])
+        middle = send(own, [(1, 2), (2, 1)])
+        outward = send(middle, [(1, 0), (2, 3)])
+        third = jnp.where(inner, middle, outward)
+        crossing = send(near, [(1, 2), (2, 1)])
+        last = send(crossing, [(1, 0), (2, 3)])
+        fourth = jnp.where(inner, crossing, last)
+        held = [own, across(own), near, across(near), third, across(third), fourth, across(fourth)]
+        swapped = [swap(block) for block in held]
+        columns = []
+        for step in range(chain):
+            source = jnp.asarray(SOURCES[step], jnp.int32)[zed]
+            for other in range(PAIR):
+                chip = source * PAIR + (why ^ other)
+                columns += [chip * CORES, chip * CORES + 1]
+    with jax.named_scope("elementals"):
+        vectors = jnp.transpose(eigvecs, (0, 2, 1, 3))
+        away = partial_rows(rows, chain, False, place, momenta, vectors)
+        arrived = swap(away)
+        kept = partial_rows(rows, chain, True, place, momenta, vectors)
+        half = chain * rows
+        outgoing = (kept[:half] + arrived[:half].astype(jnp.float32)).astype(jnp.bfloat16)
+        crossed = across(outgoing)
+        summed = kept[half:] + arrived[half:].astype(jnp.float32) + crossed.astype(jnp.float32)
+        terms = [summed[:rows]]
+        for shift in range(1, chain):
+            chunk = summed[shift * rows : (shift + 1) * rows].astype(jnp.bfloat16)
+            terms.append(send(chunk, [(z, (z + shift) % chain) for z in range(chain)]))
+    with jax.named_scope("pick"):
+        group = 16
+        owner_of = jnp.repeat(jnp.stack(columns), group)
+        row_of = jnp.arange(rows * fanout, dtype=jnp.int32) // fanout % group
+        place_of = jnp.arange(spaces * group, dtype=jnp.int32) % group
+        pick = (
+            (graph.reshape(-1)[:, None] == owner_of[None, :])
+            & (row_of[:, None] == place_of[None, :])
+        ).astype(jnp.bfloat16)
+    with jax.named_scope("contract"):
+        slots = len(held)
+        return pl.pallas_call(
+            functools.partial(contract_kernel, slots, len(terms), group),
+            out_shape=jax.ShapeDtypeStruct((rows, fanout, 2 * num_vec), jnp.bfloat16),
+            in_specs=[whole(pltpu.SMEM)] + [whole(pltpu.VMEM)] * (len(terms) + 2 * slots + 1),
+            out_specs=whole(pltpu.VMEM),
+            scratch_shapes=[pltpu.VMEM((2 * slots, rows, 2 * num_vec), jnp.bfloat16)],
+            compiler_params=pltpu.CompilerParams(vmem_limit_bytes=VMEM_LIMIT),
+            cost_estimate=pl.CostEstimate(
+                flops=16 * slots * rows * num_vec**2,
+                bytes_accessed=4 * slots * num_vec**2,
+                transcendentals=0,
+            ),
+        )(core_at, *terms, *held, *swapped, pick)
+
+
+SOURCES = ((0, 1, 2, 3), (1, 0, 3, 2), (2, 2, 1, 1), (3, 3, 0, 0))
+
+
+def on_device(eigvecs, momenta, peram, graph):
+    num_vec = eigvecs.shape[1]
+    spaces = lax.axis_size("space")
+    rows = momenta.shape[0] * num_vec // spaces
+    if spaces == CORES * PAIR * len(SOURCES) and num_vec % rows == 0 and rows % 16 == 0:
+        return gather_plan(eigvecs, momenta, peram, graph)
+    return exchange_plan(eigvecs, momenta, peram, graph)
+
+
 def solution(mesh):
     placed = (
         P(None, None, None, ("groups", "space")),

time: 395 us -> 90.5 us (0.23)
  local copies, waits for them, and re-layouts: 144 us -> 4.51 us
  waiting for transfers between devices: 119 us -> 28.8 us
  blocking collectives: 66.3 us -> 0 us
  starting transfers between devices: 5.75 us -> 33.9 us
  other arithmetic: 28 us -> 2.95 us
  Pallas kernels: 0 us -> 16.3 us
  matrix products: 14.3 us -> 0 us
  between operations: 13.7 us -> 2.23 us
    scatter x1 -> x0, local copies, waits for them, and re-layouts: 102 us -> none  [on_device(): jnp.zeros((spaces, capacity, 2 * num_vec), jnp.bfloat16)]
    reduce_scatter x1 -> x0, waiting for transfers between devices: 73.4 us -> none  [on_device(): lax.psum_scatter(lax.dot_general(left_cat, right_side, (((1,), (1,)), (()...]
    all_to_all x1 -> x0, blocking collectives: 66.3 us -> none  [on_device(): lax.all_to_all(finished, 'space', split_axis=0, concat_axis=0, tiled=True)]
    all_to_all x1 -> x0, waiting for transfers between devices: 42.8 us -> none  [on_device(): lax.all_to_all(outgoing, 'space', split_axis=0, concat_axis=0, tiled=True)]
    gather x6 -> x0, local copies, waits for them, and re-layouts: 36.5 us -> none  [the longest x1 8.68 us: on_device(): collected = returned[flat_owner, slot]]
    ppermute x1 -> x23, starting transfers between devices: 0.17 us -> 33.9 us  [the longest x10 17.3 us: swap(): return lax.ppermute(block, 'space', [(i, i ^ 1) for i in range(spaces)])]
    ppermute x1 -> x23, waiting for transfers between devices: 2.44 us -> 28.8 us  [the longest x8 19 us: send(): return lax.ppermute(block, 'space', route)]
    pallas_call x0 -> x4, Pallas kernels: none -> 16.3 us  [the longest x2 10.6 us: partial_rows(): pl.pallas_call(functools.partial(partial_kernel, rows, chain, keep), out_...]
  transfers between devices with their start and end apart: 3 -> 23, of which waited for: 3 -> 8; matrix products, arithmetic and copies ran while one was open for 1% -> 6% of each run, Pallas kernels for 0% -> 13%
where the time goes in v1:
time: 90.5 us; the launch traced here: 88.7 us
  starting transfers between devices  33.9 us (37%)
  waiting for transfers between devices  28.8 us (32%)
  Pallas kernels  16.3 us (18%)
  local copies, waits for them, and re-layouts  4.51 us (5%)
  other arithmetic  2.95 us (3%)
  between operations  2.23 us (2%)
    ppermute x8, waiting for transfers between devices, send(): return lax.ppermute(block, 'space', route)  19 us
    ppermute x10, starting transfers between devices, swap(): return lax.ppermute(block, 'space', [(i, i ^ 1) for i in range(spaces)])  17.3 us
    ppermute x8, starting transfers between devices, send(): return lax.ppermute(block, 'space', route)  12.3 us
    pallas_call x2, Pallas kernels, partial_rows(): pl.pallas_call(functools.partial(partial_kernel, rows, chain, keep), out_...  10.6 us
    ppermute x5, waiting for transfers between devices, across(): return lax.ppermute(block, 'space', [(i, i ^ CORES) for i in range(spaces)])  9.79 us
    pallas_call x1, Pallas kernels, gather_plan(): pl.pallas_call(functools.partial(contract_kernel, slots, len(terms), grou...  5.09 us
    ppermute x5, starting transfers between devices, across(): return lax.ppermute(block, 'space', [(i, i ^ CORES) for i in range(spaces)])  4.31 us
    unnamed x19, local copies, waits for them, and re-layouts  2.28 us
  transfers between devices with their start and end apart: 23, of which 8 were waited for; matrix products, arithmetic and copies ran while one was open for 6% of the time, Pallas kernels for 13%

profile of v1, /device:TPU:1, one launch (start us, length us, event | category | flops | bytes accessed | tf_op | source)
XLA Modules:
  0.0 88.7 jit_solution(7244169760674852598)
XLA Ops:
  0.0 0.1 collective-permute-start.5
  0.1 0.1 pad_add_fusion.place_ref
  0.1 1.5 %copy-done.1 = bf16[2,384,3,384]{3,1,2,0:T(8,128)(2,1)S(1)} copy-done((bf16[2,384,3,384]{3,1,2,0:T(8,128)(2,1)S(1)}, bf16[2,384,3,384]{3,1,2,0:T(8,128)(2,1)}, u32[]{:S(2)}) %copy-start.1) | copy-done | bytes 1769496
  1.6 0.7 copy-done.3
  2.3 5.8 %elementals.3 = bf16[768,768]{1,0:T(8,128)(2,1)} custom-call(s32[3]{0:T(128)S(1)} %pad_add_fusion.place_ref, s32[4,3]{1,0:T(4,128)S(1)} %copy-done.3, bf16[2,3,384,384]{3,2,1,0:T(8,128)(2,1)S(1)} %bitcast.26), custom_call_target="tpu_custom_call" | custom-call | flops 2717908992 | bytes 4128768 | tf_op jit(solution)/shard_map/elementals/pallas_call | solution.py:205
  8.2 0.0 copy-start.4
  8.2 0.5 collective-permute-start
  8.6 0.0 collective-permute-done.5.other_ref
  8.6 0.6 matrices.1.refs_4_
  9.2 2.4 %collective-permute-start.7 = (bf16[384,384]{1,0:T(8,128)(2,1)S(1)}, bf16[384,384]{1,0:T(8,128)(2,1)S(1)}, u32[]{:S(2)}, u32[]{:S(2)}) collective-permute-start(bf16[384,384]{1,0:T(8,128)(2,1)S(1)} %matrices.1.refs_4_), channel_id=1, source_target_pairs={{0,4},{1,5},{2,6},{3,7},{4,0},{5,1},{6,2},{7,3},{8,12},{9,13},{10,... | collective-permute-start | bytes 884744 | tf_op jit(solution)/shard_map/spread/ppermute | solution.py:291
  11.6 0.7 collective-permute-start.9
  12.3 6.3 %collective-permute-done.7.refs_6_ = bf16[384,384]{1,0:T(8,128)(2,1)S(1)} collective-permute-done((bf16[384,384]{1,0:T(8,128)(2,1)S(1)}, bf16[384,384]{1,0:T(8,128)(2,1)S(1)}, u32[]{:S(2)}, u32[]{:S(2)}) %collective-permute-start.7) | collective-permute-done | bytes 294944 | tf_op jit(solution)/shard_map/spread/ppermute | solution.py:291
  18.6 0.7 collective-permute-start.12
  19.4 0.6 dynamic_slice.13
  20.6 0.6 dynamic_slice.14
  21.9 0.6 dynamic_slice.15
  23.2 0.1 stack.83
  23.3 0.1 broadcast_in_dim.2
  23.4 0.1 eq.39
  23.5 0.1 copy.9
  23.5 0.1 eq.37
  23.7 4.8 %elementals.2 = f32[768,768]{1,0:T(8,128)S(1)} custom-call(s32[3]{0:T(128)S(1)} %pad_add_fusion.place_ref, s32[4,3]{1,0:T(4,128)S(1)} %copy-done.4, bf16[2,3,384,384]{3,2,1,0:T(8,128)(2,1)S(1)} %bitcast.27), custom_call_target="tpu_custom_call" | custom-call | flops 2717908992 | bytes 4128768 | tf_op jit(solution)/shard_map/elementals/pallas_call | solution.py:205
  28.5 1.1 %collective-permute-start.6 = (bf16[384,384]{1,0:T(8,128)(2,1)S(1)}, bf16[384,384]{1,0:T(8,128)(2,1)S(1)}, u32[]{:S(2)}, u32[]{:S(2)}) collective-permute-start(bf16[384,384]{1,0:T(8,128)(2,1)S(1)} %matrices.1.refs_4_), channel_id=1, source_target_pairs={{0,2},{1,3},{2,0},{3,1},{4,6},{5,7},{6,4},{7,5},{8,10},{9,11},{10,... | collective-permute-start | bytes 884744 | tf_op jit(solution)/shard_map/spread/ppermute | solution.py:294
  29.6 0.0 collective-permute-done.9
  29.6 1.3 %collective-permute-start.10 = (bf16[384,384]{1,0:T(8,128)(2,1)S(1)}, bf16[384,384]{1,0:T(8,128)(2,1)S(1)}, u32[]{:S(2)}, u32[]{:S(2)}) collective-permute-start(bf16[384,384]{1,0:T(8,128)(2,1)S(1)} %collective-permute-done.9), channel_id=1, source_target_pairs={{4,0},{5,1},{6,2},{7,3},{8,12},{9,13},{10,14},{11,15},{20,16},{21,... | collective-permute-start | bytes 884744 | tf_op jit(solution)/shard_map/spread/ppermute | solution.py:291
  30.9 0.0 collective-permute-done.12
  30.9 1.3 %collective-permute-start.13 = (bf16[384,384]{1,0:T(8,128)(2,1)S(1)}, bf16[384,384]{1,0:T(8,128)(2,1)S(1)}, u32[]{:S(2)}, u32[]{:S(2)}) collective-permute-start(bf16[384,384]{1,0:T(8,128)(2,1)S(1)} %collective-permute-done.12), channel_id=1, source_target_pairs={{4,0},{5,1},{6,2},{7,3},{8,12},{9,13},{10,14},{11,15},{20,16},{21,... | collective-permute-start | bytes 884744 | tf_op jit(solution)/shard_map/spread/ppermute | solution.py:291
  32.2 0.0 collective-permute-done
  32.2 1.2 %fusion = bf16[384,768]{1,0:T(8,128)(2,1)S(1)} fusion(f32[768,768]{1,0:T(8,128)S(1)} %elementals.2, bf16[768,768]{1,0:T(8,128)(2,1)} %collective-permute-done), kind=kLoop, calls=%fused_computation.1 | loop fusion | flops 884736 | bytes 2359296 | tf_op jit(solution)/shard_map/elementals/convert_element_type | solution.py:334
  33.4 0.5 collective-permute-start.1
  33.9 1.5 %collective-permute-start.15 = (bf16[384,384]{1,0:T(8,128)(2,1)S(1)}, bf16[384,384]{1,0:T(8,128)(2,1)S(1)}, u32[]{:S(2)}, u32[]{:S(2)}) collective-permute-start(bf16[384,384]{1,0:T(8,128)(2,1)S(1)} %matrices.1.refs_4_), channel_id=1, source_target_pairs={{0,1},{1,0},{2,3},{3,2},{4,5},{5,4},{6,7},{7,6},{8,9},{9,8},{10,11... | collective-permute-start | bytes 884744 | tf_op jit(solution)/shard_map/spread/ppermute | solution.py:297
  35.4 0.7 collective-permute-done.6.refs_5_
  36.1 0.7 collective-permute-start.8
  36.8 3.3 %collective-permute-done.10 = bf16[384,384]{1,0:T(8,128)(2,1)S(1)} collective-permute-done((bf16[384,384]{1,0:T(8,128)(2,1)S(1)}, bf16[384,384]{1,0:T(8,128)(2,1)S(1)}, u32[]{:S(2)}, u32[]{:S(2)}) %collective-permute-start.10) | collective-permute-done | bytes 294944 | tf_op jit(solution)/shard_map/spread/ppermute | solution.py:291
  40.1 4.6 %collective-permute-start.17 = (bf16[384,384]{1,0:T(8,128)(2,1)S(1)}, bf16[384,384]{1,0:T(8,128)(2,1)S(1)}, u32[]{:S(2)}, u32[]{:S(2)}) collective-permute-start(bf16[384,384]{1,0:T(8,128)(2,1)S(1)} %collective-permute-done.7.refs_6_), channel_id=1, source_target_pairs={{0,1},{1,0},{2,3},{3,2},{4,5},{5,4},{6,7},{7,6},{8,9},{9,8},{10,11... | collective-permute-start | bytes 884744 | tf_op jit(solution)/shard_map/spread/ppermute | solution.py:297
  44.7 1.7 %collective-permute-done.13 = bf16[384,384]{1,0:T(8,128)(2,1)S(1)} collective-permute-done((bf16[384,384]{1,0:T(8,128)(2,1)S(1)}, bf16[384,384]{1,0:T(8,128)(2,1)S(1)}, u32[]{:S(2)}, u32[]{:S(2)}) %collective-permute-start.13) | collective-permute-done | bytes 294944 | tf_op jit(solution)/shard_map/spread/ppermute | solution.py:291
  46.4 2.5 %collective-permute-start.16 = (bf16[384,384]{1,0:T(8,128)(2,1)S(1)}, bf16[384,384]{1,0:T(8,128)(2,1)S(1)}, u32[]{:S(2)}, u32[]{:S(2)}) collective-permute-start(bf16[384,384]{1,0:T(8,128)(2,1)S(1)} %collective-permute-done.6.refs_5_), channel_id=1, source_target_pairs={{0,1},{1,0},{2,3},{3,2},{4,5},{5,4},{6,7},{7,6},{8,9},{9,8},{10,11... | collective-permute-start | bytes 884744 | tf_op jit(solution)/shard_map/spread/ppermute | solution.py:297
  49.0 0.1 broadcast_select_fusion.1.refs_8_
  49.1 0.0 collective-permute-done.15.refs_12_
  49.1 0.3 collective-permute-start.11
  49.4 5.8 %collective-permute-done.8.refs_7_ = bf16[384,384]{1,0:T(8,128)(2,1)S(1)} collective-permute-done((bf16[384,384]{1,0:T(8,128)(2,1)S(1)}, bf16[384,384]{1,0:T(8,128)(2,1)S(1)}, u32[]{:S(2)}, u32[]{:S(2)}) %collective-permute-start.8) | collective-permute-done | bytes 294944 | tf_op jit(solution)/shard_map/spread/ppermute | solution.py:294
  55.2 3.0 %collective-permute-start.19 = (bf16[384,384]{1,0:T(8,128)(2,1)S(1)}, bf16[384,384]{1,0:T(8,128)(2,1)S(1)}, u32[]{:S(2)}, u32[]{:S(2)}) collective-permute-start(bf16[384,384]{1,0:T(8,128)(2,1)S(1)} %broadcast_select_fusion.1.refs_8_), channel_id=1, source_target_pairs={{0,1},{1,0},{2,3},{3,2},{4,5},{5,4},{6,7},{7,6},{8,9},{9,8},{10,11... | collective-permute-start | bytes 884744 | tf_op jit(solution)/shard_map/spread/ppermute | solution.py:297
  58.2 0.0 collective-permute-done.17.refs_14_
  58.2 0.0 collective-permute-start.18
  58.2 0.0 collective-permute-done.16.refs_13_
  58.2 1.6 %collective-permute-start.14 = (bf16[384,384]{1,0:T(8,128)(2,1)S(1)}, bf16[384,384]{1,0:T(8,128)(2,1)S(1)}, u32[]{:S(2)}, u32[]{:S(2)}) collective-permute-start(bf16[384,384]{1,0:T(8,128)(2,1)S(1)} %broadcast_select_fusion.refs_10_), channel_id=1, source_target_pairs={{0,2},{1,3},{2,0},{3,1},{4,6},{5,7},{6,4},{7,5},{8,10},{9,11},{10,... | collective-permute-start | bytes 884744 | tf_op jit(solution)/shard_map/spread/ppermute | solution.py:294
  59.9 0.0 collective-permute-done.1
  59.9 0.7 collective-permute-start.21
  60.6 1.3 %fusion.6 = (bf16[384,768]{1,0:T(8,128)(2,1)S(1)}, f32[384,768]{1,0:T(8,128)S(1)}) fusion(bf16[384,768]{1,0:T(8,128)(2,1)S(1)} %collective-permute-done.1, bf16[768,768]{1,0:T(8,128)(2,1)} %collective-permute-done, f32[768,768]{1,0:T(8,128)S(1)} %elementals.2), kind=kLoop, calls=%fused_computation.20 | loop fusion | flops 1474560 | bytes 4128768 | tf_op jit(solution)/shard_map/convert.2
  61.9 0.0 collective-permute-done.11.refs_9_
  61.9 2.6 %collective-permute-start.20 = (bf16[384,384]{1,0:T(8,128)(2,1)S(1)}, bf16[384,384]{1,0:T(8,128)(2,1)S(1)}, u32[]{:S(2)}, u32[]{:S(2)}) collective-permute-start(bf16[384,384]{1,0:T(8,128)(2,1)S(1)} %collective-permute-done.11.refs_9_), channel_id=1, source_target_pairs={{0,1},{1,0},{2,3},{3,2},{4,5},{5,4},{6,7},{7,6},{8,9},{9,8},{10,11... | collective-permute-start | bytes 884744 | tf_op jit(solution)/shard_map/spread/ppermute | solution.py:297
  64.5 3.3 %collective-permute-done.14.refs_11_ = bf16[384,384]{1,0:T(8,128)(2,1)S(1)} collective-permute-done((bf16[384,384]{1,0:T(8,128)(2,1)S(1)}, bf16[384,384]{1,0:T(8,128)(2,1)S(1)}, u32[]{:S(2)}, u32[]{:S(2)}) %collective-permute-start.14) | collective-permute-done | bytes 294944 | tf_op jit(solution)/shard_map/spread/ppermute | solution.py:294
  67.8 1.7 %collective-permute-start.22 = (bf16[384,384]{1,0:T(8,128)(2,1)S(1)}, bf16[384,384]{1,0:T(8,128)(2,1)S(1)}, u32[]{:S(2)}, u32[]{:S(2)}) collective-permute-start(bf16[384,384]{1,0:T(8,128)(2,1)S(1)} %collective-permute-done.14.refs_11_), channel_id=1, source_target_pairs={{0,1},{1,0},{2,3},{3,2},{4,5},{5,4},{6,7},{7,6},{8,9},{9,8},{10,11... | collective-permute-start | bytes 884744 | tf_op jit(solution)/shard_map/spread/ppermute | solution.py:297
  69.6 0.0 collective-permute-done.19.refs_16_
  69.6 3.7 %collective-permute-start.2 = (bf16[96,768]{1,0:T(8,128)(2,1)S(1)}, bf16[96,768]{1,0:T(8,128)(2,1)S(1)}, u32[]{:S(2)}, u32[]{:S(2)}) collective-permute-start(bf16[96,768]{1,0:T(8,128)(2,1)S(1)} %get-tuple-element.9), channel_id=1, source_target_pairs={{0,4},{1,5},{2,6},{3,7},{4,8},{5,9},{6,10},{7,11},{8,12},{9,13},{1... | collective-permute-start | bytes 442376 | tf_op jit(solution)/shard_map/elementals/ppermute | solution.py:291
  73.3 0.0 collective-permute-start.3
  73.3 0.0 collective-permute-done.21.refs_18_
  73.3 2.2 %collective-permute-start.4 = (bf16[96,768]{1,0:T(8,128)(2,1)S(1)}, bf16[96,768]{1,0:T(8,128)(2,1)S(1)}, u32[]{:S(2)}, u32[]{:S(2)}) collective-permute-start(bf16[96,768]{1,0:T(8,128)(2,1)S(1)} %get-tuple-element.7), channel_id=1, source_target_pairs={{0,12},{1,13},{2,14},{3,15},{4,0},{5,1},{6,2},{7,3},{8,4},{9,5},{1... | collective-permute-start | bytes 442376 | tf_op jit(solution)/shard_map/elementals/ppermute | solution.py:291
  75.6 0.3 and_convert_fusion.refs_20_
  75.9 0.0 collective-permute-done.20.refs_17_
  75.9 1.0 %collective-permute-done.2.refs_1_ = bf16[96,768]{1,0:T(8,128)(2,1)S(1)} collective-permute-done((bf16[96,768]{1,0:T(8,128)(2,1)S(1)}, bf16[96,768]{1,0:T(8,128)(2,1)S(1)}, u32[]{:S(2)}, u32[]{:S(2)}) %collective-permute-start.2) | collective-permute-done | bytes 147488 | tf_op jit(solution)/shard_map/elementals/ppermute | solution.py:291
  76.9 6.6 %collective-permute-done.3.refs_2_ = bf16[96,768]{1,0:T(8,128)(2,1)S(1)} collective-permute-done((bf16[96,768]{1,0:T(8,128)(2,1)S(1)}, bf16[96,768]{1,0:T(8,128)(2,1)S(1)}, u32[]{:S(2)}, u32[]{:S(2)}) %collective-permute-start.3) | collective-permute-done | bytes 147488 | tf_op jit(solution)/shard_map/elementals/ppermute | solution.py:291
  83.6 0.0 collective-permute-done.4.refs_3_
  83.6 5.1 %contract.1 = bf16[96,8,768]{2,1,0:T(8,128)(2,1)} custom-call(s32[1]{0:T(128)} %bitcast.core_ref, f32[96,768]{1,0:T(8,128)S(1)} %slice.39.refs_0_, bf16[96,768]{1,0:T(8,128)(2,1)S(1)} %collective-permute-done.2.refs_1_, bf16[96,768]{1,0:T(8,128)(2,1)S(1)} %collective-permute-done.3.refs_2_, bf16[96,768]{1,0:T(8,128)(2,1)S(1)} %collective-permute-done.4.refs_3_, ...), custom_call_target="tpu_custom_call" | custom-call | flops 1811939328 | bytes 4718592 | tf_op jit(solution)/shard_map/contract/pallas_call | solution.py:352
  (22 shorter events, 0.1 us)
Async XLA Ops:
  0.0 8.6 %collective-permute-start.5 = (bf16[2,384,384]{2,1,0:T(8,128)(2,1)}, bf16[2,384,384]{2,1,0:T(8,128)(2,1)S(1)}, u32[]{:S(2)}, u32[]{:S(2)}) collective-permute-start(bf16[2,384,384]{2,1,0:T(8,128)(2,1)} %bitcast.24), channel_id=1, source_target_pairs={{0,1},{1,0},{2,3},{3,2},{4,5},{5,4},{6,7},{7,6},{8,9},{9,8},{10,11... | collective-permute-start | bytes 1769480 | tf_op jit(solution)/shard_map/matrices/ppermute | solution.py:297
  0.1 1.5 %copy-start.1 = (bf16[2,384,3,384]{3,1,2,0:T(8,128)(2,1)S(1)}, bf16[2,384,3,384]{3,1,2,0:T(8,128)(2,1)}, u32[]{:S(2)}) copy-start(bf16[2,384,3,384]{3,1,2,0:T(8,128)(2,1)} %param.8) | copy-start | bytes 5308420
  1.6 0.7 copy-start.3
  2.3 6.3 %copy-start = (bf16[1,2,384,384]{3,2,1,0:T(8,128)(2,1)S(1)}, bf16[1,2,384,384]{3,2,1,0:T(8,128)(2,1)}, u32[]{:S(2)}) copy-start(bf16[1,2,384,384]{3,2,1,0:T(8,128)(2,1)} %param.10) | copy-start | bytes 1769476
  2.3 21.4 %copy-start.2 = (bf16[2,384,3,384]{3,1,2,0:T(8,128)(2,1)S(1)}, bf16[2,384,3,384]{3,1,2,0:T(8,128)(2,1)}, u32[]{:S(2)}) copy-start(bf16[2,384,3,384]{3,1,2,0:T(8,128)(2,1)} %param.8) | copy-start | bytes 5308420
  8.1 11.2 %copy-start.8 = (s32[4]{0:T(128)S(1)}, s32[4]{0:T(128)}, u32[]{:S(2)}) copy-start(s32[4]{0:T(128)} %constant.96.clone) | copy-start | bytes 52
  8.1 12.5 %copy-start.7 = (s32[4]{0:T(128)S(1)}, s32[4]{0:T(128)}, u32[]{:S(2)}) copy-start(s32[4]{0:T(128)} %constant.97.clone) | copy-start | bytes 52
  8.1 13.8 %copy-start.6 = (s32[4]{0:T(128)S(1)}, s32[4]{0:T(128)}, u32[]{:S(2)}) copy-start(s32[4]{0:T(128)} %constant.98.clone) | copy-start | bytes 52
  8.1 15.3 %copy-start.5 = (s32[96,8]{0,1:T(8,128)S(1)}, s32[96,8]{0,1:T(8,128)}, u32[]{:S(2)}) copy-start(s32[96,8]{0,1:T(8,128)} %param.11) | copy-start | bytes 9220
  8.2 15.5 %copy-start.4 = (s32[4,3]{1,0:T(4,128)S(1)}, s32[4,3]{1,0:T(4,128)}, u32[]{:S(2)}) copy-start(s32[4,3]{1,0:T(4,128)} %mom_ref.3) | copy-start | bytes 148
  8.2 24.0 %collective-permute-start = (bf16[768,768]{1,0:T(8,128)(2,1)}, bf16[768,768]{1,0:T(8,128)(2,1)}, u32[]{:S(2)}, u32[]{:S(2)}) collective-permute-start(bf16[768,768]{1,0:T(8,128)(2,1)} %elementals.3), channel_id=1, source_target_pairs={{0,1},{1,0},{2,3},{3,2},{4,5},{5,4},{6,7},{7,6},{8,9},{9,8},{10,11... | collective-permute-start | bytes 3538952 | tf_op jit(solution)/shard_map/elementals/ppermute | solution.py:297
  9.2 9.4 %collective-permute-start.7 = (bf16[384,384]{1,0:T(8,128)(2,1)S(1)}, bf16[384,384]{1,0:T(8,128)(2,1)S(1)}, u32[]{:S(2)}, u32[]{:S(2)}) collective-permute-start(bf16[384,384]{1,0:T(8,128)(2,1)S(1)} %matrices.1.refs_4_), channel_id=1, source_target_pairs={{0,4},{1,5},{2,6},{3,7},{4,0},{5,1},{6,2},{7,3},{8,12},{9,13},{10,... | collective-permute-start | bytes 884744 | tf_op jit(solution)/shard_map/spread/ppermute | solution.py:291
  11.6 17.9 %collective-permute-start.9 = (bf16[384,384]{1,0:T(8,128)(2,1)S(1)}, bf16[384,384]{1,0:T(8,128)(2,1)S(1)}, u32[]{:S(2)}, u32[]{:S(2)}) collective-permute-start(bf16[384,384]{1,0:T(8,128)(2,1)S(1)} %matrices.1.refs_4_), channel_id=1, source_target_pairs={{4,8},{5,9},{6,10},{7,11},{8,4},{9,5},{10,6},{11,7},{20,24},{21,25... | collective-permute-start | bytes 884744 | tf_op jit(solution)/shard_map/spread/ppermute | solution.py:291
  18.6 12.2 %collective-permute-start.12 = (bf16[384,384]{1,0:T(8,128)(2,1)S(1)}, bf16[384,384]{1,0:T(8,128)(2,1)S(1)}, u32[]{:S(2)}, u32[]{:S(2)}) collective-permute-start(bf16[384,384]{1,0:T(8,128)(2,1)S(1)} %collective-permute-done.7.refs_6_), channel_id=1, source_target_pairs={{4,8},{5,9},{6,10},{7,11},{8,4},{9,5},{10,6},{11,7},{20,24},{21,25... | collective-permute-start | bytes 884744 | tf_op jit(solution)/shard_map/spread/ppermute | solution.py:291
  28.5 7.6 %collective-permute-start.6 = (bf16[384,384]{1,0:T(8,128)(2,1)S(1)}, bf16[384,384]{1,0:T(8,128)(2,1)S(1)}, u32[]{:S(2)}, u32[]{:S(2)}) collective-permute-start(bf16[384,384]{1,0:T(8,128)(2,1)S(1)} %matrices.1.refs_4_), channel_id=1, source_target_pairs={{0,2},{1,3},{2,0},{3,1},{4,6},{5,7},{6,4},{7,5},{8,10},{9,11},{10,... | collective-permute-start | bytes 884744 | tf_op jit(solution)/shard_map/spread/ppermute | solution.py:294
  29.6 10.5 %collective-permute-start.10 = (bf16[384,384]{1,0:T(8,128)(2,1)S(1)}, bf16[384,384]{1,0:T(8,128)(2,1)S(1)}, u32[]{:S(2)}, u32[]{:S(2)}) collective-permute-start(bf16[384,384]{1,0:T(8,128)(2,1)S(1)} %collective-permute-done.9), channel_id=1, source_target_pairs={{4,0},{5,1},{6,2},{7,3},{8,12},{9,13},{10,14},{11,15},{20,16},{21,... | collective-permute-start | bytes 884744 | tf_op jit(solution)/shard_map/spread/ppermute | solution.py:291
  30.9 15.6 %collective-permute-start.13 = (bf16[384,384]{1,0:T(8,128)(2,1)S(1)}, bf16[384,384]{1,0:T(8,128)(2,1)S(1)}, u32[]{:S(2)}, u32[]{:S(2)}) collective-permute-start(bf16[384,384]{1,0:T(8,128)(2,1)S(1)} %collective-permute-done.12), channel_id=1, source_target_pairs={{4,0},{5,1},{6,2},{7,3},{8,12},{9,13},{10,14},{11,15},{20,16},{21,... | collective-permute-start | bytes 884744 | tf_op jit(solution)/shard_map/spread/ppermute | solution.py:291
  33.4 26.5 %collective-permute-start.1 = (bf16[384,768]{1,0:T(8,128)(2,1)S(1)}, bf16[384,768]{1,0:T(8,128)(2,1)S(1)}, u32[]{:S(2)}, u32[]{:S(2)}) collective-permute-start(bf16[384,768]{1,0:T(8,128)(2,1)S(1)} %fusion), channel_id=1, source_target_pairs={{0,2},{1,3},{2,0},{3,1},{4,6},{5,7},{6,4},{7,5},{8,10},{9,11},{10,... | collective-permute-start | bytes 1769480 | tf_op jit(solution)/shard_map/elementals/ppermute | solution.py:294
  33.9 15.2 %collective-permute-start.15 = (bf16[384,384]{1,0:T(8,128)(2,1)S(1)}, bf16[384,384]{1,0:T(8,128)(2,1)S(1)}, u32[]{:S(2)}, u32[]{:S(2)}) collective-permute-start(bf16[384,384]{1,0:T(8,128)(2,1)S(1)} %matrices.1.refs_4_), channel_id=1, source_target_pairs={{0,1},{1,0},{2,3},{3,2},{4,5},{5,4},{6,7},{7,6},{8,9},{9,8},{10,11... | collective-permute-start | bytes 884744 | tf_op jit(solution)/shard_map/spread/ppermute | solution.py:297
  36.1 19.1 %collective-permute-start.8 = (bf16[384,384]{1,0:T(8,128)(2,1)S(1)}, bf16[384,384]{1,0:T(8,128)(2,1)S(1)}, u32[]{:S(2)}, u32[]{:S(2)}) collective-permute-start(bf16[384,384]{1,0:T(8,128)(2,1)S(1)} %collective-permute-done.7.refs_6_), channel_id=1, source_target_pairs={{0,2},{1,3},{2,0},{3,1},{4,6},{5,7},{6,4},{7,5},{8,10},{9,11},{10,... | collective-permute-start | bytes 884744 | tf_op jit(solution)/shard_map/spread/ppermute | solution.py:294
  40.1 18.1 %collective-permute-start.17 = (bf16[384,384]{1,0:T(8,128)(2,1)S(1)}, bf16[384,384]{1,0:T(8,128)(2,1)S(1)}, u32[]{:S(2)}, u32[]{:S(2)}) collective-permute-start(bf16[384,384]{1,0:T(8,128)(2,1)S(1)} %collective-permute-done.7.refs_6_), channel_id=1, source_target_pairs={{0,1},{1,0},{2,3},{3,2},{4,5},{5,4},{6,7},{7,6},{8,9},{9,8},{10,11... | collective-permute-start | bytes 884744 | tf_op jit(solution)/shard_map/spread/ppermute | solution.py:297
  46.4 11.8 %collective-permute-start.16 = (bf16[384,384]{1,0:T(8,128)(2,1)S(1)}, bf16[384,384]{1,0:T(8,128)(2,1)S(1)}, u32[]{:S(2)}, u32[]{:S(2)}) collective-permute-start(bf16[384,384]{1,0:T(8,128)(2,1)S(1)} %collective-permute-done.6.refs_5_), channel_id=1, source_target_pairs={{0,1},{1,0},{2,3},{3,2},{4,5},{5,4},{6,7},{7,6},{8,9},{9,8},{10,11... | collective-permute-start | bytes 884744 | tf_op jit(solution)/shard_map/spread/ppermute | solution.py:297
  49.1 12.8 %collective-permute-start.11 = (bf16[384,384]{1,0:T(8,128)(2,1)S(1)}, bf16[384,384]{1,0:T(8,128)(2,1)S(1)}, u32[]{:S(2)}, u32[]{:S(2)}) collective-permute-start(bf16[384,384]{1,0:T(8,128)(2,1)S(1)} %broadcast_select_fusion.1.refs_8_), channel_id=1, source_target_pairs={{0,2},{1,3},{2,0},{3,1},{4,6},{5,7},{6,4},{7,5},{8,10},{9,11},{10,... | collective-permute-start | bytes 884744 | tf_op jit(solution)/shard_map/spread/ppermute | solution.py:294
  55.2 14.4 %collective-permute-start.19 = (bf16[384,384]{1,0:T(8,128)(2,1)S(1)}, bf16[384,384]{1,0:T(8,128)(2,1)S(1)}, u32[]{:S(2)}, u32[]{:S(2)}) collective-permute-start(bf16[384,384]{1,0:T(8,128)(2,1)S(1)} %broadcast_select_fusion.1.refs_8_), channel_id=1, source_target_pairs={{0,1},{1,0},{2,3},{3,2},{4,5},{5,4},{6,7},{7,6},{8,9},{9,8},{10,11... | collective-permute-start | bytes 884744 | tf_op jit(solution)/shard_map/spread/ppermute | solution.py:297
  58.2 15.1 %collective-permute-start.18 = (bf16[384,384]{1,0:T(8,128)(2,1)S(1)}, bf16[384,384]{1,0:T(8,128)(2,1)S(1)}, u32[]{:S(2)}, u32[]{:S(2)}) collective-permute-start(bf16[384,384]{1,0:T(8,128)(2,1)S(1)} %collective-permute-done.8.refs_7_), channel_id=1, source_target_pairs={{0,1},{1,0},{2,3},{3,2},{4,5},{5,4},{6,7},{7,6},{8,9},{9,8},{10,11... | collective-permute-start | bytes 884744 | tf_op jit(solution)/shard_map/spread/ppermute | solution.py:297
  58.2 9.6 %collective-permute-start.14 = (bf16[384,384]{1,0:T(8,128)(2,1)S(1)}, bf16[384,384]{1,0:T(8,128)(2,1)S(1)}, u32[]{:S(2)}, u32[]{:S(2)}) collective-permute-start(bf16[384,384]{1,0:T(8,128)(2,1)S(1)} %broadcast_select_fusion.refs_10_), channel_id=1, source_target_pairs={{0,2},{1,3},{2,0},{3,1},{4,6},{5,7},{6,4},{7,5},{8,10},{9,11},{10,... | collective-permute-start | bytes 884744 | tf_op jit(solution)/shard_map/spread/ppermute | solution.py:294
  59.9 13.4 %collective-permute-start.21 = (bf16[384,384]{1,0:T(8,128)(2,1)S(1)}, bf16[384,384]{1,0:T(8,128)(2,1)S(1)}, u32[]{:S(2)}, u32[]{:S(2)}) collective-permute-start(bf16[384,384]{1,0:T(8,128)(2,1)S(1)} %broadcast_select_fusion.refs_10_), channel_id=1, source_target_pairs={{0,1},{1,0},{2,3},{3,2},{4,5},{5,4},{6,7},{7,6},{8,9},{9,8},{10,11... | collective-permute-start | bytes 884744 | tf_op jit(solution)/shard_map/spread/ppermute | solution.py:297
  61.9 14.0 %collective-permute-start.20 = (bf16[384,384]{1,0:T(8,128)(2,1)S(1)}, bf16[384,384]{1,0:T(8,128)(2,1)S(1)}, u32[]{:S(2)}, u32[]{:S(2)}) collective-permute-start(bf16[384,384]{1,0:T(8,128)(2,1)S(1)} %collective-permute-done.11.refs_9_), channel_id=1, source_target_pairs={{0,1},{1,0},{2,3},{3,2},{4,5},{5,4},{6,7},{7,6},{8,9},{9,8},{10,11... | collective-permute-start | bytes 884744 | tf_op jit(solution)/shard_map/spread/ppermute | solution.py:297
  67.8 15.7 %collective-permute-start.22 = (bf16[384,384]{1,0:T(8,128)(2,1)S(1)}, bf16[384,384]{1,0:T(8,128)(2,1)S(1)}, u32[]{:S(2)}, u32[]{:S(2)}) collective-permute-start(bf16[384,384]{1,0:T(8,128)(2,1)S(1)} %collective-permute-done.14.refs_11_), channel_id=1, source_target_pairs={{0,1},{1,0},{2,3},{3,2},{4,5},{5,4},{6,7},{7,6},{8,9},{9,8},{10,11... | collective-permute-start | bytes 884744 | tf_op jit(solution)/shard_map/spread/ppermute | solution.py:297
  69.6 7.3 %collective-permute-start.2 = (bf16[96,768]{1,0:T(8,128)(2,1)S(1)}, bf16[96,768]{1,0:T(8,128)(2,1)S(1)}, u32[]{:S(2)}, u32[]{:S(2)}) collective-permute-start(bf16[96,768]{1,0:T(8,128)(2,1)S(1)} %get-tuple-element.9), channel_id=1, source_target_pairs={{0,4},{1,5},{2,6},{3,7},{4,8},{5,9},{6,10},{7,11},{8,12},{9,13},{1... | collective-permute-start | bytes 442376 | tf_op jit(solution)/shard_map/elementals/ppermute | solution.py:291
  73.3 10.2 %collective-permute-start.3 = (bf16[96,768]{1,0:T(8,128)(2,1)S(1)}, bf16[96,768]{1,0:T(8,128)(2,1)S(1)}, u32[]{:S(2)}, u32[]{:S(2)}) collective-permute-start(bf16[96,768]{1,0:T(8,128)(2,1)S(1)} %get-tuple-element.8), channel_id=1, source_target_pairs={{0,8},{1,9},{2,10},{3,11},{4,12},{5,13},{6,14},{7,15},{8,0},{9,1},... | collective-permute-start | bytes 442376 | tf_op jit(solution)/shard_map/elementals/ppermute | solution.py:291
  73.3 10.2 %collective-permute-start.4 = (bf16[96,768]{1,0:T(8,128)(2,1)S(1)}, bf16[96,768]{1,0:T(8,128)(2,1)S(1)}, u32[]{:S(2)}, u32[]{:S(2)}) collective-permute-start(bf16[96,768]{1,0:T(8,128)(2,1)S(1)} %get-tuple-element.7), channel_id=1, source_target_pairs={{0,12},{1,13},{2,14},{3,15},{4,0},{5,1},{6,2},{7,3},{8,4},{9,5},{1... | collective-permute-start | bytes 442376 | tf_op jit(solution)/shard_map/elementals/ppermute | solution.py:291

commit v2 on v1

--- a/solution.py
+++ b/solution.py
@@ -119,7 +119,7 @@
 
 CORES = 2
 PAIR = 2
-VMEM_LIMIT = 40 * 1024 * 1024
+VMEM_LIMIT = 20 * 1024 * 1024
 
 
 def whole(space):
@@ -138,86 +138,116 @@
     )
 
 
-def product_kernel(core_ref, own_ref, other_ref, out_ref):
+def product_kernel(flip, core_ref, own_ref, other_ref, after_ref, out_ref):
+    def real(even, odd):
+        out_ref[...] = (nt_dot(even[0], odd[0]) + nt_dot(even[1], odd[1])).astype(out_ref.dtype)
+
+    def imag(even, odd):
+        out_ref[...] = (nt_dot(even[1], odd[0]) - nt_dot(even[0], odd[1])).astype(out_ref.dtype)
+
+    first, second = (imag, real) if flip else (real, imag)
+
     @pl.when(core_ref[0] == 0)
     def _():
-        out_ref[...] = (
-            nt_dot(own_ref[0], other_ref[0]) + nt_dot(own_ref[1], other_ref[1])
-        ).astype(out_ref.dtype)
+        first(own_ref, other_ref)
 
     @pl.when(core_ref[0] != 0)
     def _():
-        out_ref[...] = (
-            nt_dot(other_ref[1], own_ref[0]) - nt_dot(other_ref[0], own_ref[1])
-        ).astype(out_ref.dtype)
-
-
-def partial_kernel(rows, chain, keep, place_ref, mom_ref, v_ref, out_ref, left_ref, right_ref):
+        second(other_ref, own_ref)
+
+
+def partial_kernel(rows, chain, stay, place_ref, mom_ref, v_ref, *refs):
+    away_ref, keep_ref, left_ref, right_ref, cos_ref, sin_ref = refs[-6:]
     num_vec, sites = v_ref.shape[2], v_ref.shape[3]
-    colours = v_ref.shape[1]
+    colours, momenta = v_ref.shape[1], mom_ref.shape[0]
+    height = chain * rows
     zed, why, core = place_ref[0], place_ref[1], place_ref[2]
     position = (zed * PAIR + why) * CORES + core
-    side = core if keep else 1 - core
-    for c in range(colours):
-        for part in range(2):
-            column = pl.ds((part * colours + c) * sites, sites)
-            right_ref[:num_vec, column] = v_ref[part, c]
-            if part == 1:
-                right_ref[num_vec:, column] = -v_ref[0, c]
-            else:
-                right_ref[num_vec:, column] = v_ref[1, c]
-    site = position * sites + lax.broadcasted_iota(jnp.int32, (1, sites), 1)
+    target_y = why if stay else 1 - why
+    for part in range(2):
+        for c in range(colours):
+            right_ref[pl.ds(part * num_vec, num_vec), pl.ds(c * sites, sites)] = v_ref[part, c]
+    site = position * sites + lax.broadcasted_iota(jnp.int32, (momenta, sites), 1)
     coord_x = site & (EXTENT - 1)
     coord_y = lax.div(site, EXTENT) & (EXTENT - 1)
     coord_z = lax.div(site, EXTENT * EXTENT)
-    for shift in range(chain):
-        for half in range(PAIR):
-            target_z = lax.rem(zed + shift, chain)
-            target_y = why if half else 1 - why
+    which = lax.broadcasted_iota(jnp.int32, (momenta, sites), 0)
+    wave = jnp.zeros((momenta, sites), jnp.int32)
+    for q in range(momenta):
+        turned = mom_ref[q, 0] * coord_x + mom_ref[q, 1] * coord_y + mom_ref[q, 2] * coord_z
+        wave = jnp.where(which == q, turned & (EXTENT - 1), wave)
+    angle = wave.astype(jnp.float32) * (2.0 * math.pi / EXTENT)
+    cos_ref[...] = jnp.cos(angle)
+    sin_ref[...] = jnp.sin(angle)
+    for keep, out_ref in ((False, away_ref), (True, keep_ref)):
+        side = core if keep else 1 - core
+        base = keep * 2 * height
+        for turn in range(chain):
+            target_z = lax.rem(zed + turn, chain)
             first = ((target_z * PAIR + target_y) * CORES + side) * rows
             momentum = lax.div(first, num_vec)
             start = pl.multiple_of(lax.rem(first, num_vec), rows)
-            wave = (
-                mom_ref[momentum, 0] * coord_x
-                + mom_ref[momentum, 1] * coord_y
-                + mom_ref[momentum, 2] * coord_z
-            ) & (EXTENT - 1)
-            angle = wave.astype(jnp.float32) * (2.0 * math.pi / EXTENT)
-            cosine, sine = jnp.cos(angle), jnp.sin(angle)
-            place = pl.ds((half * chain + shift) * rows, rows)
+            cosine, sine = cos_ref[pl.ds(momentum, 1), :], sin_ref[pl.ds(momentum, 1), :]
             for c in range(colours):
                 vec_re = v_ref[0, c, pl.ds(start, rows), :].astype(jnp.float32)
                 vec_im = v_ref[1, c, pl.ds(start, rows), :].astype(jnp.float32)
-                left_ref[place, pl.ds(c * sites, sites)] = (
+                column = pl.ds(c * sites, sites)
+                left_ref[pl.ds(base + turn * rows, rows), column] = (
                     vec_re * cosine - vec_im * sine
                 ).astype(jnp.bfloat16)
-                left_ref[place, pl.ds((colours + c) * sites, sites)] = (
+                left_ref[pl.ds(base + height + turn * rows, rows), column] = (
                     vec_re * sine + vec_im * cosine
                 ).astype(jnp.bfloat16)
-    out_ref[...] = nt_dot(left_ref[...], right_ref[...]).astype(out_ref.dtype)
-
-
-def partial_rows(rows, chain, keep, place, momenta, vectors):
+        both = nt_dot(left_ref[pl.ds(base, 2 * height), :], right_ref[...])
+        out_ref[:, :num_vec] = (both[:height, :num_vec] + both[height:, num_vec:]).astype(out_ref.dtype)
+        out_ref[:, num_vec:] = (both[:height, num_vec:] - both[height:, :num_vec]).astype(out_ref.dtype)
+
+
+def partial_rows(rows, chain, stay, place, momenta, vectors, *after):
     _, colours, num_vec, sites = vectors.shape
-    depth = 2 * colours * sites
-    height = PAIR * chain * rows
-    dtype = jnp.float32 if keep else jnp.bfloat16
+    depth = colours * sites
+    height = chain * rows
     return pl.pallas_call(
-        functools.partial(partial_kernel, rows, chain, keep),
-        out_shape=jax.ShapeDtypeStruct((height, 2 * num_vec), dtype),
-        in_specs=[whole(pltpu.SMEM), whole(pltpu.SMEM), whole(pltpu.VMEM)],
-        out_specs=whole(pltpu.VMEM),
+        functools.partial(partial_kernel, rows, chain, stay),
+        out_shape=(
+            jax.ShapeDtypeStruct((height, 2 * num_vec), jnp.bfloat16),
+            jax.ShapeDtypeStruct((height, 2 * num_vec), jnp.float32),
+        ),
+        in_specs=[whole(pltpu.SMEM), whole(pltpu.SMEM), whole(pltpu.VMEM)] + [whole(pl.ANY)] * len(after),
+        out_specs=(whole(pltpu.VMEM), whole(pltpu.VMEM)),
         scratch_shapes=[
-            pltpu.VMEM((height, depth), jnp.bfloat16),
+            pltpu.VMEM((4 * height, depth), jnp.bfloat16),
             pltpu.VMEM((2 * num_vec, depth), jnp.bfloat16),
+            pltpu.VMEM((momenta.shape[0], sites), jnp.float32),
+            pltpu.VMEM((momenta.shape[0], sites), jnp.float32),
         ],
         compiler_params=pltpu.CompilerParams(vmem_limit_bytes=VMEM_LIMIT),
-        cost_estimate=pl.CostEstimate(
-            flops=2 * height * depth * 2 * num_vec,
-            bytes_accessed=vectors.size * 2 + height * 2 * num_vec * 4,
-            transcendentals=0,
-        ),
-    )(place, momenta, vectors)
+        cost_estimate=pl.CostEstimate(flops=16 * height * depth * num_vec, bytes_accessed=vectors.size * 2 + height * num_vec * 12, transcendentals=0),
+    )(place, momenta, vectors, *after)
+
+
+def total_kernel(count, *refs):
+    total = refs[0][...].astype(jnp.float32)
+    for term in refs[1:count]:
+        total = total + term[...].astype(jnp.float32)
+    refs[-1][...] = total.astype(jnp.bfloat16)
+
+
+def total(terms, *passed):
+    def kernel(*refs):
+        count = len(terms)
+        total_kernel(count, *refs[:count], refs[count + len(passed)])
+
+    return pl.pallas_call(
+        kernel,
+        out_shape=(jax.ShapeDtypeStruct(terms[0].shape, jnp.bfloat16),)
+        + tuple(jax.ShapeDtypeStruct(block.shape, block.dtype) for block in passed),
+        in_specs=[whole(pltpu.VMEM)] * len(terms) + [whole(pl.ANY)] * len(passed),
+        out_specs=(whole(pltpu.VMEM),) + (whole(pl.ANY),) * len(passed),
+        input_output_aliases={len(terms) + i: 1 + i for i in range(len(passed))},
+        compiler_params=pltpu.CompilerParams(vmem_limit_bytes=VMEM_LIMIT),
+        cost_estimate=pl.CostEstimate(flops=4 * terms[0].size, bytes_accessed=10 * terms[0].size, transcendentals=0),
+    )(*terms, *passed)
 
 
 def owner_products(core, stacked, own, other, even_ref, odd_ref):
@@ -238,18 +268,19 @@
         ref[:, num_vec:] = imag.astype(jnp.bfloat16)
 
 
-def contract_kernel(slots, arrivals, group, core_ref, *refs):
+def rows_kernel(slots, arrivals, core_ref, *refs):
     terms, refs = refs[:arrivals], refs[arrivals:]
-    own, refs = refs[:slots], refs[slots:]
-    other, refs = refs[:slots], refs[slots:]
-    pick_ref, out_ref, full_ref = refs
-    rows, fanout, width = out_ref.shape
-    num_vec = width // 2
-    total = terms[0][...].astype(jnp.float32)
-    for term in terms[1:]:
-        total = total + term[...].astype(jnp.float32)
+    own, other = refs[:slots], refs[slots : 2 * slots]
+    stacked_ref, full_ref = refs[2 * slots :]
+    num_vec = terms[0].shape[1] // 2
+    rows = stacked_ref.shape[0] // 2
+    total = 0.0
+    for term in terms:
+        for at in range(0, term.shape[0], rows):
+            total = total + term[pl.ds(at, rows), :].astype(jnp.float32)
     elemental = total.astype(jnp.bfloat16)
     stacked = jnp.concatenate([elemental[:, :num_vec], elemental[:, num_vec:]], axis=0)
+    stacked_ref[...] = stacked
     for slot in range(slots):
         owner_products(
             core_ref[0],
@@ -259,12 +290,38 @@
             full_ref.at[2 * slot],
             full_ref.at[2 * slot + 1],
         )
+
+
+def pick_kernel(slots, group, core_ref, stacked_ref, first_ref, *refs):
+    own, other = refs[:slots], refs[slots : 2 * slots]
+    pick_ref, out_ref, last_ref = refs[2 * slots :]
+    rows, fanout, width = out_ref.shape
+    stacked = stacked_ref[...]
+    for slot in range(slots):
+        owner_products(
+            core_ref[0],
+            stacked,
+            own[slot][...],
+            other[slot][...],
+            last_ref.at[2 * slot],
+            last_ref.at[2 * slot + 1],
+        )
     for block in range(rows // group):
-        table = full_ref[:, pl.ds(block * group, group), :].reshape(2 * slots * group, width)
+        there = pl.ds(block * group, group)
+        table = jnp.concatenate(
+            [
+                first_ref[:, there, :].reshape(first_ref.shape[0] * group, width),
+                last_ref[:, there, :].reshape(2 * slots * group, width),
+            ],
+            axis=0,
+        )
         picked = nn_dot(pick_ref[pl.ds(block * group * fanout, group * fanout), :], table)
-        out_ref[pl.ds(block * group, group)] = picked.astype(jnp.bfloat16).reshape(
-            group, fanout, width
-        )
+        out_ref[there] = picked.astype(jnp.bfloat16).reshape(group, fanout, width)
+
+
+def named(name, step):
+    with jax.named_scope(name):
+        return step()
 
 
 def gather_plan(eigvecs, momenta, peram, graph):
@@ -298,80 +355,117 @@
 
     with jax.named_scope("matrices"):
         mine = peram[0]
-        own = pl.pallas_call(
-            product_kernel,
-            out_shape=jax.ShapeDtypeStruct((num_vec, num_vec), jnp.bfloat16),
-            in_specs=[whole(pltpu.SMEM), whole(pltpu.VMEM), whole(pltpu.VMEM)],
-            out_specs=whole(pltpu.VMEM),
-            compiler_params=pltpu.CompilerParams(vmem_limit_bytes=VMEM_LIMIT),
-            cost_estimate=pl.CostEstimate(
-                flops=4 * num_vec**3, bytes_accessed=10 * num_vec**2, transcendentals=0
-            ),
-        )(core_at, mine, swap(mine))
+        theirs = named("swapP", lambda: swap(mine))
+
+        def matrix(flip, after):
+            return pl.pallas_call(
+                functools.partial(product_kernel, flip),
+                out_shape=jax.ShapeDtypeStruct((num_vec, num_vec), jnp.bfloat16),
+                in_specs=[whole(pltpu.SMEM), whole(pltpu.VMEM), whole(pltpu.VMEM), whole(pl.ANY)],
+                out_specs=whole(pltpu.VMEM),
+                compiler_params=pltpu.CompilerParams(vmem_limit_bytes=VMEM_LIMIT),
+                cost_estimate=pl.CostEstimate(flops=4 * num_vec**3, bytes_accessed=10 * num_vec**2, transcendentals=0),
+            )(core_at, mine, theirs, after)
+
+        own = matrix(False, core_at)
     inner = (zed > 0) & (zed < chain - 1)
-    with jax.named_scope("spread"):
-        near = send(own, [(0, 1), (1, 0), (2, 3), (3, 2)])
-        middle = send(own, [(1, 2), (2, 1)])
-        outward = send(middle, [(1, 0), (2, 3)])
-        third = jnp.where(inner, middle, outward)
-        crossing = send(near, [(1, 2), (2, 1)])
-        last = send(crossing, [(1, 0), (2, 3)])
-        fourth = jnp.where(inner, crossing, last)
-        held = [own, across(own), near, across(near), third, across(third), fourth, across(fourth)]
-        swapped = [swap(block) for block in held]
-        columns = []
-        for step in range(chain):
-            source = jnp.asarray(SOURCES[step], jnp.int32)[zed]
-            for other in range(PAIR):
-                chip = source * PAIR + (why ^ other)
-                columns += [chip * CORES, chip * CORES + 1]
+    half = chain * rows
     with jax.named_scope("elementals"):
         vectors = jnp.transpose(eigvecs, (0, 2, 1, 3))
-        away = partial_rows(rows, chain, False, place, momenta, vectors)
-        arrived = swap(away)
-        kept = partial_rows(rows, chain, True, place, momenta, vectors)
-        half = chain * rows
-        outgoing = (kept[:half] + arrived[:half].astype(jnp.float32)).astype(jnp.bfloat16)
-        crossed = across(outgoing)
-        summed = kept[half:] + arrived[half:].astype(jnp.float32) + crossed.astype(jnp.float32)
+        away_cross, kept_cross = partial_rows(rows, chain, False, place, momenta, vectors)
+        away_stay, kept_stay = partial_rows(rows, chain, True, place, momenta, vectors, own)
+        got_cross = named("swapA", lambda: swap(away_cross))
+    with jax.named_scope("spread"):
+        near = named("near", lambda: send(own, [(0, 1), (1, 0), (2, 3), (3, 2)]))
+        middle = named("middle", lambda: send(own, [(1, 2), (2, 1)]))
+        beside = named("beside", lambda: across(own))
+    with jax.named_scope("elementals"):
+        outgoing, near, middle, away_stay = total([kept_cross, got_cross], near, middle, away_stay)
+        crossed = named("RSy", lambda: across(outgoing))
+        got_stay = named("swapB", lambda: swap(away_stay))
+    with jax.named_scope("spread"):
+        third_in = named("third_in", lambda: send(near, [(1, 2), (2, 1)]))
+        third_out = named("third_out", lambda: send(middle, [(1, 0), (2, 3)]))
+        ends = named("ends", lambda: send(third_in, [(1, 0), (2, 3)]))
+        twin = matrix(True, outgoing)
+        third = jnp.where(inner, third_in, third_out)
+        fourth = jnp.where(inner, middle, ends)
+        twin_beside, twin_near = [named("swE", lambda: swap(block)) for block in (beside, near)]
+    with jax.named_scope("elementals"):
+        summed, near, third, twin, twin_beside, twin_near = total(
+            [kept_stay, got_stay, crossed], near, third, twin, twin_beside, twin_near
+        )
+    with jax.named_scope("spread"):
+        beside_near, beside_third = [named("Y", lambda: across(block)) for block in (near, third)]
+        early = [own, beside, near, third, beside_near, beside_third]
+        early_twins = [twin, twin_beside, twin_near]
+        early_twins += [named("swE", lambda: swap(block)) for block in (third, beside_near, beside_third)]
+        late = [fourth, named("Yf", lambda: across(fourth))]
+        late_twins = [named("swL", lambda: swap(block)) for block in late]
+    with jax.named_scope("elementals"):
         terms = [summed[:rows]]
         for shift in range(1, chain):
-            chunk = summed[shift * rows : (shift + 1) * rows].astype(jnp.bfloat16)
-            terms.append(send(chunk, [(z, (z + shift) % chain) for z in range(chain)]))
+            moves = [(z, (z + shift) % chain) for z in range(chain)]
+            chunk = summed[shift * rows : (shift + 1) * rows]
+            terms.append(named("RSz", lambda: send(chunk, moves)))
     with jax.named_scope("pick"):
         group = 16
-        owner_of = jnp.repeat(jnp.stack(columns), group)
+        near_z, third_z, fourth_z = zed ^ 1, (zed + 2) % chain, chain - 1 - zed
+        chips = []
+        for z, y in (
+            (zed, why),
+            (zed, 1 - why),
+            (near_z, why),
+            (third_z, why),
+            (near_z, 1 - why),
+            (third_z, 1 - why),
+            (fourth_z, why),
+            (fourth_z, 1 - why),
+        ):
+            chips.append(z * PAIR + y)
+        columns = jnp.arange(spaces * group, dtype=jnp.int32)
+        slot_of = columns // (CORES * group)
+        owner_of = columns // group % CORES
+        for slot, chip in enumerate(chips):
+            owner_of = owner_of + jnp.where(slot_of == slot, chip * CORES, 0)
         row_of = jnp.arange(rows * fanout, dtype=jnp.int32) // fanout % group
-        place_of = jnp.arange(spaces * group, dtype=jnp.int32) % group
         pick = (
             (graph.reshape(-1)[:, None] == owner_of[None, :])
-            & (row_of[:, None] == place_of[None, :])
+            & (row_of[:, None] == (columns % group)[None, :])
         ).astype(jnp.bfloat16)
     with jax.named_scope("contract"):
-        slots = len(held)
+        slots = len(early)
+        stacked, first = pl.pallas_call(
+            functools.partial(rows_kernel, slots, len(terms)),
+            out_shape=(
+                jax.ShapeDtypeStruct((2 * rows, num_vec), jnp.bfloat16),
+                jax.ShapeDtypeStruct((2 * slots, rows, 2 * num_vec), jnp.bfloat16),
+            ),
+            in_specs=[whole(pltpu.SMEM)] + [whole(pltpu.VMEM)] * (len(terms) + 2 * slots),
+            out_specs=(whole(pltpu.VMEM), whole(pltpu.VMEM)),
+            compiler_params=pltpu.CompilerParams(vmem_limit_bytes=VMEM_LIMIT),
+            cost_estimate=pl.CostEstimate(flops=16 * slots * rows * num_vec**2, bytes_accessed=8 * slots * num_vec**2, transcendentals=0),
+        )(core_at, *terms, *early, *early_twins)
+        slots = len(late)
         return pl.pallas_call(
-            functools.partial(contract_kernel, slots, len(terms), group),
+            functools.partial(pick_kernel, slots, group),
             out_shape=jax.ShapeDtypeStruct((rows, fanout, 2 * num_vec), jnp.bfloat16),
-            in_specs=[whole(pltpu.SMEM)] + [whole(pltpu.VMEM)] * (len(terms) + 2 * slots + 1),
+            in_specs=[whole(pltpu.SMEM)] + [whole(pltpu.VMEM)] * (2 + 2 * slots + 1),
             out_specs=whole(pltpu.VMEM),
             scratch_shapes=[pltpu.VMEM((2 * slots, rows, 2 * num_vec), jnp.bfloat16)],
             compiler_params=pltpu.CompilerParams(vmem_limit_bytes=VMEM_LIMIT),
-            cost_estimate=pl.CostEstimate(
-                flops=16 * slots * rows * num_vec**2,
-                bytes_accessed=4 * slots * num_vec**2,
-                transcendentals=0,
-            ),
-        )(core_at, *terms, *held, *swapped, pick)
-
-
-SOURCES = ((0, 1, 2, 3), (1, 0, 3, 2), (2, 2, 1, 1), (3, 3, 0, 0))
+            cost_estimate=pl.CostEstimate(flops=16 * slots * rows * num_vec**2, bytes_accessed=8 * slots * num_vec**2, transcendentals=0),
+        )(core_at, stacked, first, *late, *late_twins, pick)
+
+
+LINE = 4
 
 
 def on_device(eigvecs, momenta, peram, graph):
     num_vec = eigvecs.shape[1]
     spaces = lax.axis_size("space")
     rows = momenta.shape[0] * num_vec // spaces
-    if spaces == CORES * PAIR * len(SOURCES) and num_vec % rows == 0 and rows % 16 == 0:
+    if spaces == CORES * PAIR * LINE and num_vec % rows == 0 and rows % 16 == 0:
         return gather_plan(eigvecs, momenta, peram, graph)
     return exchange_plan(eigvecs, momenta, peram, graph)
 

time: 90.5 us -> 72.9 us (0.81); the launches traced: 88.7 us -> 72.6 us
  starting transfers between devices: 33.9 us -> 24.2 us
  waiting for transfers between devices: 28.8 us -> 25.6 us
  between operations: 2.23 us -> 0.24 us
  Pallas kernels: 16.3 us -> 18.2 us
  other arithmetic: 2.95 us -> 1.41 us
  local copies, waits for them, and re-layouts: 4.51 us -> 2.97 us
    ppermute x10, starting transfers between devices: 17.3 us -> 8.95 us  [swap(): return lax.ppermute(block, 'space', [(i, i ^ 1) for i in range(spaces)])]
    ppermute x5, waiting for transfers between devices: 9.79 us -> 2.52 us  [across(): return lax.ppermute(block, 'space', [(i, i ^ CORES) for i in range(spaces)])]
    ppermute x8, waiting for transfers between devices: 19 us -> 23 us  [send(): return lax.ppermute(block, 'space', route)]
    pallas_call x4 -> x8, Pallas kernels: 16.3 us -> 18.2 us  [the longest x2 8.39 us: partial_rows(): pl.pallas_call(functools.partial(partial_kernel, rows, chain, stay), out_...]
    dynamic_slice x3 -> x0, local copies, waits for them, and re-layouts: 1.85 us -> none  [gather_plan(): source = jnp.asarray(SOURCES[step], jnp.int32)[zed]]
    ppermute x8, starting transfers between devices: 12.3 us -> 10.8 us  [send(): return lax.ppermute(block, 'space', route)]
    another operation x1 -> x0, other arithmetic: 1.3 us -> none
    convert_element_type x1 -> x0, other arithmetic: 1.21 us -> none  [gather_plan(): (kept[:half] + arrived[:half].astype(jnp.float32)).astype(jnp.bfloat16)]
  transfers between devices with their start and end apart: 23 -> 23, of which waited for: 8 -> 5; matrix products, arithmetic and copies ran while one was open for 6% -> 2% of each run, Pallas kernels for 13% -> 22%
where the time goes in v2:
time: 72.9 us; the launch traced here: 72.6 us
  waiting for transfers between devices  25.6 us (35%)
  starting transfers between devices  24.2 us (33%)
  Pallas kernels  18.2 us (25%)
  local copies, waits for them, and re-layouts  2.97 us (4%)
  other arithmetic  1.41 us (2%)
    ppermute x8, waiting for transfers between devices, send(): return lax.ppermute(block, 'space', route)  23 us
    ppermute x8, starting transfers between devices, send(): return lax.ppermute(block, 'space', route)  10.8 us
    ppermute x10, starting transfers between devices, swap(): return lax.ppermute(block, 'space', [(i, i ^ 1) for i in range(spaces)])  8.95 us
    pallas_call x2, Pallas kernels, partial_rows(): pl.pallas_call(functools.partial(partial_kernel, rows, chain, stay), out_...  8.39 us
    ppermute x5, starting transfers between devices, across(): return lax.ppermute(block, 'space', [(i, i ^ CORES) for i in range(spaces)])  4.48 us
    pallas_call x1, Pallas kernels, gather_plan(): pl.pallas_call(functools.partial(rows_kernel, slots, len(terms)), out_sha...  3.88 us
    unnamed x17, local copies, waits for them, and re-layouts  2.84 us
    ppermute x5, waiting for transfers between devices, across(): return lax.ppermute(block, 'space', [(i, i ^ CORES) for i in range(spaces)])  2.52 us
  transfers between devices with their start and end apart: 23, of which 5 were waited for; matrix products, arithmetic and copies ran while one was open for 2% of the time, Pallas kernels for 22%

profile of v2, /device:TPU:1, one launch (start us, length us, event | category | flops | bytes accessed | tf_op | source)
XLA Modules:
  0.0 72.6 jit_solution(9474124696512065155)
XLA Ops:
  0.0 0.1 collective-permute-start
  0.1 0.1 pad_add_fusion.place_ref
  0.1 1.5 %copy-done.1 = bf16[2,384,3,384]{3,1,2,0:T(8,128)(2,1)S(1)} copy-done((bf16[2,384,3,384]{3,1,2,0:T(8,128)(2,1)S(1)}, bf16[2,384,3,384]{3,1,2,0:T(8,128)(2,1)}, u32[]{:S(2)}) %copy-start.1) | copy-done | bytes 1769496
  1.6 0.7 copy-done.3
  2.3 4.2 %elementals.5 = (bf16[384,768]{1,0:T(8,128)(2,1)S(1)}, f32[384,768]{1,0:T(8,128)S(1)}) custom-call(s32[3]{0:T(128)S(1)} %pad_add_fusion.place_ref, s32[4,3]{1,0:T(4,128)S(1)} %copy-done.3, bf16[2,3,384,384]{3,2,1,0:T(8,128)(2,1)S(1)} %bitcast.8), custom_call_target="tpu_custom_call" | custom-call | flops 2717908992 | bytes 3538944 | tf_op jit(solution)/shard_map/elementals/pallas_call | solution.py:210
  6.5 0.0 copy-start.4
  6.5 0.5 collective-permute-start.1
  7.0 0.0 collective-permute-done.other_ref
  7.1 0.5 matrices.1.refs_0_.refs_4_
  7.6 2.4 %collective-permute-start.2 = (bf16[384,384]{1,0:T(8,128)(2,1)S(1)}, bf16[384,384]{1,0:T(8,128)(2,1)S(1)}, u32[]{:S(2)}, u32[]{:S(2)}) collective-permute-start(bf16[384,384]{1,0:T(8,128)(2,1)S(1)} %matrices.1.refs_0_.refs_4_), channel_id=1, source_target_pairs={{0,4},{1,5},{2,6},{3,7},{4,0},{5,1},{6,2},{7,3},{8,12},{9,13},{10,... | collective-permute-start | bytes 884744 | tf_op jit(solution)/shard_map/spread/near/ppermute | solution.py:348
  10.0 0.7 collective-permute-start.3
  10.7 1.3 %collective-permute-start.8 = (bf16[384,384]{1,0:T(8,128)(2,1)S(1)}, bf16[384,384]{1,0:T(8,128)(2,1)}, u32[]{:S(2)}, u32[]{:S(2)}) collective-permute-start(bf16[384,384]{1,0:T(8,128)(2,1)S(1)} %matrices.1.refs_0_.refs_4_), channel_id=1, source_target_pairs={{0,2},{1,3},{2,0},{3,1},{4,6},{5,7},{6,4},{7,5},{8,10},{9,11},{10,... | collective-permute-start | bytes 884744 | tf_op jit(solution)/shard_map/spread/beside/ppermute | solution.py:351
  12.0 4.2 %elementals.4 = (bf16[384,768]{1,0:T(8,128)(2,1)}, f32[384,768]{1,0:T(8,128)S(1)}) custom-call(s32[3]{0:T(128)S(1)} %pad_add_fusion.place_ref, s32[4,3]{1,0:T(4,128)S(1)} %copy-done.4, bf16[2,3,384,384]{3,2,1,0:T(8,128)(2,1)S(1)} %bitcast.9, bf16[384,384]{1,0:T(8,128)(2,1)S(1)} %matrices.1.refs_0_.refs_4_), custom_call_target="tpu_custom_call" | custom-call | flops 2717908992 | bytes 3538944 | tf_op jit(solution)/shard_map/elementals/pallas_call | solution.py:210
  16.2 0.0 collective-permute-done.1.refs_1_
  16.2 0.9 %collective-permute-done.2.refs_2_ = bf16[384,384]{1,0:T(8,128)(2,1)S(1)} collective-permute-done((bf16[384,384]{1,0:T(8,128)(2,1)S(1)}, bf16[384,384]{1,0:T(8,128)(2,1)S(1)}, u32[]{:S(2)}, u32[]{:S(2)}) %collective-permute-start.2) | collective-permute-done | bytes 294944 | tf_op jit(solution)/shard_map/spread/near/ppermute | solution.py:348
  17.1 0.0 collective-permute-done.3.refs_3_
  17.1 0.9 %elementals.6 = (bf16[384,768]{1,0:T(8,128)(2,1)}, bf16[384,384]{1,0:T(8,128)(2,1)S(1)}, bf16[384,384]{1,0:T(8,128)(2,1)S(1)}, bf16[384,768]{1,0:T(8,128)(2,1)}) custom-call(f32[384,768]{1,0:T(8,128)S(1)} %get-tuple-element.22.refs_0_, ...), custom_call_target="tpu_custom_call", output_to_operand_aliasing={{1}: (2, {}), {2}: (3, {}), {3}: (4, {})} | custom-call | flops 1179648 | bytes 2949120 | tf_op jit(solution)/shard_map/elementals/pallas_call | solution.py:241
  18.0 0.7 collective-permute-start.6
  18.7 0.9 %collective-permute-start.4 = (bf16[384,768]{1,0:T(8,128)(2,1)}, bf16[384,768]{1,0:T(8,128)(2,1)}, u32[]{:S(2)}, u32[]{:S(2)}) collective-permute-start(bf16[384,768]{1,0:T(8,128)(2,1)} %get-tuple-element.25), channel_id=1, source_target_pairs={{0,1},{1,0},{2,3},{3,2},{4,5},{5,4},{6,7},{7,6},{8,9},{9,8},{10,11... | collective-permute-start | bytes 1769480 | tf_op jit(solution)/shard_map/elementals/swapB/ppermute | solution.py:354
  19.6 1.4 %collective-permute-start.5 = (bf16[384,768]{1,0:T(8,128)(2,1)}, bf16[384,768]{1,0:T(8,128)(2,1)}, u32[]{:S(2)}, u32[]{:S(2)}) collective-permute-start(bf16[384,768]{1,0:T(8,128)(2,1)} %get-tuple-element.26.after_ref), channel_id=1, source_target_pairs={{0,2},{1,3},{2,0},{3,1},{4,6},{5,7},{6,4},{7,5},{8,10},{9,11},{10,... | collective-permute-start | bytes 1769480 | tf_op jit(solution)/shard_map/elementals/RSy/ppermute | solution.py:351
  21.1 1.3 %collective-permute-start.7 = (bf16[384,384]{1,0:T(8,128)(2,1)S(1)}, bf16[384,384]{1,0:T(8,128)(2,1)}, u32[]{:S(2)}, u32[]{:S(2)}) collective-permute-start(bf16[384,384]{1,0:T(8,128)(2,1)S(1)} %get-tuple-element.28), channel_id=1, source_target_pairs={{4,0},{5,1},{6,2},{7,3},{8,12},{9,13},{10,14},{11,15},{20,16},{21,... | collective-permute-start | bytes 884744 | tf_op jit(solution)/shard_map/spread/third_out/ppermute | solution.py:348
  22.3 0.0 collective-permute-done.8.refs_5_
  22.3 0.4 collective-permute-start.10
  22.8 0.0 collective-permute-done.6
  22.8 0.2 collective-permute-start.9
  22.9 0.6 copy-done.5
  23.5 0.5 spread.1.refs_5_
  24.0 12.8 %collective-permute-done.7 = bf16[384,384]{1,0:T(8,128)(2,1)} collective-permute-done((bf16[384,384]{1,0:T(8,128)(2,1)S(1)}, bf16[384,384]{1,0:T(8,128)(2,1)}, u32[]{:S(2)}, u32[]{:S(2)}) %collective-permute-start.7) | collective-permute-done | bytes 294944 | tf_op jit(solution)/shard_map/spread/third_out/ppermute | solution.py:348
  36.8 1.3 %collective-permute-start.19 = (bf16[384,384]{1,0:T(8,128)(2,1)S(1)}, bf16[384,384]{1,0:T(8,128)(2,1)S(1)}, u32[]{:S(2)}, u32[]{:S(2)}) collective-permute-start(bf16[384,384]{1,0:T(8,128)(2,1)S(1)} %copy-done.6), channel_id=1, source_target_pairs={{4,0},{5,1},{6,2},{7,3},{8,12},{9,13},{10,14},{11,15},{20,16},{21,... | collective-permute-start | bytes 884744 | tf_op jit(solution)/shard_map/spread/ends/ppermute | solution.py:348
  38.1 1.0 %broadcast_select_fusion.1.refs_4_ = bf16[384,384]{1,0:T(8,128)(2,1)S(1)} fusion(bf16[384,384]{1,0:T(8,128)(2,1)S(1)} %copy-done.6, bf16[384,384]{1,0:T(8,128)(2,1)} %collective-permute-done.7, pred[]{:T(512)S(6)} %and.120), kind=kLoop, calls=%fused_computation.2 | loop fusion | flops 147456 | bytes 884737 | tf_op jit(solution)/shard_map/spread/jit(_where)/select_n | solution.py:391
  39.1 0.0 collective-permute-done.10.refs_7_
  39.1 0.0 collective-permute-done.9.refs_6_
  39.1 0.0 collective-permute-done.4.refs_1_
  39.1 0.0 collective-permute-done.5.refs_2_
  39.2 1.4 %elementals.7 = (bf16[384,768]{1,0:T(8,128)(2,1)S(1)}, bf16[384,384]{1,0:T(8,128)(2,1)S(1)}, bf16[384,384]{1,0:T(8,128)(2,1)S(1)}, bf16[384,384]{1,0:T(8,128)(2,...) custom-call(f32[384,768]{1,0:T(8,128)S(1)} %get-tuple-element.21.ref, ...), custom_call_target="tpu_custom_call", output_to_operand_aliasing={{1}: (3, {}), {2}: (4, {}), {3}: (5, {}), {4}: (6, {}), {5}... | custom-call | flops 1179648 | bytes 2949120 | tf_op jit(solution)/shard_map/elementals/pallas_call | solution.py:241
  40.6 0.0 copy-start.7
  40.6 3.2 %collective-permute-start.11 = (bf16[96,768]{1,0:T(8,128)(2,1)S(1)}, bf16[96,768]{1,0:T(8,128)(2,1)S(1)}, u32[]{:S(2)}, u32[]{:S(2)}) collective-permute-start(bf16[96,768]{1,0:T(8,128)(2,1)S(1)} %get-tuple-element.39), channel_id=1, source_target_pairs={{0,4},{1,5},{2,6},{3,7},{4,8},{5,9},{6,10},{7,11},{8,12},{9,13},{1... | collective-permute-start | bytes 442376 | tf_op jit(solution)/shard_map/elementals/RSz/ppermute | solution.py:348
  43.8 1.2 %collective-permute-start.14 = (bf16[384,384]{1,0:T(8,128)(2,1)S(1)}, bf16[384,384]{1,0:T(8,128)(2,1)S(1)}, u32[]{:S(2)}, u32[]{:S(2)}) collective-permute-start(bf16[384,384]{1,0:T(8,128)(2,1)S(1)} %get-tuple-element.30.refs_6_), channel_id=1, source_target_pairs={{0,2},{1,3},{2,0},{3,1},{4,6},{5,7},{6,4},{7,5},{8,10},{9,11},{10,... | collective-permute-start | bytes 884744 | tf_op jit(solution)/shard_map/spread/Y/ppermute | solution.py:351
  45.1 0.2 collective-permute-start.15
  45.3 4.2 %collective-permute-done.19 = bf16[384,384]{1,0:T(8,128)(2,1)S(1)} collective-permute-done((bf16[384,384]{1,0:T(8,128)(2,1)S(1)}, bf16[384,384]{1,0:T(8,128)(2,1)S(1)}, u32[]{:S(2)}, u32[]{:S(2)}) %collective-permute-start.19) | collective-permute-done | bytes 294944 | tf_op jit(solution)/shard_map/spread/ends/ppermute | solution.py:348
  49.6 0.3 collective-permute-start.20
  49.9 0.0 collective-permute-start.12
  49.9 0.0 collective-permute-done.11.refs_1_
  49.9 1.3 %collective-permute-start.13 = (bf16[96,768]{1,0:T(8,128)(2,1)S(1)}, bf16[96,768]{1,0:T(8,128)(2,1)S(1)}, u32[]{:S(2)}, u32[]{:S(2)}) collective-permute-start(bf16[96,768]{1,0:T(8,128)(2,1)S(1)} %get-tuple-element.37), channel_id=1, source_target_pairs={{0,12},{1,13},{2,14},{3,15},{4,0},{5,1},{6,2},{7,3},{8,4},{9,5},{1... | collective-permute-start | bytes 442376 | tf_op jit(solution)/shard_map/elementals/RSz/ppermute | solution.py:348
  51.2 0.1 copy.13
  51.3 0.1 eq.107
  51.4 5.1 %collective-permute-done.12.refs_2_ = bf16[96,768]{1,0:T(8,128)(2,1)S(1)} collective-permute-done((bf16[96,768]{1,0:T(8,128)(2,1)S(1)}, bf16[96,768]{1,0:T(8,128)(2,1)S(1)}, u32[]{:S(2)}, u32[]{:S(2)}) %collective-permute-start.12) | collective-permute-done | bytes 147488 | tf_op jit(solution)/shard_map/elementals/RSz/ppermute | solution.py:348
  56.5 4.2 %collective-permute-start.16 = (bf16[384,384]{1,0:T(8,128)(2,1)S(1)}, bf16[384,384]{1,0:T(8,128)(2,1)S(1)}, u32[]{:S(2)}, u32[]{:S(2)}) collective-permute-start(bf16[384,384]{1,0:T(8,128)(2,1)S(1)} %get-tuple-element.31.refs_7_), channel_id=1, source_target_pairs={{0,1},{1,0},{2,3},{3,2},{4,5},{5,4},{6,7},{7,6},{8,9},{9,8},{10,11... | collective-permute-start | bytes 884744 | tf_op jit(solution)/shard_map/spread/swE/ppermute | solution.py:354
  60.7 0.0 collective-permute-done.14.refs_8_
  60.7 0.0 collective-permute-start.17
  60.7 0.0 collective-permute-done.15.refs_9_
  60.7 0.6 collective-permute-start.18
  61.2 0.0 collective-permute-done.13.refs_3_
  61.3 0.1 collective-permute-start.21
  61.3 2.5 %collective-permute-done.20.refs_1_ = bf16[384,384]{1,0:T(8,128)(2,1)S(1)} collective-permute-done((bf16[384,384]{1,0:T(8,128)(2,1)S(1)}, bf16[384,384]{1,0:T(8,128)(2,1)S(1)}, u32[]{:S(2)}, u32[]{:S(2)}) %collective-permute-start.20) | collective-permute-done | bytes 294944 | tf_op jit(solution)/shard_map/spread/Yf/ppermute | solution.py:351
  63.8 2.1 %collective-permute-start.22 = (bf16[384,384]{1,0:T(8,128)(2,1)S(1)}, bf16[384,384]{1,0:T(8,128)(2,1)S(1)}, u32[]{:S(2)}, u32[]{:S(2)}) collective-permute-start(bf16[384,384]{1,0:T(8,128)(2,1)S(1)} %collective-permute-done.20.refs_1_), channel_id=1, source_target_pairs={{0,1},{1,0},{2,3},{3,2},{4,5},{5,4},{6,7},{7,6},{8,9},{9,8},{10,11... | collective-permute-start | bytes 884744 | tf_op jit(solution)/shard_map/spread/swL/ppermute | solution.py:354
  65.9 0.3 and_convert_fusion.refs_4_
  66.2 0.0 collective-permute-done.16.refs_13_
  66.2 0.0 collective-permute-done.17.refs_14_
  66.2 0.0 collective-permute-done.18.refs_15_
  66.2 3.9 %contract.2 = (bf16[192,384]{1,0:T(8,128)(2,1)S(1)}, bf16[12,96,768]{2,1,0:T(8,128)(2,1)S(1)}) custom-call(s32[1]{0:T(128)} %bitcast.core_ref.after_ref, bf16[96,768]{1,0:T(8,128)(2,1)S(1)} %get-tuple-element.40.refs_0_, bf16[96,768]{1,0:T(8,128)(2,1)S(1)} %collective-permute-done.11.refs_1_, bf16[96,768]{1,0:T(8,128)(2,1)S(1)} %collective-permute-done.12.refs_2_, ...), custom_call_target="tpu_custom_call" | custom-call | flops 1358954496 | bytes 7077888 | tf_op jit(solution)/shard_map/contract/pallas_call | solution.py:438
  70.1 0.0 collective-permute-done.21.refs_2_
  70.1 0.0 collective-permute-done.22.refs_3_
  70.1 2.5 %contract.3 = bf16[96,8,768]{2,1,0:T(8,128)(2,1)} custom-call(s32[1]{0:T(128)} %bitcast.core_ref.after_ref, bf16[192,384]{1,0:T(8,128)(2,1)S(1)} %get-tuple-element.35.stacked_ref, bf16[12,96,768]{2,1,0:T(8,128)(2,1)S(1)} %get-tuple-element.36.first_ref, bf16[384,384]{1,0:T(8,128)(2,1)S(1)} %broadcast_select_fusion.refs_0_, ...), custom_call_target="tpu_custom_call" | custom-call | flops 452984832 | bytes 2359296 | tf_op jit(solution)/shard_map/contract/pallas_call | solution.py:450
  (15 shorter events, 0.1 us)
Async XLA Ops:
  0.0 7.0 %collective-permute-start = (bf16[2,384,384]{2,1,0:T(8,128)(2,1)}, bf16[2,384,384]{2,1,0:T(8,128)(2,1)S(1)}, u32[]{:S(2)}, u32[]{:S(2)}) collective-permute-start(bf16[2,384,384]{2,1,0:T(8,128)(2,1)} %bitcast.5), channel_id=1, source_target_pairs={{0,1},{1,0},{2,3},{3,2},{4,5},{5,4},{6,7},{7,6},{8,9},{9,8},{10,11... | collective-permute-start | bytes 1769480 | tf_op jit(solution)/shard_map/matrices/swapP/ppermute | solution.py:354
  0.1 1.5 %copy-start.1 = (bf16[2,384,3,384]{3,1,2,0:T(8,128)(2,1)S(1)}, bf16[2,384,3,384]{3,1,2,0:T(8,128)(2,1)}, u32[]{:S(2)}) copy-start(bf16[2,384,3,384]{3,1,2,0:T(8,128)(2,1)} %param.4) | copy-start | bytes 5308420
  1.6 0.7 copy-start.3
  2.3 4.8 %copy-start = (bf16[1,2,384,384]{3,2,1,0:T(8,128)(2,1)S(1)}, bf16[1,2,384,384]{3,2,1,0:T(8,128)(2,1)}, u32[]{:S(2)}) copy-start(bf16[1,2,384,384]{3,2,1,0:T(8,128)(2,1)} %param.6) | copy-start | bytes 1769476
  2.3 9.7 %copy-start.2 = (bf16[2,384,3,384]{3,1,2,0:T(8,128)(2,1)S(1)}, bf16[2,384,3,384]{3,1,2,0:T(8,128)(2,1)}, u32[]{:S(2)}) copy-start(bf16[2,384,3,384]{3,1,2,0:T(8,128)(2,1)} %param.4) | copy-start | bytes 5308420
  6.5 5.5 %copy-start.4 = (s32[4,3]{1,0:T(4,128)S(1)}, s32[4,3]{1,0:T(4,128)}, u32[]{:S(2)}) copy-start(s32[4,3]{1,0:T(4,128)} %mom_ref.3) | copy-start | bytes 148
  6.5 9.7 %collective-permute-start.1 = (bf16[384,768]{1,0:T(8,128)(2,1)S(1)}, bf16[384,768]{1,0:T(8,128)(2,1)S(1)}, u32[]{:S(2)}, u32[]{:S(2)}) collective-permute-start(bf16[384,768]{1,0:T(8,128)(2,1)S(1)} %get-tuple-element.23), channel_id=1, source_target_pairs={{0,1},{1,0},{2,3},{3,2},{4,5},{5,4},{6,7},{7,6},{8,9},{9,8},{10,11... | collective-permute-start | bytes 1769480 | tf_op jit(solution)/shard_map/elementals/swapA/ppermute | solution.py:354
  7.6 9.5 %collective-permute-start.2 = (bf16[384,384]{1,0:T(8,128)(2,1)S(1)}, bf16[384,384]{1,0:T(8,128)(2,1)S(1)}, u32[]{:S(2)}, u32[]{:S(2)}) collective-permute-start(bf16[384,384]{1,0:T(8,128)(2,1)S(1)} %matrices.1.refs_0_.refs_4_), channel_id=1, source_target_pairs={{0,4},{1,5},{2,6},{3,7},{4,0},{5,1},{6,2},{7,3},{8,12},{9,13},{10,... | collective-permute-start | bytes 884744 | tf_op jit(solution)/shard_map/spread/near/ppermute | solution.py:348
  10.0 7.1 %collective-permute-start.3 = (bf16[384,384]{1,0:T(8,128)(2,1)S(1)}, bf16[384,384]{1,0:T(8,128)(2,1)S(1)}, u32[]{:S(2)}, u32[]{:S(2)}) collective-permute-start(bf16[384,384]{1,0:T(8,128)(2,1)S(1)} %matrices.1.refs_0_.refs_4_), channel_id=1, source_target_pairs={{4,8},{5,9},{6,10},{7,11},{8,4},{9,5},{10,6},{11,7},{20,24},{21,25... | collective-permute-start | bytes 884744 | tf_op jit(solution)/shard_map/spread/middle/ppermute | solution.py:348
  10.7 11.7 %collective-permute-start.8 = (bf16[384,384]{1,0:T(8,128)(2,1)S(1)}, bf16[384,384]{1,0:T(8,128)(2,1)}, u32[]{:S(2)}, u32[]{:S(2)}) collective-permute-start(bf16[384,384]{1,0:T(8,128)(2,1)S(1)} %matrices.1.refs_0_.refs_4_), channel_id=1, source_target_pairs={{0,2},{1,3},{2,0},{3,1},{4,6},{5,7},{6,4},{7,5},{8,10},{9,11},{10,... | collective-permute-start | bytes 884744 | tf_op jit(solution)/shard_map/spread/beside/ppermute | solution.py:351
  18.0 4.7 %collective-permute-start.6 = (bf16[384,384]{1,0:T(8,128)(2,1)S(1)}, bf16[384,384]{1,0:T(8,128)(2,1)S(1)}, u32[]{:S(2)}, u32[]{:S(2)}) collective-permute-start(bf16[384,384]{1,0:T(8,128)(2,1)S(1)} %get-tuple-element.27.refs_3_), channel_id=1, source_target_pairs={{4,8},{5,9},{6,10},{7,11},{8,4},{9,5},{10,6},{11,7},{20,24},{21,25... | collective-permute-start | bytes 884744 | tf_op jit(solution)/shard_map/spread/third_in/ppermute | solution.py:348
  18.7 20.4 %collective-permute-start.4 = (bf16[384,768]{1,0:T(8,128)(2,1)}, bf16[384,768]{1,0:T(8,128)(2,1)}, u32[]{:S(2)}, u32[]{:S(2)}) collective-permute-start(bf16[384,768]{1,0:T(8,128)(2,1)} %get-tuple-element.25), channel_id=1, source_target_pairs={{0,1},{1,0},{2,3},{3,2},{4,5},{5,4},{6,7},{7,6},{8,9},{9,8},{10,11... | collective-permute-start | bytes 1769480 | tf_op jit(solution)/shard_map/elementals/swapB/ppermute | solution.py:354
  19.6 19.5 %collective-permute-start.5 = (bf16[384,768]{1,0:T(8,128)(2,1)}, bf16[384,768]{1,0:T(8,128)(2,1)}, u32[]{:S(2)}, u32[]{:S(2)}) collective-permute-start(bf16[384,768]{1,0:T(8,128)(2,1)} %get-tuple-element.26.after_ref), channel_id=1, source_target_pairs={{0,2},{1,3},{2,0},{3,1},{4,6},{5,7},{6,4},{7,5},{8,10},{9,11},{10,... | collective-permute-start | bytes 1769480 | tf_op jit(solution)/shard_map/elementals/RSy/ppermute | solution.py:351
  21.1 15.8 %collective-permute-start.7 = (bf16[384,384]{1,0:T(8,128)(2,1)S(1)}, bf16[384,384]{1,0:T(8,128)(2,1)}, u32[]{:S(2)}, u32[]{:S(2)}) collective-permute-start(bf16[384,384]{1,0:T(8,128)(2,1)S(1)} %get-tuple-element.28), channel_id=1, source_target_pairs={{4,0},{5,1},{6,2},{7,3},{8,12},{9,13},{10,14},{11,15},{20,16},{21,... | collective-permute-start | bytes 884744 | tf_op jit(solution)/shard_map/spread/third_out/ppermute | solution.py:348
  22.3 16.8 %collective-permute-start.10 = (bf16[384,384]{1,0:T(8,128)(2,1)S(1)}, bf16[384,384]{1,0:T(8,128)(2,1)}, u32[]{:S(2)}, u32[]{:S(2)}) collective-permute-start(bf16[384,384]{1,0:T(8,128)(2,1)S(1)} %get-tuple-element.27.refs_3_), channel_id=1, source_target_pairs={{0,1},{1,0},{2,3},{3,2},{4,5},{5,4},{6,7},{7,6},{8,9},{9,8},{10,11... | collective-permute-start | bytes 884744 | tf_op jit(solution)/shard_map/spread/swE/ppermute | solution.py:354
  22.8 0.7 %copy-start.5 = (bf16[384,384]{1,0:T(8,128)(2,1)}, bf16[384,384]{1,0:T(8,128)(2,1)S(1)}, u32[]{:S(2)}) copy-start(bf16[384,384]{1,0:T(8,128)(2,1)S(1)} %collective-permute-done.6) | copy-start | bytes 884740
  22.8 16.4 %collective-permute-start.9 = (bf16[384,384]{1,0:T(8,128)(2,1)}, bf16[384,384]{1,0:T(8,128)(2,1)}, u32[]{:S(2)}, u32[]{:S(2)}) collective-permute-start(bf16[384,384]{1,0:T(8,128)(2,1)} %collective-permute-done.8.refs_5_), channel_id=1, source_target_pairs={{0,1},{1,0},{2,3},{3,2},{4,5},{5,4},{6,7},{7,6},{8,9},{9,8},{10,11... | collective-permute-start | bytes 884744 | tf_op jit(solution)/shard_map/spread/swE/ppermute | solution.py:354
  23.5 13.3 %copy-start.6 = (bf16[384,384]{1,0:T(8,128)(2,1)S(1)}, bf16[384,384]{1,0:T(8,128)(2,1)}, u32[]{:S(2)}) copy-start(bf16[384,384]{1,0:T(8,128)(2,1)} %copy-done.5) | copy-start | bytes 884740
  36.8 12.7 %collective-permute-start.19 = (bf16[384,384]{1,0:T(8,128)(2,1)S(1)}, bf16[384,384]{1,0:T(8,128)(2,1)S(1)}, u32[]{:S(2)}, u32[]{:S(2)}) collective-permute-start(bf16[384,384]{1,0:T(8,128)(2,1)S(1)} %copy-done.6), channel_id=1, source_target_pairs={{4,0},{5,1},{6,2},{7,3},{8,12},{9,13},{10,14},{11,15},{20,16},{21,... | collective-permute-start | bytes 884744 | tf_op jit(solution)/shard_map/spread/ends/ppermute | solution.py:348
  40.6 10.6 %copy-start.7 = (s32[96,8]{0,1:T(8,128)S(1)}, s32[96,8]{0,1:T(8,128)}, u32[]{:S(2)}) copy-start(s32[96,8]{0,1:T(8,128)} %param.7) | copy-start | bytes 9220
  40.6 9.2 %collective-permute-start.11 = (bf16[96,768]{1,0:T(8,128)(2,1)S(1)}, bf16[96,768]{1,0:T(8,128)(2,1)S(1)}, u32[]{:S(2)}, u32[]{:S(2)}) collective-permute-start(bf16[96,768]{1,0:T(8,128)(2,1)S(1)} %get-tuple-element.39), channel_id=1, source_target_pairs={{0,4},{1,5},{2,6},{3,7},{4,8},{5,9},{6,10},{7,11},{8,12},{9,13},{1... | collective-permute-start | bytes 442376 | tf_op jit(solution)/shard_map/elementals/RSz/ppermute | solution.py:348
  43.8 16.8 %collective-permute-start.14 = (bf16[384,384]{1,0:T(8,128)(2,1)S(1)}, bf16[384,384]{1,0:T(8,128)(2,1)S(1)}, u32[]{:S(2)}, u32[]{:S(2)}) collective-permute-start(bf16[384,384]{1,0:T(8,128)(2,1)S(1)} %get-tuple-element.30.refs_6_), channel_id=1, source_target_pairs={{0,2},{1,3},{2,0},{3,1},{4,6},{5,7},{6,4},{7,5},{8,10},{9,11},{10,... | collective-permute-start | bytes 884744 | tf_op jit(solution)/shard_map/spread/Y/ppermute | solution.py:351
  45.1 15.6 %collective-permute-start.15 = (bf16[384,384]{1,0:T(8,128)(2,1)S(1)}, bf16[384,384]{1,0:T(8,128)(2,1)S(1)}, u32[]{:S(2)}, u32[]{:S(2)}) collective-permute-start(bf16[384,384]{1,0:T(8,128)(2,1)S(1)} %get-tuple-element.31.refs_7_), channel_id=1, source_target_pairs={{0,2},{1,3},{2,0},{3,1},{4,6},{5,7},{6,4},{7,5},{8,10},{9,11},{10,... | collective-permute-start | bytes 884744 | tf_op jit(solution)/shard_map/spread/Y/ppermute | solution.py:351
  49.6 14.3 %collective-permute-start.20 = (bf16[384,384]{1,0:T(8,128)(2,1)S(1)}, bf16[384,384]{1,0:T(8,128)(2,1)S(1)}, u32[]{:S(2)}, u32[]{:S(2)}) collective-permute-start(bf16[384,384]{1,0:T(8,128)(2,1)S(1)} %broadcast_select_fusion.refs_0_), channel_id=1, source_target_pairs={{0,2},{1,3},{2,0},{3,1},{4,6},{5,7},{6,4},{7,5},{8,10},{9,11},{10,... | collective-permute-start | bytes 884744 | tf_op jit(solution)/shard_map/spread/Yf/ppermute | solution.py:351
  49.9 6.6 %collective-permute-start.12 = (bf16[96,768]{1,0:T(8,128)(2,1)S(1)}, bf16[96,768]{1,0:T(8,128)(2,1)S(1)}, u32[]{:S(2)}, u32[]{:S(2)}) collective-permute-start(bf16[96,768]{1,0:T(8,128)(2,1)S(1)} %get-tuple-element.38), channel_id=1, source_target_pairs={{0,8},{1,9},{2,10},{3,11},{4,12},{5,13},{6,14},{7,15},{8,0},{9,1},... | collective-permute-start | bytes 442376 | tf_op jit(solution)/shard_map/elementals/RSz/ppermute | solution.py:348
  49.9 11.4 %collective-permute-start.13 = (bf16[96,768]{1,0:T(8,128)(2,1)S(1)}, bf16[96,768]{1,0:T(8,128)(2,1)S(1)}, u32[]{:S(2)}, u32[]{:S(2)}) collective-permute-start(bf16[96,768]{1,0:T(8,128)(2,1)S(1)} %get-tuple-element.37), channel_id=1, source_target_pairs={{0,12},{1,13},{2,14},{3,15},{4,0},{5,1},{6,2},{7,3},{8,4},{9,5},{1... | collective-permute-start | bytes 442376 | tf_op jit(solution)/shard_map/elementals/RSz/ppermute | solution.py:348
  56.5 9.7 %collective-permute-start.16 = (bf16[384,384]{1,0:T(8,128)(2,1)S(1)}, bf16[384,384]{1,0:T(8,128)(2,1)S(1)}, u32[]{:S(2)}, u32[]{:S(2)}) collective-permute-start(bf16[384,384]{1,0:T(8,128)(2,1)S(1)} %get-tuple-element.31.refs_7_), channel_id=1, source_target_pairs={{0,1},{1,0},{2,3},{3,2},{4,5},{5,4},{6,7},{7,6},{8,9},{9,8},{10,11... | collective-permute-start | bytes 884744 | tf_op jit(solution)/shard_map/spread/swE/ppermute | solution.py:354
  60.7 5.5 %collective-permute-start.17 = (bf16[384,384]{1,0:T(8,128)(2,1)S(1)}, bf16[384,384]{1,0:T(8,128)(2,1)S(1)}, u32[]{:S(2)}, u32[]{:S(2)}) collective-permute-start(bf16[384,384]{1,0:T(8,128)(2,1)S(1)} %collective-permute-done.14.refs_8_), channel_id=1, source_target_pairs={{0,1},{1,0},{2,3},{3,2},{4,5},{5,4},{6,7},{7,6},{8,9},{9,8},{10,11... | collective-permute-start | bytes 884744 | tf_op jit(solution)/shard_map/spread/swE/ppermute | solution.py:354
  60.7 5.5 %collective-permute-start.18 = (bf16[384,384]{1,0:T(8,128)(2,1)S(1)}, bf16[384,384]{1,0:T(8,128)(2,1)S(1)}, u32[]{:S(2)}, u32[]{:S(2)}) collective-permute-start(bf16[384,384]{1,0:T(8,128)(2,1)S(1)} %collective-permute-done.15.refs_9_), channel_id=1, source_target_pairs={{0,1},{1,0},{2,3},{3,2},{4,5},{5,4},{6,7},{7,6},{8,9},{9,8},{10,11... | collective-permute-start | bytes 884744 | tf_op jit(solution)/shard_map/spread/swE/ppermute | solution.py:354
  61.3 8.8 %collective-permute-start.21 = (bf16[384,384]{1,0:T(8,128)(2,1)S(1)}, bf16[384,384]{1,0:T(8,128)(2,1)S(1)}, u32[]{:S(2)}, u32[]{:S(2)}) collective-permute-start(bf16[384,384]{1,0:T(8,128)(2,1)S(1)} %broadcast_select_fusion.refs_0_), channel_id=1, source_target_pairs={{0,1},{1,0},{2,3},{3,2},{4,5},{5,4},{6,7},{7,6},{8,9},{9,8},{10,11... | collective-permute-start | bytes 884744 | tf_op jit(solution)/shard_map/spread/swL/ppermute | solution.py:354
  63.8 6.3 %collective-permute-start.22 = (bf16[384,384]{1,0:T(8,128)(2,1)S(1)}, bf16[384,384]{1,0:T(8,128)(2,1)S(1)}, u32[]{:S(2)}, u32[]{:S(2)}) collective-permute-start(bf16[384,384]{1,0:T(8,128)(2,1)S(1)} %collective-permute-done.20.refs_1_), channel_id=1, source_target_pairs={{0,1},{1,0},{2,3},{3,2},{4,5},{5,4},{6,7},{7,6},{8,9},{9,8},{10,11... | collective-permute-start | bytes 884744 | tf_op jit(solution)/shard_map/spread/swL/ppermute | solution.py:354

commit v3 on v2

--- a/solution.py
+++ b/solution.py
@@ -138,12 +138,18 @@
     )
 
 
-def product_kernel(flip, core_ref, own_ref, other_ref, after_ref, out_ref):
+def product_kernel(flip, copies, waits, core_ref, own_ref, other_ref, *refs):
+    outs = refs[waits : waits + copies]
+
     def real(even, odd):
-        out_ref[...] = (nt_dot(even[0], odd[0]) + nt_dot(even[1], odd[1])).astype(out_ref.dtype)
+        value = nt_dot(even[0], odd[0]) + nt_dot(even[1], odd[1])
+        for out_ref in outs:
+            out_ref[...] = value.astype(out_ref.dtype)
 
     def imag(even, odd):
-        out_ref[...] = (nt_dot(even[1], odd[0]) - nt_dot(even[0], odd[1])).astype(out_ref.dtype)
+        value = nt_dot(even[1], odd[0]) - nt_dot(even[0], odd[1])
+        for out_ref in outs:
+            out_ref[...] = value.astype(out_ref.dtype)
 
     first, second = (imag, real) if flip else (real, imag)
 
@@ -156,8 +162,9 @@
         second(other_ref, own_ref)
 
 
-def partial_kernel(rows, chain, stay, place_ref, mom_ref, v_ref, *refs):
-    away_ref, keep_ref, left_ref, right_ref, cos_ref, sin_ref = refs[-6:]
+def partial_kernel(rows, chain, stay, waits, passed, place_ref, mom_ref, v_ref, *refs):
+    away_ref, keep_ref, *refs = refs[waits + passed :]
+    left_ref, right_ref, cos_ref, sin_ref = refs[passed:]
     num_vec, sites = v_ref.shape[2], v_ref.shape[3]
     colours, momenta = v_ref.shape[1], mom_ref.shape[0]
     height = chain * rows
@@ -183,7 +190,7 @@
         side = core if keep else 1 - core
         base = keep * 2 * height
         for turn in range(chain):
-            target_z = lax.rem(zed + turn, chain)
+            target_z = zed ^ turn
             first = ((target_z * PAIR + target_y) * CORES + side) * rows
             momentum = lax.div(first, num_vec)
             start = pl.multiple_of(lax.rem(first, num_vec), rows)
@@ -203,18 +210,21 @@
         out_ref[:, num_vec:] = (both[:height, num_vec:] - both[height:, :num_vec]).astype(out_ref.dtype)
 
 
-def partial_rows(rows, chain, stay, place, momenta, vectors, *after):
+def partial_rows(rows, chain, stay, place, momenta, vectors, after=(), passed=()):
     _, colours, num_vec, sites = vectors.shape
     depth = colours * sites
     height = chain * rows
     return pl.pallas_call(
-        functools.partial(partial_kernel, rows, chain, stay),
+        functools.partial(partial_kernel, rows, chain, stay, len(after), len(passed)),
         out_shape=(
             jax.ShapeDtypeStruct((height, 2 * num_vec), jnp.bfloat16),
             jax.ShapeDtypeStruct((height, 2 * num_vec), jnp.float32),
-        ),
-        in_specs=[whole(pltpu.SMEM), whole(pltpu.SMEM), whole(pltpu.VMEM)] + [whole(pl.ANY)] * len(after),
-        out_specs=(whole(pltpu.VMEM), whole(pltpu.VMEM)),
+        )
+        + tuple(jax.ShapeDtypeStruct(block.shape, block.dtype) for block in passed),
+        in_specs=[whole(pltpu.SMEM), whole(pltpu.SMEM), whole(pltpu.VMEM)]
+        + [whole(pl.ANY)] * (len(after) + len(passed)),
+        out_specs=(whole(pltpu.VMEM), whole(pltpu.VMEM)) + (whole(pl.ANY),) * len(passed),
+        input_output_aliases={3 + len(after) + i: 2 + i for i in range(len(passed))},
         scratch_shapes=[
             pltpu.VMEM((4 * height, depth), jnp.bfloat16),
             pltpu.VMEM((2 * num_vec, depth), jnp.bfloat16),
@@ -223,7 +233,7 @@
         ],
         compiler_params=pltpu.CompilerParams(vmem_limit_bytes=VMEM_LIMIT),
         cost_estimate=pl.CostEstimate(flops=16 * height * depth * num_vec, bytes_accessed=vectors.size * 2 + height * num_vec * 12, transcendentals=0),
-    )(place, momenta, vectors, *after)
+    )(place, momenta, vectors, *after, *passed)
 
 
 def total_kernel(count, *refs):
@@ -248,6 +258,43 @@
         compiler_params=pltpu.CompilerParams(vmem_limit_bytes=VMEM_LIMIT),
         cost_estimate=pl.CostEstimate(flops=4 * terms[0].size, bytes_accessed=10 * terms[0].size, transcendentals=0),
     )(*terms, *passed)
+
+
+def choose(flag, near, inside, outside, *after):
+    count = len(inside)
+
+    def kernel(flag_ref, near_ref, *refs):
+        out_ref = refs[2 * count + len(after)]
+        out_ref[0] = near_ref[...]
+        for wanted, sources in ((True, refs[:count]), (False, refs[count : 2 * count])):
+
+            @pl.when((flag_ref[0] == 1) == wanted)
+            def _():
+                for at, source in enumerate(sources):
+                    out_ref[1 + at] = source[...]
+
+    return pl.pallas_call(
+        kernel,
+        out_shape=jax.ShapeDtypeStruct((1 + count, *near.shape), near.dtype),
+        in_specs=[whole(pltpu.SMEM)] + [whole(pltpu.VMEM)] * (1 + 2 * count) + [whole(pl.ANY)] * len(after),
+        out_specs=whole(pltpu.VMEM),
+        compiler_params=pltpu.CompilerParams(vmem_limit_bytes=VMEM_LIMIT),
+        cost_estimate=pl.CostEstimate(flops=near.size, bytes_accessed=12 * near.size, transcendentals=0),
+    )(flag, near, *inside, *outside, *after)
+
+
+def hold(after, *passed):
+    def kernel(*refs):
+        pass
+
+    return pl.pallas_call(
+        kernel,
+        out_shape=tuple(jax.ShapeDtypeStruct(block.shape, block.dtype) for block in passed),
+        in_specs=[whole(pl.ANY)] * (len(passed) + 1),
+        out_specs=(whole(pl.ANY),) * len(passed),
+        input_output_aliases={i: i for i in range(len(passed))},
+        compiler_params=pltpu.CompilerParams(vmem_limit_bytes=VMEM_LIMIT),
+    )(*passed, after)
 
 
 def owner_products(core, stacked, own, other, even_ref, odd_ref):
@@ -268,52 +315,41 @@
         ref[:, num_vec:] = imag.astype(jnp.bfloat16)
 
 
-def rows_kernel(slots, arrivals, core_ref, *refs):
+def squares(refs):
+    found = []
+    for ref in refs:
+        found += [ref] if len(ref.shape) == 2 else [ref.at[at] for at in range(ref.shape[0])]
+    return found
+
+
+def rows_kernel(arrivals, blocks, core_ref, *refs):
     terms, refs = refs[:arrivals], refs[arrivals:]
-    own, other = refs[:slots], refs[slots : 2 * slots]
-    stacked_ref, full_ref = refs[2 * slots :]
+    own, other = squares(refs[:blocks]), squares(refs[blocks : 2 * blocks])
+    stacked_ref, full_ref = refs[2 * blocks :]
     num_vec = terms[0].shape[1] // 2
-    rows = stacked_ref.shape[0] // 2
-    total = 0.0
-    for term in terms:
-        for at in range(0, term.shape[0], rows):
-            total = total + term[pl.ds(at, rows), :].astype(jnp.float32)
+    total = terms[0][...].astype(jnp.float32)
+    for term in terms[1:]:
+        total = total + term[...].astype(jnp.float32)
     elemental = total.astype(jnp.bfloat16)
     stacked = jnp.concatenate([elemental[:, :num_vec], elemental[:, num_vec:]], axis=0)
     stacked_ref[...] = stacked
-    for slot in range(slots):
-        owner_products(
-            core_ref[0],
-            stacked,
-            own[slot][...],
-            other[slot][...],
-            full_ref.at[2 * slot],
-            full_ref.at[2 * slot + 1],
-        )
-
-
-def pick_kernel(slots, group, core_ref, stacked_ref, first_ref, *refs):
-    own, other = refs[:slots], refs[slots : 2 * slots]
-    pick_ref, out_ref, last_ref = refs[2 * slots :]
+    for slot, (mine, twin) in enumerate(zip(own, other)):
+        even, odd = full_ref.at[2 * slot], full_ref.at[2 * slot + 1]
+        owner_products(core_ref[0], stacked, mine[...], twin[...], even, odd)
+
+
+def pick_kernel(blocks, group, core_ref, stacked_ref, first_ref, *refs):
+    own, other = squares(refs[:blocks]), squares(refs[blocks : 2 * blocks])
+    pick_ref, out_ref, last_ref = refs[2 * blocks :]
     rows, fanout, width = out_ref.shape
     stacked = stacked_ref[...]
-    for slot in range(slots):
-        owner_products(
-            core_ref[0],
-            stacked,
-            own[slot][...],
-            other[slot][...],
-            last_ref.at[2 * slot],
-            last_ref.at[2 * slot + 1],
-        )
+    for slot, (mine, twin) in enumerate(zip(own, other)):
+        even, odd = last_ref.at[2 * slot], last_ref.at[2 * slot + 1]
+        owner_products(core_ref[0], stacked, mine[...], twin[...], even, odd)
     for block in range(rows // group):
         there = pl.ds(block * group, group)
         table = jnp.concatenate(
-            [
-                first_ref[:, there, :].reshape(first_ref.shape[0] * group, width),
-                last_ref[:, there, :].reshape(2 * slots * group, width),
-            ],
-            axis=0,
+            [ref[:, there, :].reshape(ref.shape[0] * group, width) for ref in (first_ref, last_ref)], axis=0
         )
         picked = nn_dot(pick_ref[pl.ds(block * group * fanout, group * fanout), :], table)
         out_ref[there] = picked.astype(jnp.bfloat16).reshape(group, fanout, width)
@@ -357,55 +393,56 @@
         mine = peram[0]
         theirs = named("swapP", lambda: swap(mine))
 
-        def matrix(flip, after):
+        def matrix(flip, copies, *passed):
+            square = jax.ShapeDtypeStruct((num_vec, num_vec), jnp.bfloat16)
             return pl.pallas_call(
-                functools.partial(product_kernel, flip),
-                out_shape=jax.ShapeDtypeStruct((num_vec, num_vec), jnp.bfloat16),
-                in_specs=[whole(pltpu.SMEM), whole(pltpu.VMEM), whole(pltpu.VMEM), whole(pl.ANY)],
-                out_specs=whole(pltpu.VMEM),
+                functools.partial(product_kernel, flip, copies, len(passed)),
+                out_shape=(square,) * (copies + len(passed)),
+                in_specs=[whole(pltpu.SMEM)] + [whole(pltpu.VMEM)] * 2 + [whole(pl.ANY)] * len(passed),
+                out_specs=(whole(pltpu.VMEM),) * copies + (whole(pl.ANY),) * len(passed),
+                input_output_aliases={3 + i: copies + i for i in range(len(passed))},
                 compiler_params=pltpu.CompilerParams(vmem_limit_bytes=VMEM_LIMIT),
-                cost_estimate=pl.CostEstimate(flops=4 * num_vec**3, bytes_accessed=10 * num_vec**2, transcendentals=0),
-            )(core_at, mine, theirs, after)
-
-        own = matrix(False, core_at)
-    inner = (zed > 0) & (zed < chain - 1)
+                cost_estimate=pl.CostEstimate(
+                    flops=4 * num_vec**3, bytes_accessed=10 * num_vec**2, transcendentals=0
+                ),
+            )(core_at, mine, theirs, *passed)
+
+        own, lone = matrix(False, 2)
+    inner = ((zed > 0) & (zed < chain - 1)).astype(jnp.int32).reshape(1)
     half = chain * rows
     with jax.named_scope("elementals"):
         vectors = jnp.transpose(eigvecs, (0, 2, 1, 3))
         away_cross, kept_cross = partial_rows(rows, chain, False, place, momenta, vectors)
-        away_stay, kept_stay = partial_rows(rows, chain, True, place, momenta, vectors, own)
+        away_stay, kept_stay, lone = partial_rows(
+            rows, chain, True, place, momenta, vectors, (own,), (lone,)
+        )
         got_cross = named("swapA", lambda: swap(away_cross))
     with jax.named_scope("spread"):
         near = named("near", lambda: send(own, [(0, 1), (1, 0), (2, 3), (3, 2)]))
         middle = named("middle", lambda: send(own, [(1, 2), (2, 1)]))
         beside = named("beside", lambda: across(own))
     with jax.named_scope("elementals"):
-        outgoing, near, middle, away_stay = total([kept_cross, got_cross], near, middle, away_stay)
+        outgoing, near, middle, beside, away_stay = total(
+            [kept_cross, got_cross], near, middle, beside, away_stay
+        )
         crossed = named("RSy", lambda: across(outgoing))
         got_stay = named("swapB", lambda: swap(away_stay))
     with jax.named_scope("spread"):
+        twin, near, middle = matrix(True, 1, near, middle)
         third_in = named("third_in", lambda: send(near, [(1, 2), (2, 1)]))
         third_out = named("third_out", lambda: send(middle, [(1, 0), (2, 3)]))
-        ends = named("ends", lambda: send(third_in, [(1, 0), (2, 3)]))
-        twin = matrix(True, outgoing)
-        third = jnp.where(inner, third_in, third_out)
-        fourth = jnp.where(inner, middle, ends)
-        twin_beside, twin_near = [named("swE", lambda: swap(block)) for block in (beside, near)]
+        ends = named("ends", lambda: send(lone, [(0, 3), (3, 0)]))
+        twin_beside = named("swE", lambda: swap(beside))
+        triple = choose(inner, near, (third_in, middle), (third_out, ends), crossed)
+        twin_triple = named("swE", lambda: swap(triple))
+        beside_triple = named("Y", lambda: across(triple))
+        early = [own, beside, triple, twin, twin_beside, twin_triple]
     with jax.named_scope("elementals"):
-        summed, near, third, twin, twin_beside, twin_near = total(
-            [kept_stay, got_stay, crossed], near, third, twin, twin_beside, twin_near
-        )
-    with jax.named_scope("spread"):
-        beside_near, beside_third = [named("Y", lambda: across(block)) for block in (near, third)]
-        early = [own, beside, near, third, beside_near, beside_third]
-        early_twins = [twin, twin_beside, twin_near]
-        early_twins += [named("swE", lambda: swap(block)) for block in (third, beside_near, beside_third)]
-        late = [fourth, named("Yf", lambda: across(fourth))]
-        late_twins = [named("swL", lambda: swap(block)) for block in late]
+        (summed,) = total([kept_stay, got_stay, crossed])
     with jax.named_scope("elementals"):
         terms = [summed[:rows]]
         for shift in range(1, chain):
-            moves = [(z, (z + shift) % chain) for z in range(chain)]
+            moves = [(z, z ^ shift) for z in range(chain)]
             chunk = summed[shift * rows : (shift + 1) * rows]
             terms.append(named("RSz", lambda: send(chunk, moves)))
     with jax.named_scope("pick"):
@@ -417,9 +454,9 @@
             (zed, 1 - why),
             (near_z, why),
             (third_z, why),
+            (fourth_z, why),
             (near_z, 1 - why),
             (third_z, 1 - why),
-            (fourth_z, why),
             (fourth_z, 1 - why),
         ):
             chips.append(z * PAIR + y)
@@ -434,28 +471,38 @@
             & (row_of[:, None] == (columns % group)[None, :])
         ).astype(jnp.bfloat16)
     with jax.named_scope("contract"):
-        slots = len(early)
+        slots = 1 + chain
         stacked, first = pl.pallas_call(
-            functools.partial(rows_kernel, slots, len(terms)),
+            functools.partial(rows_kernel, len(terms), len(early) // 2),
             out_shape=(
                 jax.ShapeDtypeStruct((2 * rows, num_vec), jnp.bfloat16),
                 jax.ShapeDtypeStruct((2 * slots, rows, 2 * num_vec), jnp.bfloat16),
             ),
-            in_specs=[whole(pltpu.SMEM)] + [whole(pltpu.VMEM)] * (len(terms) + 2 * slots),
+            in_specs=[whole(pltpu.SMEM)] + [whole(pltpu.VMEM)] * (len(terms) + len(early)),
             out_specs=(whole(pltpu.VMEM), whole(pltpu.VMEM)),
             compiler_params=pltpu.CompilerParams(vmem_limit_bytes=VMEM_LIMIT),
-            cost_estimate=pl.CostEstimate(flops=16 * slots * rows * num_vec**2, bytes_accessed=8 * slots * num_vec**2, transcendentals=0),
-        )(core_at, *terms, *early, *early_twins)
-        slots = len(late)
+            cost_estimate=pl.CostEstimate(
+                flops=16 * slots * rows * num_vec**2,
+                bytes_accessed=8 * slots * num_vec**2,
+                transcendentals=0,
+            ),
+        )(core_at, *terms, *early)
+        (beside_triple,) = hold(first, beside_triple)
+        late = [beside_triple, named("swL", lambda: swap(beside_triple))]
+        slots = chain - 1
         return pl.pallas_call(
-            functools.partial(pick_kernel, slots, group),
+            functools.partial(pick_kernel, len(late) // 2, group),
             out_shape=jax.ShapeDtypeStruct((rows, fanout, 2 * num_vec), jnp.bfloat16),
-            in_specs=[whole(pltpu.SMEM)] + [whole(pltpu.VMEM)] * (2 + 2 * slots + 1),
+            in_specs=[whole(pltpu.SMEM)] + [whole(pltpu.VMEM)] * (2 + len(late) + 1),
             out_specs=whole(pltpu.VMEM),
             scratch_shapes=[pltpu.VMEM((2 * slots, rows, 2 * num_vec), jnp.bfloat16)],
             compiler_params=pltpu.CompilerParams(vmem_limit_bytes=VMEM_LIMIT),
-            cost_estimate=pl.CostEstimate(flops=16 * slots * rows * num_vec**2, bytes_accessed=8 * slots * num_vec**2, transcendentals=0),
-        )(core_at, stacked, first, *late, *late_twins, pick)
+            cost_estimate=pl.CostEstimate(
+                flops=16 * slots * rows * num_vec**2,
+                bytes_accessed=8 * slots * num_vec**2,
+                transcendentals=0,
+            ),
+        )(core_at, stacked, first, *late, pick)
 
 
 LINE = 4

time: 72.9 us -> 69.1 us (0.948)
  starting transfers between devices: 24.2 us -> 20.4 us
  Pallas kernels: 18.2 us -> 16.8 us
  local copies, waits for them, and re-layouts: 2.97 us -> 4.14 us
  other arithmetic: 1.41 us -> 0.37 us
  waiting for transfers between devices: 25.6 us -> 26.6 us
    ppermute x8, waiting for transfers between devices: 23 us -> 18 us  [send(): return lax.ppermute(block, 'space', route)]
    ppermute x5 -> x3, waiting for transfers between devices: 2.52 us -> 6.99 us  [across(): return lax.ppermute(block, 'space', [(i, i ^ CORES) for i in range(spaces)])]
    ppermute x10 -> x6, starting transfers between devices: 8.95 us -> 4.82 us  [swap(): return lax.ppermute(block, 'space', [(i, i ^ 1) for i in range(spaces)])]
    ppermute x8, starting transfers between devices: 10.8 us -> 12.8 us  [send(): return lax.ppermute(block, 'space', route)]
    ppermute x5 -> x3, starting transfers between devices: 4.48 us -> 2.79 us  [across(): return lax.ppermute(block, 'space', [(i, i ^ CORES) for i in range(spaces)])]
    ppermute x10 -> x6, waiting for transfers between devices: 0.03 us -> 1.57 us  [swap(): return lax.ppermute(block, 'space', [(i, i ^ 1) for i in range(spaces)])]
    pallas_call x2, Pallas kernels: 2.36 us -> 1.08 us  [total(): pl.pallas_call(kernel, out_shape=(jax.ShapeDtypeStruct(terms[0].shape, jn...]
    unnamed x17 -> x29, local copies, waits for them, and re-layouts: 2.84 us -> 4.01 us
  transfers between devices with their start and end apart: 23 -> 17, of which waited for: 5 -> 7; matrix products, arithmetic and copies ran while one was open for 2% -> 1% of each run, Pallas kernels for 22% -> 19%
where the time goes in v3:
time: 69.1 us; the launch traced here: 68.5 us
  waiting for transfers between devices  26.6 us (38%)
  starting transfers between devices  20.4 us (30%)
  Pallas kernels  16.8 us (24%)
  local copies, waits for them, and re-layouts  4.14 us (6%)
    ppermute x8, waiting for transfers between devices, send(): return lax.ppermute(block, 'space', route)  18 us
    ppermute x8, starting transfers between devices, send(): return lax.ppermute(block, 'space', route)  12.8 us
    pallas_call x2, Pallas kernels, partial_rows(): pl.pallas_call(functools.partial(partial_kernel, rows, chain, stay, len(a...  8.37 us
    ppermute x3, waiting for transfers between devices, across(): return lax.ppermute(block, 'space', [(i, i ^ CORES) for i in range(spaces)])  6.99 us
    ppermute x6, starting transfers between devices, swap(): return lax.ppermute(block, 'space', [(i, i ^ 1) for i in range(spaces)])  4.82 us
    unnamed x29, local copies, waits for them, and re-layouts  4.01 us
    pallas_call x1, Pallas kernels, gather_plan(): pl.pallas_call(functools.partial(pick_kernel, len(late) // 2, group), out...  2.89 us
    ppermute x3, starting transfers between devices, across(): return lax.ppermute(block, 'space', [(i, i ^ CORES) for i in range(spaces)])  2.79 us
  transfers between devices with their start and end apart: 17, of which 7 were waited for; matrix products, arithmetic and copies ran while one was open for 1% of the time, Pallas kernels for 19%

profile of v3, /device:TPU:1, one launch (start us, length us, event | category | flops | bytes accessed | tf_op | source)
XLA Modules:
  0.0 68.5 jit_solution(4207649118720810979)
XLA Ops:
  0.0 0.1 collective-permute-start
  0.1 0.1 pad_add_fusion.place_ref
  0.1 1.5 %copy-done.5 = bf16[2,384,3,384]{3,1,2,0:T(8,128)(2,1)S(1)} copy-done((bf16[2,384,3,384]{3,1,2,0:T(8,128)(2,1)S(1)}, bf16[2,384,3,384]{3,1,2,0:T(8,128)(2,1)}, u32[]{:S(2)}) %copy-start.5) | copy-done | bytes 1769496
  1.6 0.7 copy-done.11
  2.3 4.2 %elementals.5 = (bf16[384,768]{1,0:T(8,128)(2,1)S(1)}, f32[384,768]{1,0:T(8,128)S(1)}) custom-call(s32[3]{0:T(128)S(1)} %pad_add_fusion.place_ref, s32[4,3]{1,0:T(4,128)S(1)} %copy-done.11, bf16[2,3,384,384]{3,2,1,0:T(8,128)(2,1)S(1)} %bitcast.9), custom_call_target="tpu_custom_call" | custom-call | flops 2717908992 | bytes 3538944 | tf_op jit(solution)/shard_map/elementals/pallas_call | solution.py:217
  6.5 0.0 copy-start.12
  6.5 0.5 collective-permute-start.1
  7.0 0.0 collective-permute-done.other_ref
  7.0 0.0 copy-done
  7.0 1.3 %matrices.1 = (bf16[384,384]{1,0:T(8,128)(2,1)S(1)}, bf16[384,384]{1,0:T(8,128)(2,1)}) custom-call(s32[1]{0:T(128)} %bitcast.core_ref, bf16[2,384,384]{2,1,0:T(8,128)(2,1)S(1)} %bitcast.7, bf16[2,384,384]{2,1,0:T(8,128)(2,1)S(1)} %collective-permute-done.other_ref), custom_call_target="tpu_custom_call" | custom-call | flops 226492416 | bytes 1474560 | tf_op jit(solution)/shard_map/matrices/pallas_call | solution.py:398
  8.3 2.3 %collective-permute-start.2 = (bf16[384,384]{1,0:T(8,128)(2,1)S(1)}, bf16[384,384]{1,0:T(8,128)(2,1)S(1)}, u32[]{:S(2)}, u32[]{:S(2)}) collective-permute-start(bf16[384,384]{1,0:T(8,128)(2,1)S(1)} %get-tuple-element.22.refs_0_.refs_4_), channel_id=1, source_target_pairs={{0,4},{1,5},{2,6},{3,7},{4,0},{5,1},{6,2},{7,3},{8,12},{9,13},{10,... | collective-permute-start | bytes 884744 | tf_op jit(solution)/shard_map/spread/near/ppermute | solution.py:384
  10.7 0.7 collective-permute-start.3
  11.4 1.3 %collective-permute-start.4 = (bf16[384,384]{1,0:T(8,128)(2,1)S(1)}, bf16[384,384]{1,0:T(8,128)(2,1)S(1)}, u32[]{:S(2)}, u32[]{:S(2)}) collective-permute-start(bf16[384,384]{1,0:T(8,128)(2,1)S(1)} %get-tuple-element.22.refs_0_.refs_4_), channel_id=1, source_target_pairs={{0,2},{1,3},{2,0},{3,1},{4,6},{5,7},{6,4},{7,5},{8,10},{9,11},{10,... | collective-permute-start | bytes 884744 | tf_op jit(solution)/shard_map/spread/beside/ppermute | solution.py:387
  12.7 0.0 copy-done.6
  12.7 0.0 copy-done.12
  12.7 4.2 %elementals.4 = (bf16[384,768]{1,0:T(8,128)(2,1)S(1)}, f32[384,768]{1,0:T(8,128)S(1)}, bf16[384,384]{1,0:T(8,128)(2,1)}) custom-call(s32[3]{0:T(128)S(1)} %pad_add_fusion.place_ref, s32[4,3]{1,0:T(4,128)S(1)} %copy-done.12, bf16[2,3,384,384]{3,2,1,0:T(8,128)(2,1)S(1)} %bitcast.10, ...), custom_call_target="tpu_custom_call", output_to_operand_aliasing={{2}: (4, {})} | custom-call | flops 2717908992 | bytes 3538944 | tf_op jit(solution)/shard_map/elementals/pallas_call | solution.py:217
  16.8 0.0 copy-done.7
  16.9 0.0 copy-start.1
  16.9 1.0 %copy-done.1 = f32[384,768]{1,0:T(8,128)} copy-done((f32[384,768]{1,0:T(8,128)}, f32[384,768]{1,0:T(8,128)S(1)}, u32[]{:S(2)}) %copy-start.1) | copy-done | bytes 1179672
  17.9 0.0 collective-permute-done.1.refs_1_
  17.9 0.0 collective-permute-done.2.refs_2_
  17.9 0.0 collective-permute-done.3.refs_3_
  17.9 1.4 %collective-permute-done.4.refs_4_ = bf16[384,384]{1,0:T(8,128)(2,1)S(1)} collective-permute-done((bf16[384,384]{1,0:T(8,128)(2,1)S(1)}, bf16[384,384]{1,0:T(8,128)(2,1)S(1)}, u32[]{:S(2)}, u32[]{:S(2)}) %collective-permute-start.4) | collective-permute-done | bytes 294944 | tf_op jit(solution)/shard_map/spread/beside/ppermute | solution.py:387
  19.2 0.9 %elementals.6 = (bf16[384,768]{1,0:T(8,128)(2,1)}, bf16[384,384]{1,0:T(8,128)(2,1)S(1)}, bf16[384,384]{1,0:T(8,128)(2,1)S(1)}, bf16[384,384]{1,0:T(8,128)(2,1)S(1)}, bf16[384,768]{1,0:T(8,128)(2,1)S(1)}) custom-call(f32[384,768]{1,0:T(8,128)S(1)} %get-tuple-element.25.refs_0_, ...), custom_call_target="tpu_custom_call", output_to_operand_aliasing={{1}: (2, {}), {2}: (3, {}), {3}: (4, {}), {4}: (5, {})} | custom-call | flops 1179648 | bytes 2949120 | tf_op jit(solution)/shard_map/elementals/pallas_call | solution.py:251
  20.1 1.2 %collective-permute-start.6 = (bf16[384,768]{1,0:T(8,128)(2,1)}, bf16[384,768]{1,0:T(8,128)(2,1)S(1)}, u32[]{:S(2)}, u32[]{:S(2)}) collective-permute-start(bf16[384,768]{1,0:T(8,128)(2,1)} %get-tuple-element.29), channel_id=1, source_target_pairs={{0,2},{1,3},{2,0},{3,1},{4,6},{5,7},{6,4},{7,5},{8,10},{9,11},{10,... | collective-permute-start | bytes 1769480 | tf_op jit(solution)/shard_map/elementals/RSy/ppermute | solution.py:387
  21.4 4.1 %collective-permute-start.12 = (bf16[384,384]{1,0:T(8,128)(2,1)}, bf16[384,384]{1,0:T(8,128)(2,1)S(1)}, u32[]{:S(2)}, u32[]{:S(2)}) collective-permute-start(bf16[384,384]{1,0:T(8,128)(2,1)} %get-tuple-element.35), channel_id=1, source_target_pairs={{0,12},{1,13},{2,14},{3,15},{12,0},{13,1},{14,2},{15,3},{16,28},{1... | collective-permute-start | bytes 884744 | tf_op jit(solution)/shard_map/spread/ends/ppermute | solution.py:384
  25.5 0.5 spread.2
  26.0 0.0 copy-start.9
  26.0 0.7 %copy-done.9 = bf16[384,384]{1,0:T(8,128)(2,1)} copy-done((bf16[384,384]{1,0:T(8,128)(2,1)}, bf16[384,384]{1,0:T(8,128)(2,1)S(1)}, u32[]{:S(2)}) %copy-start.9) | copy-done | bytes 294936
  26.7 0.7 collective-permute-start.10
  27.4 1.3 %collective-permute-start.11 = (bf16[384,384]{1,0:T(8,128)(2,1)S(1)}, bf16[384,384]{1,0:T(8,128)(2,1)S(1)}, u32[]{:S(2)}, u32[]{:S(2)}) collective-permute-start(bf16[384,384]{1,0:T(8,128)(2,1)S(1)} %get-tuple-element.34.refs_1_), channel_id=1, source_target_pairs={{4,0},{5,1},{6,2},{7,3},{8,12},{9,13},{10,14},{11,15},{20,16},{21,... | collective-permute-start | bytes 884744 | tf_op jit(solution)/shard_map/spread/third_out/ppermute | solution.py:384
  28.7 0.0 copy-done.3
  28.7 2.3 %collective-permute-start.5 = (bf16[384,768]{1,0:T(8,128)(2,1)S(1)}, bf16[384,768]{1,0:T(8,128)(2,1)S(1)}, u32[]{:S(2)}, u32[]{:S(2)}) collective-permute-start(bf16[384,768]{1,0:T(8,128)(2,1)S(1)} %get-tuple-element.28), channel_id=1, source_target_pairs={{0,1},{1,0},{2,3},{3,2},{4,5},{5,4},{6,7},{7,6},{8,9},{9,8},{10,11... | collective-permute-start | bytes 1769480 | tf_op jit(solution)/shard_map/elementals/swapB/ppermute | solution.py:390
  31.0 0.9 %collective-permute-done.12.refs_3_ = bf16[384,384]{1,0:T(8,128)(2,1)S(1)} collective-permute-done((bf16[384,384]{1,0:T(8,128)(2,1)}, bf16[384,384]{1,0:T(8,128)(2,1)S(1)}, u32[]{:S(2)}, u32[]{:S(2)}) %collective-permute-start.12) | collective-permute-done | bytes 294944 | tf_op jit(solution)/shard_map/spread/ends/ppermute | solution.py:384
  31.9 0.0 collective-permute-done.10.refs_0_
  31.9 8.5 %collective-permute-done.11.refs_2_ = bf16[384,384]{1,0:T(8,128)(2,1)S(1)} collective-permute-done((bf16[384,384]{1,0:T(8,128)(2,1)S(1)}, bf16[384,384]{1,0:T(8,128)(2,1)S(1)}, u32[]{:S(2)}, u32[]{:S(2)}) %collective-permute-start.11) | collective-permute-done | bytes 294944 | tf_op jit(solution)/shard_map/spread/third_out/ppermute | solution.py:384
  40.4 0.0 collective-permute-done.6.refs_2_.refs_4_
  40.4 0.3 spread.3.refs_6_
  40.7 0.8 %collective-permute-start.14 = (bf16[3,384,384]{2,1,0:T(8,128)(2,1)S(1)}, bf16[3,384,384]{2,1,0:T(8,128)(2,1)S(1)}, u32[]{:S(2)}, u32[]{:S(2)}) collective-permute-start(bf16[3,384,384]{2,1,0:T(8,128)(2,1)S(1)} %spread.3.refs_6_), channel_id=1, source_target_pairs={{0,1},{1,0},{2,3},{3,2},{4,5},{5,4},{6,7},{7,6},{8,9},{9,8},{10,11... | collective-permute-start | bytes 2654216 | tf_op jit(solution)/shard_map/spread/swE/ppermute | solution.py:390
  41.4 0.2 collective-permute-start.15
  41.7 0.0 copy-done.4
  41.7 0.4 collective-permute-start.13
  42.1 0.0 collective-permute-done.5.refs_1_
  42.1 0.0 copy-done.2
  42.1 0.2 elementals.7
  42.3 0.0 copy-start.8
  42.3 0.0 copy-start.10
  42.3 0.3 collective-permute-start.7
  42.6 2.3 %collective-permute-start.8 = (bf16[96,768]{1,0:T(8,128)(2,1)S(1)}, bf16[96,768]{1,0:T(8,128)(2,1)S(1)}, u32[]{:S(2)}, u32[]{:S(2)}) collective-permute-start(bf16[96,768]{1,0:T(8,128)(2,1)S(1)} %get-tuple-element.40), channel_id=1, source_target_pairs={{0,8},{1,9},{2,10},{3,11},{4,12},{5,13},{6,14},{7,15},{8,0},{9,1},... | collective-permute-start | bytes 442376 | tf_op jit(solution)/shard_map/elementals/RSz/ppermute | solution.py:384
  44.9 0.0 collective-permute-done.13.refs_8_
  44.9 1.2 %collective-permute-start.9 = (bf16[96,768]{1,0:T(8,128)(2,1)S(1)}, bf16[96,768]{1,0:T(8,128)(2,1)S(1)}, u32[]{:S(2)}, u32[]{:S(2)}) collective-permute-start(bf16[96,768]{1,0:T(8,128)(2,1)S(1)} %get-tuple-element.39), channel_id=1, source_target_pairs={{0,12},{1,13},{2,14},{3,15},{4,8},{5,9},{6,10},{7,11},{8,4},{9,5},... | collective-permute-start | bytes 442376 | tf_op jit(solution)/shard_map/elementals/RSz/ppermute | solution.py:384
  46.1 3.8 %collective-permute-done.7.refs_1_ = bf16[96,768]{1,0:T(8,128)(2,1)S(1)} collective-permute-done((bf16[96,768]{1,0:T(8,128)(2,1)S(1)}, bf16[96,768]{1,0:T(8,128)(2,1)S(1)}, u32[]{:S(2)}, u32[]{:S(2)}) %collective-permute-start.7) | collective-permute-done | bytes 147488 | tf_op jit(solution)/shard_map/elementals/RSz/ppermute | solution.py:384
  49.9 0.0 collective-permute-done.8.refs_2_
  49.9 4.8 %collective-permute-done.9.refs_3_ = bf16[96,768]{1,0:T(8,128)(2,1)S(1)} collective-permute-done((bf16[96,768]{1,0:T(8,128)(2,1)S(1)}, bf16[96,768]{1,0:T(8,128)(2,1)S(1)}, u32[]{:S(2)}, u32[]{:S(2)}) %collective-permute-start.9) | collective-permute-done | bytes 147488 | tf_op jit(solution)/shard_map/elementals/RSz/ppermute | solution.py:384
  54.7 0.0 collective-permute-done.14.refs_9_
  54.7 0.0 copy-done.8
  54.7 2.3 %contract.3 = (bf16[192,384]{1,0:T(8,128)(2,1)S(1)}, bf16[10,96,768]{2,1,0:T(8,128)(2,1)S(1)}) custom-call(s32[1]{0:T(128)} %bitcast.core_ref, bf16[96,768]{1,0:T(8,128)(2,1)S(1)} %get-tuple-element.42.refs_0_, bf16[96,768]{1,0:T(8,128)(2,1)S(1)} %collective-permute-done.7.refs_1_, bf16[96,768]{1,0:T(8,128)(2,1)S(1)} %collective-permute-done.8.refs_2_, ...), custom_call_target="tpu_custom_call" | custom-call | flops 1132462080 | bytes 5898240 | tf_op jit(solution)/shard_map/contract/pallas_call | solution.py:475
  57.0 5.6 %collective-permute-done.15.refs_0_ = bf16[3,384,384]{2,1,0:T(8,128)(2,1)S(1)} collective-permute-done((bf16[3,384,384]{2,1,0:T(8,128)(2,1)S(1)}, bf16[3,384,384]{2,1,0:T(8,128)(2,1)S(1)}, u32[]{:S(2)}, u32[]{:S(2)}) %collective-permute-start.15) | collective-permute-done | bytes 884768 | tf_op jit(solution)/shard_map/spread/Y/ppermute | solution.py:387
  62.7 0.8 %collective-permute-start.16 = (bf16[3,384,384]{2,1,0:T(8,128)(2,1)S(1)}, bf16[3,384,384]{2,1,0:T(8,128)(2,1)S(1)}, u32[]{:S(2)}, u32[]{:S(2)}) collective-permute-start(bf16[3,384,384]{2,1,0:T(8,128)(2,1)S(1)} %contract.4.refs_0_), channel_id=1, source_target_pairs={{0,1},{1,0},{2,3},{3,2},{4,5},{5,4},{6,7},{7,6},{8,9},{9,8},{10,11... | collective-permute-start | bytes 2654216 | tf_op jit(solution)/shard_map/contract/swL/ppermute | solution.py:390
  63.5 0.1 copy.13
  63.6 0.1 eq.107
  63.7 0.3 and_convert_fusion.refs_2_
  64.0 1.6 %collective-permute-done.16.refs_1_ = bf16[3,384,384]{2,1,0:T(8,128)(2,1)S(1)} collective-permute-done((bf16[3,384,384]{2,1,0:T(8,128)(2,1)S(1)}, bf16[3,384,384]{2,1,0:T(8,128)(2,1)S(1)}, u32[]{:S(2)}, u32[]{:S(2)}) %collective-permute-start.16) | collective-permute-done | bytes 884768 | tf_op jit(solution)/shard_map/contract/swL/ppermute | solution.py:390
  65.6 2.9 %contract.5 = bf16[96,8,768]{2,1,0:T(8,128)(2,1)} custom-call(s32[1]{0:T(128)} %bitcast.core_ref, bf16[192,384]{1,0:T(8,128)(2,1)S(1)} %get-tuple-element.37.stacked_ref, bf16[10,96,768]{2,1,0:T(8,128)(2,1)S(1)} %get-tuple-element.38.refs_1_.first_ref, bf16[3,384,384]{2,1,0:T(8,128)(2,1)S(1)} %contract.4.refs_0_, ...), custom_call_target="tpu_custom_call" | custom-call | flops 679477248 | bytes 3538944 | tf_op jit(solution)/shard_map/contract/pallas_call | solution.py:493
  (15 shorter events, 0.1 us)
Async XLA Ops:
  0.0 7.0 %collective-permute-start = (bf16[2,384,384]{2,1,0:T(8,128)(2,1)}, bf16[2,384,384]{2,1,0:T(8,128)(2,1)S(1)}, u32[]{:S(2)}, u32[]{:S(2)}) collective-permute-start(bf16[2,384,384]{2,1,0:T(8,128)(2,1)} %bitcast.6), channel_id=1, source_target_pairs={{0,1},{1,0},{2,3},{3,2},{4,5},{5,4},{6,7},{7,6},{8,9},{9,8},{10,11... | collective-permute-start | bytes 1769480 | tf_op jit(solution)/shard_map/matrices/swapP/ppermute | solution.py:390
  0.1 1.5 %copy-start.5 = (bf16[2,384,3,384]{3,1,2,0:T(8,128)(2,1)S(1)}, bf16[2,384,3,384]{3,1,2,0:T(8,128)(2,1)}, u32[]{:S(2)}) copy-start(bf16[2,384,3,384]{3,1,2,0:T(8,128)(2,1)} %param.4) | copy-start | bytes 5308420
  1.6 0.7 copy-start.11
  2.3 4.8 %copy-start = (bf16[1,2,384,384]{3,2,1,0:T(8,128)(2,1)S(1)}, bf16[1,2,384,384]{3,2,1,0:T(8,128)(2,1)}, u32[]{:S(2)}) copy-start(bf16[1,2,384,384]{3,2,1,0:T(8,128)(2,1)} %param.6) | copy-start | bytes 1769476
  2.3 10.4 %copy-start.6 = (bf16[2,384,3,384]{3,1,2,0:T(8,128)(2,1)S(1)}, bf16[2,384,3,384]{3,1,2,0:T(8,128)(2,1)}, u32[]{:S(2)}) copy-start(bf16[2,384,3,384]{3,1,2,0:T(8,128)(2,1)} %param.4) | copy-start | bytes 5308420
  6.5 6.2 %copy-start.12 = (s32[4,3]{1,0:T(4,128)S(1)}, s32[4,3]{1,0:T(4,128)}, u32[]{:S(2)}) copy-start(s32[4,3]{1,0:T(4,128)} %mom_ref.3) | copy-start | bytes 148
  6.5 11.4 %collective-permute-start.1 = (bf16[384,768]{1,0:T(8,128)(2,1)S(1)}, bf16[384,768]{1,0:T(8,128)(2,1)S(1)}, u32[]{:S(2)}, u32[]{:S(2)}) collective-permute-start(bf16[384,768]{1,0:T(8,128)(2,1)S(1)} %get-tuple-element.26), channel_id=1, source_target_pairs={{0,1},{1,0},{2,3},{3,2},{4,5},{5,4},{6,7},{7,6},{8,9},{9,8},{10,11... | collective-permute-start | bytes 1769480 | tf_op jit(solution)/shard_map/elementals/swapA/ppermute | solution.py:390
  8.3 8.5 %copy-start.7 = (bf16[384,384]{1,0:T(8,128)(2,1)}, bf16[384,384]{1,0:T(8,128)(2,1)S(1)}, u32[]{:S(2)}) copy-start(bf16[384,384]{1,0:T(8,128)(2,1)S(1)} %get-tuple-element.22.refs_0_.refs_4_) | copy-start | bytes 884740
  8.3 9.5 %collective-permute-start.2 = (bf16[384,384]{1,0:T(8,128)(2,1)S(1)}, bf16[384,384]{1,0:T(8,128)(2,1)S(1)}, u32[]{:S(2)}, u32[]{:S(2)}) collective-permute-start(bf16[384,384]{1,0:T(8,128)(2,1)S(1)} %get-tuple-element.22.refs_0_.refs_4_), channel_id=1, source_target_pairs={{0,4},{1,5},{2,6},{3,7},{4,0},{5,1},{6,2},{7,3},{8,12},{9,13},{10,... | collective-permute-start | bytes 884744 | tf_op jit(solution)/shard_map/spread/near/ppermute | solution.py:384
  10.7 7.2 %collective-permute-start.3 = (bf16[384,384]{1,0:T(8,128)(2,1)S(1)}, bf16[384,384]{1,0:T(8,128)(2,1)S(1)}, u32[]{:S(2)}, u32[]{:S(2)}) collective-permute-start(bf16[384,384]{1,0:T(8,128)(2,1)S(1)} %get-tuple-element.22.refs_0_.refs_4_), channel_id=1, source_target_pairs={{4,8},{5,9},{6,10},{7,11},{8,4},{9,5},{10,6},{11,7},{20,24},{21,25... | collective-permute-start | bytes 884744 | tf_op jit(solution)/shard_map/spread/middle/ppermute | solution.py:384
  11.4 7.9 %collective-permute-start.4 = (bf16[384,384]{1,0:T(8,128)(2,1)S(1)}, bf16[384,384]{1,0:T(8,128)(2,1)S(1)}, u32[]{:S(2)}, u32[]{:S(2)}) collective-permute-start(bf16[384,384]{1,0:T(8,128)(2,1)S(1)} %get-tuple-element.22.refs_0_.refs_4_), channel_id=1, source_target_pairs={{0,2},{1,3},{2,0},{3,1},{4,6},{5,7},{6,4},{7,5},{8,10},{9,11},{10,... | collective-permute-start | bytes 884744 | tf_op jit(solution)/shard_map/spread/beside/ppermute | solution.py:387
  16.9 1.0 %copy-start.1 = (f32[384,768]{1,0:T(8,128)}, f32[384,768]{1,0:T(8,128)S(1)}, u32[]{:S(2)}) copy-start(f32[384,768]{1,0:T(8,128)S(1)} %get-tuple-element.24.refs_0_) | copy-start | bytes 3538948
  20.1 8.6 %copy-start.3 = (bf16[384,384]{1,0:T(8,128)(2,1)}, bf16[384,384]{1,0:T(8,128)(2,1)S(1)}, u32[]{:S(2)}) copy-start(bf16[384,384]{1,0:T(8,128)(2,1)S(1)} %get-tuple-element.30.refs_5_) | copy-start | bytes 884740
  20.1 20.3 %collective-permute-start.6 = (bf16[384,768]{1,0:T(8,128)(2,1)}, bf16[384,768]{1,0:T(8,128)(2,1)S(1)}, u32[]{:S(2)}, u32[]{:S(2)}) collective-permute-start(bf16[384,768]{1,0:T(8,128)(2,1)} %get-tuple-element.29), channel_id=1, source_target_pairs={{0,2},{1,3},{2,0},{3,1},{4,6},{5,7},{6,4},{7,5},{8,10},{9,11},{10,... | collective-permute-start | bytes 1769480 | tf_op jit(solution)/shard_map/elementals/RSy/ppermute | solution.py:387
  21.4 10.5 %collective-permute-start.12 = (bf16[384,384]{1,0:T(8,128)(2,1)}, bf16[384,384]{1,0:T(8,128)(2,1)S(1)}, u32[]{:S(2)}, u32[]{:S(2)}) collective-permute-start(bf16[384,384]{1,0:T(8,128)(2,1)} %get-tuple-element.35), channel_id=1, source_target_pairs={{0,12},{1,13},{2,14},{3,15},{12,0},{13,1},{14,2},{15,3},{16,28},{1... | collective-permute-start | bytes 884744 | tf_op jit(solution)/shard_map/spread/ends/ppermute | solution.py:384
  26.0 0.7 %copy-start.9 = (bf16[384,384]{1,0:T(8,128)(2,1)}, bf16[384,384]{1,0:T(8,128)(2,1)S(1)}, u32[]{:S(2)}) copy-start(bf16[384,384]{1,0:T(8,128)(2,1)S(1)} %get-tuple-element.36.refs_7_) | copy-start | bytes 884740
  26.7 5.2 %collective-permute-start.10 = (bf16[384,384]{1,0:T(8,128)(2,1)S(1)}, bf16[384,384]{1,0:T(8,128)(2,1)S(1)}, u32[]{:S(2)}, u32[]{:S(2)}) collective-permute-start(bf16[384,384]{1,0:T(8,128)(2,1)S(1)} %get-tuple-element.33.near_ref), channel_id=1, source_target_pairs={{4,8},{5,9},{6,10},{7,11},{8,4},{9,5},{10,6},{11,7},{20,24},{21,25... | collective-permute-start | bytes 884744 | tf_op jit(solution)/shard_map/spread/third_in/ppermute | solution.py:384
  27.4 13.0 %collective-permute-start.11 = (bf16[384,384]{1,0:T(8,128)(2,1)S(1)}, bf16[384,384]{1,0:T(8,128)(2,1)S(1)}, u32[]{:S(2)}, u32[]{:S(2)}) collective-permute-start(bf16[384,384]{1,0:T(8,128)(2,1)S(1)} %get-tuple-element.34.refs_1_), channel_id=1, source_target_pairs={{4,0},{5,1},{6,2},{7,3},{8,12},{9,13},{10,14},{11,15},{20,16},{21,... | collective-permute-start | bytes 884744 | tf_op jit(solution)/shard_map/spread/third_out/ppermute | solution.py:384
  28.7 13.3 %collective-permute-start.5 = (bf16[384,768]{1,0:T(8,128)(2,1)S(1)}, bf16[384,768]{1,0:T(8,128)(2,1)S(1)}, u32[]{:S(2)}, u32[]{:S(2)}) collective-permute-start(bf16[384,768]{1,0:T(8,128)(2,1)S(1)} %get-tuple-element.28), channel_id=1, source_target_pairs={{0,1},{1,0},{2,3},{3,2},{4,5},{5,4},{6,7},{7,6},{8,9},{9,8},{10,11... | collective-permute-start | bytes 1769480 | tf_op jit(solution)/shard_map/elementals/swapB/ppermute | solution.py:390
  40.4 1.3 %copy-start.4 = (bf16[384,384]{1,0:T(8,128)(2,1)S(1)}, bf16[384,384]{1,0:T(8,128)(2,1)}, u32[]{:S(2)}) copy-start(bf16[384,384]{1,0:T(8,128)(2,1)} %copy-done.3) | copy-start | bytes 884740
  40.4 1.7 %copy-start.2 = (f32[384,768]{1,0:T(8,128)S(1)}, f32[384,768]{1,0:T(8,128)}, u32[]{:S(2)}) copy-start(f32[384,768]{1,0:T(8,128)} %copy-done.1) | copy-start | bytes 3538948
  40.7 14.0 %collective-permute-start.14 = (bf16[3,384,384]{2,1,0:T(8,128)(2,1)S(1)}, bf16[3,384,384]{2,1,0:T(8,128)(2,1)S(1)}, u32[]{:S(2)}, u32[]{:S(2)}) collective-permute-start(bf16[3,384,384]{2,1,0:T(8,128)(2,1)S(1)} %spread.3.refs_6_), channel_id=1, source_target_pairs={{0,1},{1,0},{2,3},{3,2},{4,5},{5,4},{6,7},{7,6},{8,9},{9,8},{10,11... | collective-permute-start | bytes 2654216 | tf_op jit(solution)/shard_map/spread/swE/ppermute | solution.py:390
  41.4 21.2 %collective-permute-start.15 = (bf16[3,384,384]{2,1,0:T(8,128)(2,1)S(1)}, bf16[3,384,384]{2,1,0:T(8,128)(2,1)S(1)}, u32[]{:S(2)}, u32[]{:S(2)}) collective-permute-start(bf16[3,384,384]{2,1,0:T(8,128)(2,1)S(1)} %spread.3.refs_6_), channel_id=1, source_target_pairs={{0,2},{1,3},{2,0},{3,1},{4,6},{5,7},{6,4},{7,5},{8,10},{9,11},{10,... | collective-permute-start | bytes 2654216 | tf_op jit(solution)/shard_map/spread/Y/ppermute | solution.py:387
  41.7 3.2 %collective-permute-start.13 = (bf16[384,384]{1,0:T(8,128)(2,1)S(1)}, bf16[384,384]{1,0:T(8,128)(2,1)S(1)}, u32[]{:S(2)}, u32[]{:S(2)}) collective-permute-start(bf16[384,384]{1,0:T(8,128)(2,1)S(1)} %copy-done.4), channel_id=1, source_target_pairs={{0,1},{1,0},{2,3},{3,2},{4,5},{5,4},{6,7},{7,6},{8,9},{9,8},{10,11... | collective-permute-start | bytes 884744 | tf_op jit(solution)/shard_map/spread/swE/ppermute | solution.py:390
  42.3 12.4 %copy-start.8 = (bf16[384,384]{1,0:T(8,128)(2,1)S(1)}, bf16[384,384]{1,0:T(8,128)(2,1)}, u32[]{:S(2)}) copy-start(bf16[384,384]{1,0:T(8,128)(2,1)} %copy-done.7) | copy-start | bytes 884740
  42.3 12.4 %copy-start.10 = (bf16[384,384]{1,0:T(8,128)(2,1)S(1)}, bf16[384,384]{1,0:T(8,128)(2,1)}, u32[]{:S(2)}) copy-start(bf16[384,384]{1,0:T(8,128)(2,1)} %copy-done.9) | copy-start | bytes 884740
  42.3 7.5 %collective-permute-start.7 = (bf16[96,768]{1,0:T(8,128)(2,1)S(1)}, bf16[96,768]{1,0:T(8,128)(2,1)S(1)}, u32[]{:S(2)}, u32[]{:S(2)}) collective-permute-start(bf16[96,768]{1,0:T(8,128)(2,1)S(1)} %get-tuple-element.41), channel_id=1, source_target_pairs={{0,4},{1,5},{2,6},{3,7},{4,0},{5,1},{6,2},{7,3},{8,12},{9,13},{10,... | collective-permute-start | bytes 442376 | tf_op jit(solution)/shard_map/elementals/RSz/ppermute | solution.py:384
  42.6 7.3 %collective-permute-start.8 = (bf16[96,768]{1,0:T(8,128)(2,1)S(1)}, bf16[96,768]{1,0:T(8,128)(2,1)S(1)}, u32[]{:S(2)}, u32[]{:S(2)}) collective-permute-start(bf16[96,768]{1,0:T(8,128)(2,1)S(1)} %get-tuple-element.40), channel_id=1, source_target_pairs={{0,8},{1,9},{2,10},{3,11},{4,12},{5,13},{6,14},{7,15},{8,0},{9,1},... | collective-permute-start | bytes 442376 | tf_op jit(solution)/shard_map/elementals/RSz/ppermute | solution.py:384
  44.9 9.8 %collective-permute-start.9 = (bf16[96,768]{1,0:T(8,128)(2,1)S(1)}, bf16[96,768]{1,0:T(8,128)(2,1)S(1)}, u32[]{:S(2)}, u32[]{:S(2)}) collective-permute-start(bf16[96,768]{1,0:T(8,128)(2,1)S(1)} %get-tuple-element.39), channel_id=1, source_target_pairs={{0,12},{1,13},{2,14},{3,15},{4,8},{5,9},{6,10},{7,11},{8,4},{9,5},... | collective-permute-start | bytes 442376 | tf_op jit(solution)/shard_map/elementals/RSz/ppermute | solution.py:384
  62.7 0.9 %copy-start.13 = (s32[96,8]{0,1:T(8,128)S(1)}, s32[96,8]{0,1:T(8,128)}, u32[]{:S(2)}) copy-start(s32[96,8]{0,1:T(8,128)} %param.7) | copy-start | bytes 9220
  62.7 2.9 %collective-permute-start.16 = (bf16[3,384,384]{2,1,0:T(8,128)(2,1)S(1)}, bf16[3,384,384]{2,1,0:T(8,128)(2,1)S(1)}, u32[]{:S(2)}, u32[]{:S(2)}) collective-permute-start(bf16[3,384,384]{2,1,0:T(8,128)(2,1)S(1)} %contract.4.refs_0_), channel_id=1, source_target_pairs={{0,1},{1,0},{2,3},{3,2},{4,5},{5,4},{6,7},{7,6},{8,9},{9,8},{10,11... | collective-permute-start | bytes 2654216 | tf_op jit(solution)/shard_map/contract/swL/ppermute | solution.py:390

commit v4 on v3

--- a/solution.py
+++ b/solution.py
@@ -422,13 +422,11 @@
         middle = named("middle", lambda: send(own, [(1, 2), (2, 1)]))
         beside = named("beside", lambda: across(own))
     with jax.named_scope("elementals"):
-        outgoing, near, middle, beside, away_stay = total(
-            [kept_cross, got_cross], near, middle, beside, away_stay
-        )
+        outgoing, near, middle, away_stay = total([kept_cross, got_cross], near, middle, away_stay)
         crossed = named("RSy", lambda: across(outgoing))
         got_stay = named("swapB", lambda: swap(away_stay))
     with jax.named_scope("spread"):
-        twin, near, middle = matrix(True, 1, near, middle)
+        twin, near, middle, beside = matrix(True, 1, near, middle, beside)
         third_in = named("third_in", lambda: send(near, [(1, 2), (2, 1)]))
         third_out = named("third_out", lambda: send(middle, [(1, 0), (2, 3)]))
         ends = named("ends", lambda: send(lone, [(0, 3), (3, 0)]))

time: 69.1 us -> 67.4 us (0.975)
  waiting for transfers between devices: 26.6 us -> 21.2 us
  starting transfers between devices: 20.4 us -> 23.5 us
  local copies, waits for them, and re-layouts: 4.14 us -> 4.85 us
    ppermute x8, waiting for transfers between devices: 18 us -> 15 us  [send(): return lax.ppermute(block, 'space', route)]
    ppermute x3, waiting for transfers between devices: 6.99 us -> 4.59 us  [across(): return lax.ppermute(block, 'space', [(i, i ^ CORES) for i in range(spaces)])]
    ppermute x8, starting transfers between devices: 12.8 us -> 14.7 us  [send(): return lax.ppermute(block, 'space', route)]
    ppermute x6, starting transfers between devices: 4.82 us -> 6.08 us  [swap(): return lax.ppermute(block, 'space', [(i, i ^ 1) for i in range(spaces)])]
    unnamed x29, local copies, waits for them, and re-layouts: 4.01 us -> 4.72 us
  transfers between devices with their start and end apart: 17 -> 17, of which waited for: 7 -> 5; matrix products, arithmetic and copies ran while one was open for 1% -> 1% of each run, Pallas kernels for 19% -> 21%
where the time goes in v4:
time: 67.4 us; the launch traced here: 66.8 us
  starting transfers between devices  23.5 us (35%)
  waiting for transfers between devices  21.2 us (31%)
  Pallas kernels  16.7 us (25%)
  local copies, waits for them, and re-layouts  4.85 us (7%)
    ppermute x8, waiting for transfers between devices, send(): return lax.ppermute(block, 'space', route)  15 us
    ppermute x8, starting transfers between devices, send(): return lax.ppermute(block, 'space', route)  14.7 us
    pallas_call x2, Pallas kernels, partial_rows(): pl.pallas_call(functools.partial(partial_kernel, rows, chain, stay, len(a...  8.37 us
    ppermute x6, starting transfers between devices, swap(): return lax.ppermute(block, 'space', [(i, i ^ 1) for i in range(spaces)])  6.08 us
    unnamed x29, local copies, waits for them, and re-layouts  4.72 us
    ppermute x3, waiting for transfers between devices, across(): return lax.ppermute(block, 'space', [(i, i ^ CORES) for i in range(spaces)])  4.59 us
    pallas_call x1, Pallas kernels, gather_plan(): pl.pallas_call(functools.partial(pick_kernel, len(late) // 2, group), out...  2.88 us
    ppermute x3, starting transfers between devices, across(): return lax.ppermute(block, 'space', [(i, i ^ CORES) for i in range(spaces)])  2.72 us
  transfers between devices with their start and end apart: 17, of which 5 were waited for; matrix products, arithmetic and copies ran while one was open for 1% of the time, Pallas kernels for 21%

profile of v4, /device:TPU:1, one launch (start us, length us, event | category | flops | bytes accessed | tf_op | source)
XLA Modules:
  0.0 66.8 jit_solution(11208174751394167216)
XLA Ops:
  0.0 0.1 collective-permute-start
  0.1 0.1 pad_add_fusion.place_ref
  0.1 1.5 %copy-done.5 = bf16[2,384,3,384]{3,1,2,0:T(8,128)(2,1)S(1)} copy-done((bf16[2,384,3,384]{3,1,2,0:T(8,128)(2,1)S(1)}, bf16[2,384,3,384]{3,1,2,0:T(8,128)(2,1)}, u32[]{:S(2)}) %copy-start.5) | copy-done | bytes 1769496
  1.6 0.7 %copy-done.11 = s32[4,3]{1,0:T(4,128)S(1)} copy-done((s32[4,3]{1,0:T(4,128)S(1)}, s32[4,3]{1,0:T(4,128)}, u32[]{:S(2)}) %copy-start.11) | copy-done | bytes 72
  2.3 4.2 %elementals.5 = (bf16[384,768]{1,0:T(8,128)(2,1)S(1)}, f32[384,768]{1,0:T(8,128)S(1)}) custom-call(s32[3]{0:T(128)S(1)} %pad_add_fusion.place_ref, s32[4,3]{1,0:T(4,128)S(1)} %copy-done.11, bf16[2,3,384,384]{3,2,1,0:T(8,128)(2,1)S(1)} %bitcast.9), custom_call_target="tpu_custom_call" | custom-call | flops 2717908992 | bytes 3538944 | tf_op jit(solution)/shard_map/elementals/pallas_call | solution.py:217
  6.5 0.0 copy-start.12
  6.5 0.5 collective-permute-start.1
  7.0 0.0 collective-permute-done.other_ref
  7.0 0.0 copy-done
  7.0 1.3 %matrices.1 = (bf16[384,384]{1,0:T(8,128)(2,1)S(1)}, bf16[384,384]{1,0:T(8,128)(2,1)}) custom-call(s32[1]{0:T(128)} %bitcast.core_ref, bf16[2,384,384]{2,1,0:T(8,128)(2,1)S(1)} %bitcast.7, bf16[2,384,384]{2,1,0:T(8,128)(2,1)S(1)} %collective-permute-done.other_ref), custom_call_target="tpu_custom_call" | custom-call | flops 226492416 | bytes 1474560 | tf_op jit(solution)/shard_map/matrices/pallas_call | solution.py:398
  8.3 2.3 %collective-permute-start.2 = (bf16[384,384]{1,0:T(8,128)(2,1)S(1)}, bf16[384,384]{1,0:T(8,128)(2,1)S(1)}, u32[]{:S(2)}, u32[]{:S(2)}) collective-permute-start(bf16[384,384]{1,0:T(8,128)(2,1)S(1)} %get-tuple-element.22.refs_0_.refs_4_), channel_id=1, source_target_pairs={{0,4},{1,5},{2,6},{3,7},{4,0},{5,1},{6,2},{7,3},{8,12},{9,13},{10,... | collective-permute-start | bytes 884744 | tf_op jit(solution)/shard_map/spread/near/ppermute | solution.py:384
  10.7 0.7 collective-permute-start.3
  11.4 1.3 %collective-permute-start.9 = (bf16[384,384]{1,0:T(8,128)(2,1)S(1)}, bf16[384,384]{1,0:T(8,128)(2,1)S(1)}, u32[]{:S(2)}, u32[]{:S(2)}) collective-permute-start(bf16[384,384]{1,0:T(8,128)(2,1)S(1)} %get-tuple-element.22.refs_0_.refs_4_), channel_id=1, source_target_pairs={{0,2},{1,3},{2,0},{3,1},{4,6},{5,7},{6,4},{7,5},{8,10},{9,11},{10,... | collective-permute-start | bytes 884744 | tf_op jit(solution)/shard_map/spread/beside/ppermute | solution.py:387
  12.7 0.0 copy-done.6
  12.7 0.0 copy-done.12
  12.7 4.2 %elementals.4 = (bf16[384,768]{1,0:T(8,128)(2,1)S(1)}, f32[384,768]{1,0:T(8,128)S(1)}, bf16[384,384]{1,0:T(8,128)(2,1)}) custom-call(s32[3]{0:T(128)S(1)} %pad_add_fusion.place_ref, s32[4,3]{1,0:T(4,128)S(1)} %copy-done.12, bf16[2,3,384,384]{3,2,1,0:T(8,128)(2,1)S(1)} %bitcast.10, ...), custom_call_target="tpu_custom_call", output_to_operand_aliasing={{2}: (4, {})} | custom-call | flops 2717908992 | bytes 3538944 | tf_op jit(solution)/shard_map/elementals/pallas_call | solution.py:217
  16.8 0.0 copy-done.7
  16.9 0.0 copy-start.1
  16.9 1.0 %copy-done.1 = f32[384,768]{1,0:T(8,128)} copy-done((f32[384,768]{1,0:T(8,128)}, f32[384,768]{1,0:T(8,128)S(1)}, u32[]{:S(2)}) %copy-start.1) | copy-done | bytes 1179672
  17.9 0.0 collective-permute-done.1.refs_1_
  17.9 0.0 collective-permute-done.2.refs_2_
  17.9 0.0 collective-permute-done.3.refs_3_
  17.9 0.9 %elementals.6 = (bf16[384,768]{1,0:T(8,128)(2,1)}, bf16[384,384]{1,0:T(8,128)(2,1)S(1)}, bf16[384,384]{1,0:T(8,128)(2,1)S(1)}, bf16[384,768]{1,0:T(8,128)(2,1)S(1)}) custom-call(f32[384,768]{1,0:T(8,128)S(1)} %get-tuple-element.25.refs_0_, ...), custom_call_target="tpu_custom_call", output_to_operand_aliasing={{1}: (2, {}), {2}: (3, {}), {3}: (4, {})} | custom-call | flops 1179648 | bytes 2949120 | tf_op jit(solution)/shard_map/elementals/pallas_call | solution.py:251
  18.8 0.9 %collective-permute-start.5 = (bf16[384,768]{1,0:T(8,128)(2,1)}, bf16[384,768]{1,0:T(8,128)(2,1)S(1)}, u32[]{:S(2)}, u32[]{:S(2)}) collective-permute-start(bf16[384,768]{1,0:T(8,128)(2,1)} %get-tuple-element.29), channel_id=1, source_target_pairs={{0,2},{1,3},{2,0},{3,1},{4,6},{5,7},{6,4},{7,5},{8,10},{9,11},{10,... | collective-permute-start | bytes 1769480 | tf_op jit(solution)/shard_map/elementals/RSy/ppermute | solution.py:387
  19.7 5.2 %collective-permute-start.12 = (bf16[384,384]{1,0:T(8,128)(2,1)}, bf16[384,384]{1,0:T(8,128)(2,1)S(1)}, u32[]{:S(2)}, u32[]{:S(2)}) collective-permute-start(bf16[384,384]{1,0:T(8,128)(2,1)} %get-tuple-element.35), channel_id=1, source_target_pairs={{0,12},{1,13},{2,14},{3,15},{12,0},{13,1},{14,2},{15,3},{16,28},{1... | collective-permute-start | bytes 884744 | tf_op jit(solution)/shard_map/spread/ends/ppermute | solution.py:384
  24.9 0.0 collective-permute-done.9.refs_2_
  24.9 0.5 spread.2
  25.4 0.0 copy-start.3
  25.5 0.7 %copy-done.3 = bf16[384,384]{1,0:T(8,128)(2,1)} copy-done((bf16[384,384]{1,0:T(8,128)(2,1)}, bf16[384,384]{1,0:T(8,128)(2,1)S(1)}, u32[]{:S(2)}) %copy-start.3) | copy-done | bytes 294936
  26.2 0.7 %copy-done.9 = bf16[384,384]{1,0:T(8,128)(2,1)} copy-done((bf16[384,384]{1,0:T(8,128)(2,1)}, bf16[384,384]{1,0:T(8,128)(2,1)S(1)}, u32[]{:S(2)}) %copy-start.9) | copy-done | bytes 294936
  26.9 0.7 collective-permute-start.10
  27.6 1.3 %collective-permute-start.11 = (bf16[384,384]{1,0:T(8,128)(2,1)S(1)}, bf16[384,384]{1,0:T(8,128)(2,1)S(1)}, u32[]{:S(2)}, u32[]{:S(2)}) collective-permute-start(bf16[384,384]{1,0:T(8,128)(2,1)S(1)} %get-tuple-element.34.refs_1_), channel_id=1, source_target_pairs={{4,0},{5,1},{6,2},{7,3},{8,12},{9,13},{10,14},{11,15},{20,16},{21,... | collective-permute-start | bytes 884744 | tf_op jit(solution)/shard_map/spread/third_out/ppermute | solution.py:384
  28.9 1.9 %collective-permute-start.4 = (bf16[384,768]{1,0:T(8,128)(2,1)S(1)}, bf16[384,768]{1,0:T(8,128)(2,1)S(1)}, u32[]{:S(2)}, u32[]{:S(2)}) collective-permute-start(bf16[384,768]{1,0:T(8,128)(2,1)S(1)} %get-tuple-element.28), channel_id=1, source_target_pairs={{0,1},{1,0},{2,3},{3,2},{4,5},{5,4},{6,7},{7,6},{8,9},{9,8},{10,11... | collective-permute-start | bytes 1769480 | tf_op jit(solution)/shard_map/elementals/swapB/ppermute | solution.py:390
  30.8 0.0 collective-permute-done.12.refs_3_
  30.8 0.0 collective-permute-done.10.refs_0_
  30.8 6.4 %collective-permute-done.11.refs_2_ = bf16[384,384]{1,0:T(8,128)(2,1)S(1)} collective-permute-done((bf16[384,384]{1,0:T(8,128)(2,1)S(1)}, bf16[384,384]{1,0:T(8,128)(2,1)S(1)}, u32[]{:S(2)}, u32[]{:S(2)}) %collective-permute-start.11) | collective-permute-done | bytes 294944 | tf_op jit(solution)/shard_map/spread/third_out/ppermute | solution.py:384
  37.2 0.0 collective-permute-done.5.refs_2_.refs_4_
  37.2 0.3 spread.3.refs_6_
  37.4 2.4 %collective-permute-start.14 = (bf16[3,384,384]{2,1,0:T(8,128)(2,1)S(1)}, bf16[3,384,384]{2,1,0:T(8,128)(2,1)S(1)}, u32[]{:S(2)}, u32[]{:S(2)}) collective-permute-start(bf16[3,384,384]{2,1,0:T(8,128)(2,1)S(1)} %spread.3.refs_6_), channel_id=1, source_target_pairs={{0,1},{1,0},{2,3},{3,2},{4,5},{5,4},{6,7},{7,6},{8,9},{9,8},{10,11... | collective-permute-start | bytes 2654216 | tf_op jit(solution)/shard_map/spread/swE/ppermute | solution.py:390
  39.8 0.5 collective-permute-start.15
  40.3 0.0 copy-done.4
  40.4 0.3 collective-permute-start.13
  40.7 0.0 collective-permute-done.4.refs_1_
  40.7 0.0 copy-done.2
  40.7 0.2 elementals.7
  40.9 0.0 copy-start.8
  40.9 0.0 copy-start.10
  40.9 0.3 collective-permute-start.6
  41.2 3.0 %collective-permute-start.7 = (bf16[96,768]{1,0:T(8,128)(2,1)S(1)}, bf16[96,768]{1,0:T(8,128)(2,1)S(1)}, u32[]{:S(2)}, u32[]{:S(2)}) collective-permute-start(bf16[96,768]{1,0:T(8,128)(2,1)S(1)} %get-tuple-element.40), channel_id=1, source_target_pairs={{0,8},{1,9},{2,10},{3,11},{4,12},{5,13},{6,14},{7,15},{8,0},{9,1},... | collective-permute-start | bytes 442376 | tf_op jit(solution)/shard_map/elementals/RSz/ppermute | solution.py:384
  44.2 0.0 collective-permute-done.13.refs_8_
  44.2 1.2 %collective-permute-start.8 = (bf16[96,768]{1,0:T(8,128)(2,1)S(1)}, bf16[96,768]{1,0:T(8,128)(2,1)S(1)}, u32[]{:S(2)}, u32[]{:S(2)}) collective-permute-start(bf16[96,768]{1,0:T(8,128)(2,1)S(1)} %get-tuple-element.39), channel_id=1, source_target_pairs={{0,12},{1,13},{2,14},{3,15},{4,8},{5,9},{6,10},{7,11},{8,4},{9,5},... | collective-permute-start | bytes 442376 | tf_op jit(solution)/shard_map/elementals/RSz/ppermute | solution.py:384
  45.5 3.4 %collective-permute-done.6.refs_1_ = bf16[96,768]{1,0:T(8,128)(2,1)S(1)} collective-permute-done((bf16[96,768]{1,0:T(8,128)(2,1)S(1)}, bf16[96,768]{1,0:T(8,128)(2,1)S(1)}, u32[]{:S(2)}, u32[]{:S(2)}) %collective-permute-start.6) | collective-permute-done | bytes 147488 | tf_op jit(solution)/shard_map/elementals/RSz/ppermute | solution.py:384
  48.9 0.0 collective-permute-done.7.refs_2_
  48.9 5.3 %collective-permute-done.8.refs_3_ = bf16[96,768]{1,0:T(8,128)(2,1)S(1)} collective-permute-done((bf16[96,768]{1,0:T(8,128)(2,1)S(1)}, bf16[96,768]{1,0:T(8,128)(2,1)S(1)}, u32[]{:S(2)}, u32[]{:S(2)}) %collective-permute-start.8) | collective-permute-done | bytes 147488 | tf_op jit(solution)/shard_map/elementals/RSz/ppermute | solution.py:384
  54.1 0.0 collective-permute-done.14.refs_9_
  54.1 0.0 copy-done.8
  54.1 2.3 %contract.3 = (bf16[192,384]{1,0:T(8,128)(2,1)S(1)}, bf16[10,96,768]{2,1,0:T(8,128)(2,1)S(1)}) custom-call(s32[1]{0:T(128)} %bitcast.core_ref, bf16[96,768]{1,0:T(8,128)(2,1)S(1)} %get-tuple-element.42.refs_0_, bf16[96,768]{1,0:T(8,128)(2,1)S(1)} %collective-permute-done.6.refs_1_, bf16[96,768]{1,0:T(8,128)(2,1)S(1)} %collective-permute-done.7.refs_2_, ...), custom_call_target="tpu_custom_call" | custom-call | flops 1132462080 | bytes 5898240 | tf_op jit(solution)/shard_map/contract/pallas_call | solution.py:473
  56.4 4.6 %collective-permute-done.15.refs_0_ = bf16[3,384,384]{2,1,0:T(8,128)(2,1)S(1)} collective-permute-done((bf16[3,384,384]{2,1,0:T(8,128)(2,1)S(1)}, bf16[3,384,384]{2,1,0:T(8,128)(2,1)S(1)}, u32[]{:S(2)}, u32[]{:S(2)}) %collective-permute-start.15) | collective-permute-done | bytes 884768 | tf_op jit(solution)/shard_map/spread/Y/ppermute | solution.py:387
  61.0 0.8 %collective-permute-start.16 = (bf16[3,384,384]{2,1,0:T(8,128)(2,1)S(1)}, bf16[3,384,384]{2,1,0:T(8,128)(2,1)S(1)}, u32[]{:S(2)}, u32[]{:S(2)}) collective-permute-start(bf16[3,384,384]{2,1,0:T(8,128)(2,1)S(1)} %contract.4.refs_0_), channel_id=1, source_target_pairs={{0,1},{1,0},{2,3},{3,2},{4,5},{5,4},{6,7},{7,6},{8,9},{9,8},{10,11... | collective-permute-start | bytes 2654216 | tf_op jit(solution)/shard_map/contract/swL/ppermute | solution.py:390
  61.9 0.1 copy.13
  62.0 0.1 eq.107
  62.1 0.3 and_convert_fusion.refs_2_
  62.4 1.6 %collective-permute-done.16.refs_1_ = bf16[3,384,384]{2,1,0:T(8,128)(2,1)S(1)} collective-permute-done((bf16[3,384,384]{2,1,0:T(8,128)(2,1)S(1)}, bf16[3,384,384]{2,1,0:T(8,128)(2,1)S(1)}, u32[]{:S(2)}, u32[]{:S(2)}) %collective-permute-start.16) | collective-permute-done | bytes 884768 | tf_op jit(solution)/shard_map/contract/swL/ppermute | solution.py:390
  63.9 2.9 %contract.5 = bf16[96,8,768]{2,1,0:T(8,128)(2,1)} custom-call(s32[1]{0:T(128)} %bitcast.core_ref, bf16[192,384]{1,0:T(8,128)(2,1)S(1)} %get-tuple-element.37.stacked_ref, bf16[10,96,768]{2,1,0:T(8,128)(2,1)S(1)} %get-tuple-element.38.refs_1_.first_ref, bf16[3,384,384]{2,1,0:T(8,128)(2,1)S(1)} %contract.4.refs_0_, ...), custom_call_target="tpu_custom_call" | custom-call | flops 679477248 | bytes 3538944 | tf_op jit(solution)/shard_map/contract/pallas_call | solution.py:491
  (15 shorter events, 0.1 us)
Async XLA Ops:
  0.0 7.0 %collective-permute-start = (bf16[2,384,384]{2,1,0:T(8,128)(2,1)}, bf16[2,384,384]{2,1,0:T(8,128)(2,1)S(1)}, u32[]{:S(2)}, u32[]{:S(2)}) collective-permute-start(bf16[2,384,384]{2,1,0:T(8,128)(2,1)} %bitcast.6), channel_id=1, source_target_pairs={{0,1},{1,0},{2,3},{3,2},{4,5},{5,4},{6,7},{7,6},{8,9},{9,8},{10,11... | collective-permute-start | bytes 1769480 | tf_op jit(solution)/shard_map/matrices/swapP/ppermute | solution.py:390
  0.1 1.5 %copy-start.5 = (bf16[2,384,3,384]{3,1,2,0:T(8,128)(2,1)S(1)}, bf16[2,384,3,384]{3,1,2,0:T(8,128)(2,1)}, u32[]{:S(2)}) copy-start(bf16[2,384,3,384]{3,1,2,0:T(8,128)(2,1)} %param.4) | copy-start | bytes 5308420
  1.6 0.7 %copy-start.11 = (s32[4,3]{1,0:T(4,128)S(1)}, s32[4,3]{1,0:T(4,128)}, u32[]{:S(2)}) copy-start(s32[4,3]{1,0:T(4,128)} %mom_ref.3) | copy-start | bytes 148
  2.3 4.8 %copy-start = (bf16[1,2,384,384]{3,2,1,0:T(8,128)(2,1)S(1)}, bf16[1,2,384,384]{3,2,1,0:T(8,128)(2,1)}, u32[]{:S(2)}) copy-start(bf16[1,2,384,384]{3,2,1,0:T(8,128)(2,1)} %param.6) | copy-start | bytes 1769476
  2.3 10.4 %copy-start.6 = (bf16[2,384,3,384]{3,1,2,0:T(8,128)(2,1)S(1)}, bf16[2,384,3,384]{3,1,2,0:T(8,128)(2,1)}, u32[]{:S(2)}) copy-start(bf16[2,384,3,384]{3,1,2,0:T(8,128)(2,1)} %param.4) | copy-start | bytes 5308420
  6.5 6.2 %copy-start.12 = (s32[4,3]{1,0:T(4,128)S(1)}, s32[4,3]{1,0:T(4,128)}, u32[]{:S(2)}) copy-start(s32[4,3]{1,0:T(4,128)} %mom_ref.3) | copy-start | bytes 148
  6.5 11.4 %collective-permute-start.1 = (bf16[384,768]{1,0:T(8,128)(2,1)S(1)}, bf16[384,768]{1,0:T(8,128)(2,1)S(1)}, u32[]{:S(2)}, u32[]{:S(2)}) collective-permute-start(bf16[384,768]{1,0:T(8,128)(2,1)S(1)} %get-tuple-element.26), channel_id=1, source_target_pairs={{0,1},{1,0},{2,3},{3,2},{4,5},{5,4},{6,7},{7,6},{8,9},{9,8},{10,11... | collective-permute-start | bytes 1769480 | tf_op jit(solution)/shard_map/elementals/swapA/ppermute | solution.py:390
  8.3 8.5 %copy-start.7 = (bf16[384,384]{1,0:T(8,128)(2,1)}, bf16[384,384]{1,0:T(8,128)(2,1)S(1)}, u32[]{:S(2)}) copy-start(bf16[384,384]{1,0:T(8,128)(2,1)S(1)} %get-tuple-element.22.refs_0_.refs_4_) | copy-start | bytes 884740
  8.3 9.5 %collective-permute-start.2 = (bf16[384,384]{1,0:T(8,128)(2,1)S(1)}, bf16[384,384]{1,0:T(8,128)(2,1)S(1)}, u32[]{:S(2)}, u32[]{:S(2)}) collective-permute-start(bf16[384,384]{1,0:T(8,128)(2,1)S(1)} %get-tuple-element.22.refs_0_.refs_4_), channel_id=1, source_target_pairs={{0,4},{1,5},{2,6},{3,7},{4,0},{5,1},{6,2},{7,3},{8,12},{9,13},{10,... | collective-permute-start | bytes 884744 | tf_op jit(solution)/shard_map/spread/near/ppermute | solution.py:384
  10.7 7.2 %collective-permute-start.3 = (bf16[384,384]{1,0:T(8,128)(2,1)S(1)}, bf16[384,384]{1,0:T(8,128)(2,1)S(1)}, u32[]{:S(2)}, u32[]{:S(2)}) collective-permute-start(bf16[384,384]{1,0:T(8,128)(2,1)S(1)} %get-tuple-element.22.refs_0_.refs_4_), channel_id=1, source_target_pairs={{4,8},{5,9},{6,10},{7,11},{8,4},{9,5},{10,6},{11,7},{20,24},{21,25... | collective-permute-start | bytes 884744 | tf_op jit(solution)/shard_map/spread/middle/ppermute | solution.py:384
  11.4 13.5 %collective-permute-start.9 = (bf16[384,384]{1,0:T(8,128)(2,1)S(1)}, bf16[384,384]{1,0:T(8,128)(2,1)S(1)}, u32[]{:S(2)}, u32[]{:S(2)}) collective-permute-start(bf16[384,384]{1,0:T(8,128)(2,1)S(1)} %get-tuple-element.22.refs_0_.refs_4_), channel_id=1, source_target_pairs={{0,2},{1,3},{2,0},{3,1},{4,6},{5,7},{6,4},{7,5},{8,10},{9,11},{10,... | collective-permute-start | bytes 884744 | tf_op jit(solution)/shard_map/spread/beside/ppermute | solution.py:387
  16.9 1.0 %copy-start.1 = (f32[384,768]{1,0:T(8,128)}, f32[384,768]{1,0:T(8,128)S(1)}, u32[]{:S(2)}) copy-start(f32[384,768]{1,0:T(8,128)S(1)} %get-tuple-element.24.refs_0_) | copy-start | bytes 3538948
  18.8 18.4 %collective-permute-start.5 = (bf16[384,768]{1,0:T(8,128)(2,1)}, bf16[384,768]{1,0:T(8,128)(2,1)S(1)}, u32[]{:S(2)}, u32[]{:S(2)}) collective-permute-start(bf16[384,768]{1,0:T(8,128)(2,1)} %get-tuple-element.29), channel_id=1, source_target_pairs={{0,2},{1,3},{2,0},{3,1},{4,6},{5,7},{6,4},{7,5},{8,10},{9,11},{10,... | collective-permute-start | bytes 1769480 | tf_op jit(solution)/shard_map/elementals/RSy/ppermute | solution.py:387
  19.7 11.1 %collective-permute-start.12 = (bf16[384,384]{1,0:T(8,128)(2,1)}, bf16[384,384]{1,0:T(8,128)(2,1)S(1)}, u32[]{:S(2)}, u32[]{:S(2)}) collective-permute-start(bf16[384,384]{1,0:T(8,128)(2,1)} %get-tuple-element.35), channel_id=1, source_target_pairs={{0,12},{1,13},{2,14},{3,15},{12,0},{13,1},{14,2},{15,3},{16,28},{1... | collective-permute-start | bytes 884744 | tf_op jit(solution)/shard_map/spread/ends/ppermute | solution.py:384
  25.4 0.7 %copy-start.3 = (bf16[384,384]{1,0:T(8,128)(2,1)}, bf16[384,384]{1,0:T(8,128)(2,1)S(1)}, u32[]{:S(2)}) copy-start(bf16[384,384]{1,0:T(8,128)(2,1)S(1)} %get-tuple-element.32.refs_5_) | copy-start | bytes 884740
  26.2 0.7 %copy-start.9 = (bf16[384,384]{1,0:T(8,128)(2,1)}, bf16[384,384]{1,0:T(8,128)(2,1)S(1)}, u32[]{:S(2)}) copy-start(bf16[384,384]{1,0:T(8,128)(2,1)S(1)} %get-tuple-element.36.refs_7_) | copy-start | bytes 884740
  26.9 3.9 %collective-permute-start.10 = (bf16[384,384]{1,0:T(8,128)(2,1)S(1)}, bf16[384,384]{1,0:T(8,128)(2,1)S(1)}, u32[]{:S(2)}, u32[]{:S(2)}) collective-permute-start(bf16[384,384]{1,0:T(8,128)(2,1)S(1)} %get-tuple-element.33.near_ref), channel_id=1, source_target_pairs={{4,8},{5,9},{6,10},{7,11},{8,4},{9,5},{10,6},{11,7},{20,24},{21,25... | collective-permute-start | bytes 884744 | tf_op jit(solution)/shard_map/spread/third_in/ppermute | solution.py:384
  27.6 9.6 %collective-permute-start.11 = (bf16[384,384]{1,0:T(8,128)(2,1)S(1)}, bf16[384,384]{1,0:T(8,128)(2,1)S(1)}, u32[]{:S(2)}, u32[]{:S(2)}) collective-permute-start(bf16[384,384]{1,0:T(8,128)(2,1)S(1)} %get-tuple-element.34.refs_1_), channel_id=1, source_target_pairs={{4,0},{5,1},{6,2},{7,3},{8,12},{9,13},{10,14},{11,15},{20,16},{21,... | collective-permute-start | bytes 884744 | tf_op jit(solution)/shard_map/spread/third_out/ppermute | solution.py:384
  28.9 11.8 %collective-permute-start.4 = (bf16[384,768]{1,0:T(8,128)(2,1)S(1)}, bf16[384,768]{1,0:T(8,128)(2,1)S(1)}, u32[]{:S(2)}, u32[]{:S(2)}) collective-permute-start(bf16[384,768]{1,0:T(8,128)(2,1)S(1)} %get-tuple-element.28), channel_id=1, source_target_pairs={{0,1},{1,0},{2,3},{3,2},{4,5},{5,4},{6,7},{7,6},{8,9},{9,8},{10,11... | collective-permute-start | bytes 1769480 | tf_op jit(solution)/shard_map/elementals/swapB/ppermute | solution.py:390
  37.2 3.2 %copy-start.4 = (bf16[384,384]{1,0:T(8,128)(2,1)S(1)}, bf16[384,384]{1,0:T(8,128)(2,1)}, u32[]{:S(2)}) copy-start(bf16[384,384]{1,0:T(8,128)(2,1)} %copy-done.3) | copy-start | bytes 884740
  37.2 3.5 %copy-start.2 = (f32[384,768]{1,0:T(8,128)S(1)}, f32[384,768]{1,0:T(8,128)}, u32[]{:S(2)}) copy-start(f32[384,768]{1,0:T(8,128)} %copy-done.1) | copy-start | bytes 3538948
  37.4 16.7 %collective-permute-start.14 = (bf16[3,384,384]{2,1,0:T(8,128)(2,1)S(1)}, bf16[3,384,384]{2,1,0:T(8,128)(2,1)S(1)}, u32[]{:S(2)}, u32[]{:S(2)}) collective-permute-start(bf16[3,384,384]{2,1,0:T(8,128)(2,1)S(1)} %spread.3.refs_6_), channel_id=1, source_target_pairs={{0,1},{1,0},{2,3},{3,2},{4,5},{5,4},{6,7},{7,6},{8,9},{9,8},{10,11... | collective-permute-start | bytes 2654216 | tf_op jit(solution)/shard_map/spread/swE/ppermute | solution.py:390
  39.8 21.2 %collective-permute-start.15 = (bf16[3,384,384]{2,1,0:T(8,128)(2,1)S(1)}, bf16[3,384,384]{2,1,0:T(8,128)(2,1)S(1)}, u32[]{:S(2)}, u32[]{:S(2)}) collective-permute-start(bf16[3,384,384]{2,1,0:T(8,128)(2,1)S(1)} %spread.3.refs_6_), channel_id=1, source_target_pairs={{0,2},{1,3},{2,0},{3,1},{4,6},{5,7},{6,4},{7,5},{8,10},{9,11},{10,... | collective-permute-start | bytes 2654216 | tf_op jit(solution)/shard_map/spread/Y/ppermute | solution.py:387
  40.4 3.9 %collective-permute-start.13 = (bf16[384,384]{1,0:T(8,128)(2,1)S(1)}, bf16[384,384]{1,0:T(8,128)(2,1)S(1)}, u32[]{:S(2)}, u32[]{:S(2)}) collective-permute-start(bf16[384,384]{1,0:T(8,128)(2,1)S(1)} %copy-done.4), channel_id=1, source_target_pairs={{0,1},{1,0},{2,3},{3,2},{4,5},{5,4},{6,7},{7,6},{8,9},{9,8},{10,11... | collective-permute-start | bytes 884744 | tf_op jit(solution)/shard_map/spread/swE/ppermute | solution.py:390
  40.9 13.2 %copy-start.8 = (bf16[384,384]{1,0:T(8,128)(2,1)S(1)}, bf16[384,384]{1,0:T(8,128)(2,1)}, u32[]{:S(2)}) copy-start(bf16[384,384]{1,0:T(8,128)(2,1)} %copy-done.7) | copy-start | bytes 884740
  40.9 13.2 %copy-start.10 = (bf16[384,384]{1,0:T(8,128)(2,1)S(1)}, bf16[384,384]{1,0:T(8,128)(2,1)}, u32[]{:S(2)}) copy-start(bf16[384,384]{1,0:T(8,128)(2,1)} %copy-done.9) | copy-start | bytes 884740
  40.9 7.9 %collective-permute-start.6 = (bf16[96,768]{1,0:T(8,128)(2,1)S(1)}, bf16[96,768]{1,0:T(8,128)(2,1)S(1)}, u32[]{:S(2)}, u32[]{:S(2)}) collective-permute-start(bf16[96,768]{1,0:T(8,128)(2,1)S(1)} %get-tuple-element.41), channel_id=1, source_target_pairs={{0,4},{1,5},{2,6},{3,7},{4,0},{5,1},{6,2},{7,3},{8,12},{9,13},{10,... | collective-permute-start | bytes 442376 | tf_op jit(solution)/shard_map/elementals/RSz/ppermute | solution.py:384
  41.2 7.6 %collective-permute-start.7 = (bf16[96,768]{1,0:T(8,128)(2,1)S(1)}, bf16[96,768]{1,0:T(8,128)(2,1)S(1)}, u32[]{:S(2)}, u32[]{:S(2)}) collective-permute-start(bf16[96,768]{1,0:T(8,128)(2,1)S(1)} %get-tuple-element.40), channel_id=1, source_target_pairs={{0,8},{1,9},{2,10},{3,11},{4,12},{5,13},{6,14},{7,15},{8,0},{9,1},... | collective-permute-start | bytes 442376 | tf_op jit(solution)/shard_map/elementals/RSz/ppermute | solution.py:384
  44.2 9.9 %collective-permute-start.8 = (bf16[96,768]{1,0:T(8,128)(2,1)S(1)}, bf16[96,768]{1,0:T(8,128)(2,1)S(1)}, u32[]{:S(2)}, u32[]{:S(2)}) collective-permute-start(bf16[96,768]{1,0:T(8,128)(2,1)S(1)} %get-tuple-element.39), channel_id=1, source_target_pairs={{0,12},{1,13},{2,14},{3,15},{4,8},{5,9},{6,10},{7,11},{8,4},{9,5},... | collective-permute-start | bytes 442376 | tf_op jit(solution)/shard_map/elementals/RSz/ppermute | solution.py:384
  61.0 0.9 %copy-start.13 = (s32[96,8]{0,1:T(8,128)S(1)}, s32[96,8]{0,1:T(8,128)}, u32[]{:S(2)}) copy-start(s32[96,8]{0,1:T(8,128)} %param.7) | copy-start | bytes 9220
  61.0 2.9 %collective-permute-start.16 = (bf16[3,384,384]{2,1,0:T(8,128)(2,1)S(1)}, bf16[3,384,384]{2,1,0:T(8,128)(2,1)S(1)}, u32[]{:S(2)}, u32[]{:S(2)}) collective-permute-start(bf16[3,384,384]{2,1,0:T(8,128)(2,1)S(1)} %contract.4.refs_0_), channel_id=1, source_target_pairs={{0,1},{1,0},{2,3},{3,2},{4,5},{5,4},{6,7},{7,6},{8,9},{9,8},{10,11... | collective-permute-start | bytes 2654216 | tf_op jit(solution)/shard_map/contract/swL/ppermute | solution.py:390
